TPU v7x, 32 devices: a whole 2x2x4 slice. The times are simulated.
32 devices in a mesh: rows: 16 (over z, y, x), cols: 2 (over core).
Axes of the slice: x: 2, y: 2, z: 4, core: 2. Of those that a mesh axis runs over, the one named last changes fastest.
Arguments:
- whitening: float32 [6144, 384], P('rows'), as said below
- sensor_states: int32 [6144, 4], P('rows'), may hold values from 0 to 1023, as said below
- sensor_coefficients: float32 [6144, 4], P('rows'), may hold values from -5 to 5
- sensor_readings: float32 [6144], P('rows'), may hold values from -6 to 6
- conduit_endpoints: int32 [2048, 2], P('rows'), may hold values from 0 to 1023
- conductance: float32 [2048], P('rows'), may hold values from 0.2 to 1
- balance_right_side: float32 [2048], P('rows'), may hold values from -3 to 3
- prior_root_factor: float32 [1024, 1024], P('rows'), as said below
- prior_information: float32 [1024], P('rows'), may hold values from -6 to 6
- transition: float32 [1024, 1024], P('cols'), may hold values from -0.1875 to 0.1875
Outputs:
- r_post: float32 [1024, 1024], P('rows', 'cols')
- z_post: float32 [1024], P('cols')
- x_next: float32 [1024], P('cols')
Inputs may be any that keep to these rules, and one draw needn't show every extreme that they name: `prior_root_factor`: upper triangular, with diagonal entries between 1.5 and 3. `whitening`: each aligned block of 384 rows is a lower triangular matrix with a positive diagonal. `sensor_states`: the 4 states of a row are consecutive, counted modulo 1024.
All inputs are finite; a program needn't handle non-finite values.
Results may differ from a plain program's by a relative error of at most 0.0003.
Values sent between devices are 32-bit elements; how exact they have to be, the bound alone decides.
No kernel may reach another device: no remote copies, remote signals or barrier semaphores. Data moves between devices by JAX's collectives and lax.ppermute only.
A program may use at most 128 MiB of HBM per device.

v0:
```python
import jax
import jax.numpy as jnp
from jax import lax
from jax.sharding import PartitionSpec as P


def incidence_matrix(states, coeffs, state_total_count):
    column_ids = lax.broadcasted_iota(jnp.int32, (states.shape[0], state_total_count), 1)
    summed = jnp.zeros((states.shape[0], state_total_count), jnp.float32)
    for position in range(states.shape[1]):
        summed = summed + jnp.where(
            column_ids == states[:, position : position + 1],
            coeffs[:, position : position + 1],
            0.0,
        )
    return summed


def per_device(
    whitening,
    sensor_states,
    sensor_coefficients,
    sensor_readings,
    conduit_endpoints,
    conductance,
    balance_right_side,
    prior_root_factor,
    prior_information,
    transition,
):
    highest_accuracy = lax.Precision.HIGHEST
    state_total_count = prior_root_factor.shape[1]
    col_width = state_total_count // lax.axis_size("cols")
    col_start = lax.axis_index("cols") * col_width
    sensed_states = incidence_matrix(sensor_states, sensor_coefficients, state_total_count)
    sensor_row_list = jnp.dot(whitening, sensed_states, precision=highest_accuracy)
    sensor_right_side = jnp.dot(whitening, sensor_readings, precision=highest_accuracy)
    pair_coeffs = jnp.stack([conductance, -conductance], axis=1)
    balance_row_list = incidence_matrix(conduit_endpoints, pair_coeffs, state_total_count)
    stacked_system = jnp.concatenate([prior_root_factor, sensor_row_list, balance_row_list], axis=0)
    combined_right_side = jnp.concatenate(
        [prior_information, sensor_right_side, conductance * balance_right_side], axis=0
    )
    moment_part = lax.dot_general(
        stacked_system, combined_right_side, (((0,), (0,)), ((), ())), precision=highest_accuracy
    )
    stacked_cols = lax.dynamic_slice_in_dim(stacked_system, col_start, col_width, 1)
    gram_part = lax.dot_general(
        stacked_system, stacked_cols, (((0,), (0,)), ((), ())), precision=highest_accuracy
    )
    gram_sum, moment = lax.psum((gram_part, moment_part), "rows")
    gram = lax.all_gather(gram_sum, "cols", axis=1, tiled=True)
    lower_factor = jnp.linalg.cholesky(gram)
    z_col = lax.linalg.triangular_solve(lower_factor, moment[:, None], left_side=True, lower=True)
    est_col = lax.linalg.triangular_solve(
        lower_factor, z_col, left_side=True, lower=True, transpose_a=True
    )
    row_count = state_total_count // lax.axis_size("rows")
    row_start = lax.axis_index("rows") * row_count
    factor_piece = lax.dynamic_slice(lower_factor, (col_start, row_start), (col_width, row_count)).T
    z_piece = lax.dynamic_slice_in_dim(z_col[:, 0], col_start, col_width, 0)
    x_piece = jnp.dot(transition, est_col[:, 0], precision=highest_accuracy)
    return (factor_piece, z_piece, x_piece)


def solution(mesh):
    in_specs = (
        P("rows", None),
        P("rows", None),
        P("rows", None),
        P("rows"),
        P("rows", None),
        P("rows"),
        P("rows"),
        P("rows", None),
        P("rows"),
        P("cols", None),
    )
    out_specs = (P("rows", "cols"), P("cols"), P("cols"))
    return jax.shard_map(
        per_device, mesh=mesh, in_specs=in_specs, out_specs=out_specs, check_vma=False
    )
```

profile of v0, /device:TPU:0, one launch (start us, length us, event | category | flops | bytes accessed | tf_op | source)
XLA Modules:
  0.0 556.9 jit_solution(15437152902200995242)
XLA Ops:
  11.4 4.6 fusion.10
  16.0 1.1 copy-done.2
  17.4 6.6 %fusion.13 = f32[1024,512]{0,1:T(8,128)} fusion(f32[576,1024]{1,0:T(8,128)S(1)} %pad_maximum_fusion, s32[]{:T(128)S(6)} %select_n.38), kind=kOutput, calls=%fused_computation.27 | convolution fusion | flops 3623878656 | bytes 5636100 | tf_op jit(solution)/shard_map/dot_general | solution.py:48
  24.1 128.8 %all-reduce.3.cloned.1.call-done = f32[1024,512]{0,1:T(8,128)} async-done(((f32[1024,512]{0,1:T(8,128)}), f32[1024,512]{0,1:T(8,128)}) %all-reduce.3.cloned.1.call-update) | async-done | bytes 2097168 | tf_op jit(solution)/shard_map/psum | solution.py:51
  153.7 2.7 fusion.142
  156.5 40.1 %psum.15 = f32[1024]{0:T(1024)S(1)} all-reduce(f32[1024]{0:T(1024)S(1)} %bitcast.355), channel_id=1, replica_groups=mesh['rows'=16,'cols'=2] {'rows'}, use_global_device_ids=true, to_apply=%region_17.18 | all-reduce | flops 1024 | bytes 8192 | tf_op jit(solution)/shard_map/psum | solution.py:51
  196.6 5.5 copy.14
  202.1 4.4 fusion
  206.6 1.9 copy-done.1
  208.5 11.7 %cholesky.223 = f32[128,128]{1,0:T(8,128)S(1)} custom-call(f32[128,128]{1,0:T(8,128)S(1)} %cholesky.580), custom_call_target="Cholesky" | custom-call | tf_op jit(solution)/shard_map/jit(cholesky)/cholesky | solution.py:53
  220.2 9.8 %custom-call.64 = f32[1,128,128]{1,2,0:T(8,128)S(1)} custom-call(f32[1,128,128]{2,1,0:T(8,128)S(1)} %get-tuple-element.55), custom_call_target="InvertDiagBlocksLowerTriangular" | custom-call | tf_op jit(solution)/shard_map/jit(cholesky)/cholesky | solution.py:53
  230.1 1.6 fusion.61
  231.7 1.9 convolution_subtract_fusion
  233.8 11.9 %cholesky.244 = f32[128,128]{1,0:T(8,128)S(1)} custom-call(f32[128,128]{1,0:T(8,128)S(1)} %cholesky.584), custom_call_target="Cholesky" | custom-call | tf_op jit(solution)/shard_map/jit(cholesky)/cholesky | solution.py:53
  245.7 2.5 cholesky.255
  249.7 9.8 %custom-call.65 = f32[1,128,128]{1,2,0:T(8,128)S(1)} custom-call(f32[1,128,128]{2,1,0:T(8,128)S(1)} %get-tuple-element.52), custom_call_target="InvertDiagBlocksLowerTriangular" | custom-call | tf_op jit(solution)/shard_map/jit(cholesky)/cholesky | solution.py:53
  259.6 1.2 convolution_dynamic-update-slice_fusion
  260.8 2.1 convolution_subtract_fusion.1
  262.9 11.7 %cholesky.468 = f32[128,128]{1,0:T(8,128)S(1)} custom-call(f32[128,128]{1,0:T(8,128)S(1)} %cholesky.589), custom_call_target="Cholesky" | custom-call | tf_op jit(solution)/shard_map/jit(cholesky)/cholesky | solution.py:53
  275.9 9.8 %custom-call.66 = f32[1,128,128]{1,2,0:T(8,128)S(1)} custom-call(f32[1,128,128]{2,1,0:T(8,128)S(1)} %get-tuple-element.49), custom_call_target="InvertDiagBlocksLowerTriangular" | custom-call | tf_op jit(solution)/shard_map/jit(cholesky)/cholesky | solution.py:53
  285.7 1.2 convolution_dynamic-update-slice_fusion.1
  286.9 2.3 convolution_subtract_fusion.2
  289.3 12.1 %cholesky.487 = f32[128,128]{1,0:T(8,128)S(1)} custom-call(f32[128,128]{1,0:T(8,128)S(1)} %cholesky.594), custom_call_target="Cholesky" | custom-call | tf_op jit(solution)/shard_map/jit(cholesky)/cholesky | solution.py:53
  302.7 9.8 %custom-call.67 = f32[1,128,128]{1,2,0:T(8,128)S(1)} custom-call(f32[1,128,128]{2,1,0:T(8,128)S(1)} %get-tuple-element.46), custom_call_target="InvertDiagBlocksLowerTriangular" | custom-call | tf_op jit(solution)/shard_map/jit(cholesky)/cholesky | solution.py:53
  312.5 1.1 convolution_dynamic-update-slice_fusion.2
  313.6 2.3 convolution_subtract_fusion.3
  316.0 11.7 %cholesky.506 = f32[128,128]{1,0:T(8,128)S(1)} custom-call(f32[128,128]{1,0:T(8,128)S(1)} %cholesky.599), custom_call_target="Cholesky" | custom-call | tf_op jit(solution)/shard_map/jit(cholesky)/cholesky | solution.py:53
  329.0 10.0 %custom-call.68 = f32[1,128,128]{1,2,0:T(8,128)S(1)} custom-call(f32[1,128,128]{2,1,0:T(8,128)S(1)} %get-tuple-element.43), custom_call_target="InvertDiagBlocksLowerTriangular" | custom-call | tf_op jit(solution)/shard_map/jit(cholesky)/cholesky | solution.py:53
  338.9 1.0 convolution_dynamic-update-slice_fusion.3
  340.0 2.3 convolution_subtract_fusion.4
  342.3 11.7 %cholesky.526 = f32[128,128]{1,0:T(8,128)S(1)} custom-call(f32[128,128]{1,0:T(8,128)S(1)} %cholesky.604), custom_call_target="Cholesky" | custom-call | tf_op jit(solution)/shard_map/jit(cholesky)/cholesky | solution.py:53
  355.3 9.8 %custom-call.69 = f32[1,128,128]{1,2,0:T(8,128)S(1)} custom-call(f32[1,128,128]{2,1,0:T(8,128)S(1)} %get-tuple-element.40), custom_call_target="InvertDiagBlocksLowerTriangular" | custom-call | tf_op jit(solution)/shard_map/jit(cholesky)/cholesky | solution.py:53
  365.1 0.9 convolution_dynamic-update-slice_fusion.4
  366.0 2.0 convolution_subtract_fusion.5
  368.1 11.9 %cholesky.546 = f32[128,128]{1,0:T(8,128)S(1)} custom-call(f32[128,128]{1,0:T(8,128)S(1)} %cholesky.609), custom_call_target="Cholesky" | custom-call | tf_op jit(solution)/shard_map/jit(cholesky)/cholesky | solution.py:53
  381.3 9.8 %custom-call.70 = f32[1,128,128]{1,2,0:T(8,128)S(1)} custom-call(f32[1,128,128]{2,1,0:T(8,128)S(1)} %get-tuple-element.37), custom_call_target="InvertDiagBlocksLowerTriangular" | custom-call | tf_op jit(solution)/shard_map/jit(cholesky)/cholesky | solution.py:53
  391.9 1.8 convolution_subtract_fusion.6
  393.7 11.7 %cholesky.564 = f32[128,128]{1,0:T(8,128)S(1)} custom-call(f32[128,128]{1,0:T(8,128)S(1)} %convolution_subtract_fusion.6), custom_call_target="Cholesky" | custom-call | tf_op jit(solution)/shard_map/jit(cholesky)/cholesky | solution.py:53
  412.5 4.8 fusion.1
  418.2 27.8 %while.1 = (s32[]{:T(128)}, f32[1024,1024]{1,0:T(8,128)}, s32[8,2]{0,1:T(2,128)S(1)}, f32[8,128,128]{2,1,0:T(8,128)}, s32[]{:T(128)}) while((s32[]{:T(128)}, f32[1024,1024]{1,0:T(8,128)}, s32[8,2]{0,1:T(2,128)S(1)}, f32[8,128,128]{2,1,0:T(8,128)}, s32[]{:T(128)}) %tuple.77), condition=%wide.while_cond, body=%wide.while_body.sunk | while | flops 2 | bytes 132205 | solution.py:54
  418.8 2.9 bitcast_dynamic-update-slice_fusion.2
  422.3 2.9 bitcast_dynamic-update-slice_fusion.2
  425.8 2.9 bitcast_dynamic-update-slice_fusion.2
  429.3 2.9 bitcast_dynamic-update-slice_fusion.2
  432.7 2.9 bitcast_dynamic-update-slice_fusion.2
  436.2 2.9 bitcast_dynamic-update-slice_fusion.2
  439.7 2.9 bitcast_dynamic-update-slice_fusion.2
  443.2 2.8 bitcast_dynamic-update-slice_fusion.2
  446.0 79.6 %custom-call.71 = f32[8,128,128]{1,2,0:T(8,128)S(1)} custom-call(f32[8,128,128]{2,1,0:T(8,128)} %get-tuple-element.10), custom_call_target="InvertDiagBlocksLowerTriangular" | custom-call | tf_op jit(solution)/shard_map/triangular_solve | solution.py:54
  525.8 1.0 fusion.23
  527.1 1.1 fusion.24
  528.4 1.2 fusion.43
  529.8 1.2 fusion.29
  531.2 1.4 fusion.41
  532.8 1.4 fusion.31
  534.4 1.5 fusion.25
  536.9 1.0 fusion.19
  538.2 1.1 fusion.26
  539.5 1.2 fusion.39
  540.9 1.2 fusion.33
  542.4 1.3 fusion.37
  543.9 1.3 fusion.35
  545.5 1.4 fusion.27
  547.2 2.4 fusion.145
  (112 shorter events, 26.0 us)
Async XLA Ops:
  7.2 540.1 %copy-start = (f32[512,1024]{1,0:T(8,128)S(1)}, f32[512,1024]{1,0:T(8,128)}, u32[]{:S(2)}) copy-start(f32[512,1024]{1,0:T(8,128)} %param.19) | copy-start | bytes 6291460
  7.2 9.9 %copy-start.4 = (f32[64,1024]{1,0:T(8,128)S(1)}, f32[64,1024]{1,0:T(8,128)}, u32[]{:S(2)}) copy-start(f32[64,1024]{1,0:T(8,128)} %param.17) | copy-start | bytes 786436
  7.2 145.7 %all-reduce.3.cloned.1.call-start = ((), (), s32[]{:S(2)}) async-start(), calls=%async_computation | async-start | bytes 4194304 | tf_op jit(solution)/shard_map/psum | solution.py:51
  16.0 1.1 copy-start.2
  17.4 135.6 %copy-start.5 = (f32[384]{0:T(512)S(1)}, f32[384]{0:T(512)}, u32[]{:S(2)}) copy-start(f32[384]{0:T(512)} %param.13) | copy-start | bytes 4612
  17.4 135.6 %copy-start.3 = (f32[384,384]{1,0:T(8,128)S(1)}, f32[384,384]{1,0:T(8,128)}, u32[]{:S(2)}) copy-start(f32[384,384]{1,0:T(8,128)} %param.10) | copy-start | bytes 1769476
  17.4 136.2 %copy-start.6 = (f32[64]{0:T(128)S(1)}, f32[64]{0:T(128)}, u32[]{:S(2)}) copy-start(f32[64]{0:T(128)} %param.18) | copy-start | bytes 772
  24.0 172.6 %all-gather.2.cloned.1.call-start = ((), (), s32[]{:S(2)}) async-start(), calls=%async_computation.1 | async-start | bytes 6291456 | tf_op jit(solution)/shard_map/all_gather | solution.py:52
  206.6 1.9 copy-start.1
Sparse Core Ops, SparseCore 0:
  24.2 128.7 all-reduce.2
  154.5 13.0 all-gather.1
where the time goes:
time: 567 us; the launch traced here: 557 us
  other arithmetic  263 us (46%)
  waiting for transfers between devices  129 us (23%)
  matrix products  60.2 us (11%)
  local copies, waits for them, and re-layouts  44.4 us (8%)
  blocking collectives  40.1 us (7%)
  between operations  20 us (4%)
    another operation x30, other arithmetic, per_device(): lower_factor = jnp.linalg.cholesky(gram)  172 us
    psum x1, waiting for transfers between devices, per_device(): gram_sum, moment = lax.psum((gram_part, moment_part), 'rows')  129 us
    another operation x3, other arithmetic, per_device(): lax.linalg.triangular_solve(lower_factor, moment[:, None], left_side=True...  84.5 us
    psum x1, blocking collectives, per_device(): gram_sum, moment = lax.psum((gram_part, moment_part), 'rows')  40.1 us
    another operation x24, local copies, waits for them, and re-layouts  27.8 us
    another operation x14, matrix products, per_device(): lower_factor = jnp.linalg.cholesky(gram)  22.7 us
  transfers between devices with their start and end apart: 2, of which 1 were waited for; matrix products, arithmetic and copies ran while one was open for 1% of the time, Pallas kernels for 0%

commit v1 on v0

v1 whole, which is shorter than its diff:
```python
import functools

import jax
import jax.numpy as jnp
from jax import lax
from jax.experimental import pallas as pl
from jax.experimental.pallas import tpu as pltpu
from jax.sharding import PartitionSpec as P

BLK = 128
MIC = 16
F32 = jnp.float32
BF16 = jnp.bfloat16
VMEM_LIMIT = 56 * 1024 * 1024


def split2(value):
    high = value.astype(BF16)
    low = (value - high.astype(F32)).astype(BF16)
    return high, low


def dot(left, right, left_dim, right_dim):
    return lax.dot_general(
        left, right, (((left_dim,), (right_dim,)), ((), ())), preferred_element_type=F32
    )


def radices(count):
    found = []
    while count > 1:
        found.append(4 if count % 4 == 0 else 2)
        count //= found[-1]
    return tuple(found)


class Plan:
    def __init__(self, state_total, rows, cols):
        self.state_total = state_total
        self.blocks = state_total // BLK
        self.tiles = self.blocks * (self.blocks + 1) // 2
        self.rows, self.cols = rows, cols
        self.radix = radices(rows)
        self.stride = []
        step = 1
        for f in self.radix:
            self.stride.append(step)
            step *= f
        used = self.tiles * BLK + self.blocks
        unit = 8 * rows * cols
        self.total = -(-used // unit) * unit
        self.piece = self.total // (rows * cols)
        self.moment_row = self.tiles * BLK

    def tile_row(self, i, j):
        return (j * (j + 1) // 2 + i) * BLK

    def digit(self, index, stage):
        return lax.rem(index // self.stride[stage], self.radix[stage])

    def span(self, stage):
        size = self.piece
        for f in self.radix[stage + 1 :]:
            size *= f
        return size


def assemble_kernel(
    plan,
    white_ref,
    states_ref,
    coeffs_ref,
    readings_ref,
    ends_ref,
    conductance_ref,
    balance_rhs_ref,
    prior_ref,
    prior_info_ref,
    *rest,
):
    first = plan.radix[0]
    outs, (sens_ref, left_ref, right_ref, prior_pad, packed) = rest[:first], rest[first:]
    n = plan.state_total
    block_rows = white_ref.shape[0]
    bal_rows = conductance_ref.shape[1]
    prior_rows = prior_ref.shape[0]
    depth = block_rows + bal_rows + BLK
    head = 16
    step = 64

    def put_left(rows, col, high, low):
        left_ref[rows, col : col + high.shape[1]] = high
        left_ref[rows, depth + col : depth + col + high.shape[1]] = high
        left_ref[rows, 2 * depth + col : 2 * depth + col + high.shape[1]] = low

    def put_right(rows, col, high, low):
        right_ref[rows, col : col + high.shape[1]] = high
        right_ref[rows, depth + col : depth + col + high.shape[1]] = low
        right_ref[rows, 2 * depth + col : 2 * depth + col + high.shape[1]] = high

    def head_rows(row):
        top = lax.broadcasted_iota(jnp.int32, (head, row.shape[1]), 0) == 0
        return jnp.where(top, jnp.broadcast_to(row, (head, row.shape[1])), 0.0)

    high, low = split2(head_rows(readings_ref[...]))
    sens_ref[0:head, 0:block_rows] = high
    sens_ref[0:head, block_rows : 2 * block_rows] = high
    sens_ref[0:head, 2 * block_rows : 3 * block_rows] = low
    for at in range(0, n, step):
        ids = lax.broadcasted_iota(jnp.int32, (step, block_rows), 0) + at
        summed = jnp.zeros((step, block_rows), F32)
        for k in range(states_ref.shape[0]):
            summed = summed + jnp.where(ids == states_ref[k : k + 1, :], coeffs_ref[k : k + 1, :], 0.0)
        high, low = split2(summed)
        rows = slice(head + at, head + at + step)
        sens_ref[rows, 0:block_rows] = high
        sens_ref[rows, block_rows : 2 * block_rows] = high
        sens_ref[rows, 2 * block_rows : 3 * block_rows] = low
    white_high, white_low = split2(white_ref[...])
    white_cat = jnp.concatenate([white_high, white_low, white_high], axis=1)
    whitened = dot(sens_ref[...], white_cat, 1, 1)
    for at in range(0, n + head, step):
        size = min(step, n + head - at)
        high, low = split2(whitened[at : at + size, :])
        put_left(slice(at, at + size), 0, high, low)
        if at == 0:
            put_right(slice(0, size - head), 0, high[head:], low[head:])
        else:
            put_right(slice(at - head, at - head + size), 0, high, low)

    conductance = conductance_ref[...]
    high, low = split2(head_rows(conductance * balance_rhs_ref[...]))
    put_left(slice(0, head), block_rows, high, low)
    for at in range(0, n, step):
        ids = lax.broadcasted_iota(jnp.int32, (step, bal_rows), 0) + at
        value = jnp.where(ids == ends_ref[0:1, :], conductance, 0.0)
        value = value + jnp.where(ids == ends_ref[1:2, :], -conductance, 0.0)
        high, low = split2(value)
        put_left(slice(head + at, head + at + step), block_rows, high, low)
        put_right(slice(at, at + step), block_rows, high, low)

    prior_col = block_rows + bal_rows
    prior_pad[...] = jnp.zeros_like(prior_pad)
    prior_pad[0:prior_rows, 0:n] = prior_ref[...]
    info = jnp.concatenate(
        [prior_info_ref[...], jnp.zeros((1, BLK - prior_rows), F32)], axis=1
    )
    high, low = split2(head_rows(info))
    put_left(slice(0, head), prior_col, high, low)
    for at in range(0, n, BLK):
        high, low = split2(prior_pad[:, at : at + BLK].T)
        put_left(slice(head + at, head + at + BLK), prior_col, high, low)
        put_right(slice(at, at + BLK), prior_col, high, low)

    packed[plan.moment_row :, :] = jnp.zeros((plan.total - plan.moment_row, BLK), F32)
    wide = 2 * BLK
    for at in range(0, n, wide):
        out = dot(left_ref[0 : head + at + wide, :], right_ref[at : at + wide, :], 1, 1)
        for part in range(2):
            j = at // BLK + part
            lanes = slice(part * BLK, (part + 1) * BLK)
            packed[plan.moment_row + j : plan.moment_row + j + 1, :] = out[0:1, lanes]
            for i in range(j + 1):
                row = plan.tile_row(i, j)
                packed[row : row + BLK, :] = out[head + i * BLK : head + (i + 1) * BLK, lanes]

    me, core = lax.axis_index("rows"), lax.axis_index("cols")
    span = plan.span(0)
    for d in range(first):
        at = (core * plan.radix[0] + (plan.digit(me, 0) ^ d)) * span
        outs[d][...] = packed[pl.ds(pl.multiple_of(at, 8), span), :]


def sum_kernel(plan, stage, *refs):
    before, after = plan.radix[stage - 1], plan.radix[stage]
    ins, outs = refs[:before], refs[before:]
    mine = plan.digit(lax.axis_index("rows"), stage)
    span = plan.span(stage)
    for d in range(after):
        rows = pl.ds(pl.multiple_of((mine ^ d) * span, 8), span)
        total = ins[0][rows, :]
        for other in ins[1:]:
            total = total + other[rows, :]
        outs[d][...] = total


def factor_block(d_ref, inv_ref, cast_ref, strip_ref, row_ref):
    lane = lax.broadcasted_iota(jnp.int32, (MIC, BLK), 1)
    sub = lax.broadcasted_iota(jnp.int32, (MIC, BLK), 0)
    for m in range(BLK // MIC):
        r0 = m * MIC
        strip = d_ref[r0 : r0 + MIC, :]
        top, bottom = strip[0:8, :], strip[8:16, :]
        for c in range(MIC):
            col = slice(r0 + c, r0 + c + 1)
            if c < 8:
                cast_ref[c * MIC : c * MIC + 8, :] = jnp.broadcast_to(top[:, col], (8, BLK))
            cast_ref[c * MIC + 8 : c * MIC + 16, :] = jnp.broadcast_to(bottom[:, col], (8, BLK))
        inside = (lane >= r0) & (lane < r0 + MIC)
        strip_ref[...] = jnp.where(inside, jnp.where(lane == r0 + sub, 1.0, 0.0), strip)
        s = [[cast_ref[c * MIC + i : c * MIC + i + 1, :] if i >= c else None for c in range(MIC)] for i in range(MIC)]
        rows = [strip_ref[i : i + 1, :] for i in range(MIC)]
        for j in range(MIC):
            scale = lax.rsqrt(s[j][j])
            u = [s[i][j] * scale if i > j else None for i in range(MIC)]
            for c in range(j + 1, MIC):
                for i in range(c, MIC):
                    s[i][c] = s[i][c] - u[i] * u[c]
            done = rows[j] * scale
            row_ref[j : j + 1, :] = done
            for i in range(j + 1, MIC):
                rows[i] = rows[i] - u[i] * done
        solved = row_ref[...]
        inv_ref[r0 : r0 + MIC, :] = jnp.where(lane < r0 + MIC, solved, 0.0)
        if r0 + MIC < BLK:
            high, low = split2(solved)
            fix = dot(
                jnp.concatenate([high, high, low], axis=0),
                jnp.concatenate([high, low, high], axis=0),
                0,
                0,
            )
            lanes = lax.broadcasted_iota(jnp.int32, (BLK - r0 - MIC, BLK), 1)
            keep = (lanes < r0) | (lanes >= r0 + MIC)
            left = jnp.where(keep, d_ref[r0 + MIC :, :], 0.0)
            d_ref[r0 + MIC :, :] = left - fix[r0 + MIC :, :]


def factor_kernel(plan, out_rows, *refs):
    first, cols = plan.radix[0], plan.cols
    ins = refs[: first * cols]
    trans_ref, r_ref, z_ref, x_ref = refs[first * cols : first * cols + 4]
    packed, d_ref, inv_ref, cast_ref, strip_ref, row_ref, left_ref, right_ref, full_ref, z_all, sem = refs[
        first * cols + 4 :
    ]
    n, nb = plan.state_total, plan.blocks
    width = trans_ref.shape[1]
    me, core = lax.axis_index("rows"), lax.axis_index("cols")

    copies = []
    inner = plan.span(0) // plan.piece
    for e in range(cols):
        for d0 in range(first):
            for f in range(inner):
                place = (core ^ e) * first + (plan.digit(me, 0) ^ d0)
                left = f
                size = inner
                for stage in range(1, len(plan.radix)):
                    size //= plan.radix[stage]
                    place = place * plan.radix[stage] + (plan.digit(me, stage) ^ (left // size))
                    left %= size
                copy = pltpu.make_async_copy(
                    ins[e * first + d0].at[pl.ds(f * plan.piece, plan.piece), :],
                    packed.at[pl.ds(pl.multiple_of(place * plan.piece, 8), plan.piece), :],
                    sem.at[(e * first + d0) * inner + f],
                )
                copy.start()
                copies.append(copy)
    full_ref[...] = jnp.zeros_like(full_ref)
    for copy in copies:
        copy.wait()

    x_total = jnp.zeros((1, width), F32)
    row_id = lax.broadcasted_iota(jnp.int32, (BLK, BLK), 0)
    col_id = lax.broadcasted_iota(jnp.int32, (BLK, BLK), 1)
    for k in range(nb):
        lo = k * BLK
        moment = jnp.broadcast_to(packed[plan.moment_row + k : plan.moment_row + k + 1, :], (BLK, BLK)).T
        tiles = [packed[plan.tile_row(k, j) : plan.tile_row(k, j) + BLK, :] for j in range(k, nb)]
        panel = jnp.concatenate(tiles + [trans_ref[lo : lo + BLK, :], moment], axis=1)
        if k:
            panel = panel - dot(left_ref[lo : lo + BLK, 0 : 3 * lo], right_ref[0 : 3 * lo, lo:], 1, 0)
        d_ref[...] = panel[:, 0:BLK]
        factor_block(d_ref, inv_ref, cast_ref, strip_ref, row_ref)
        inv_high, inv_low = split2(inv_ref[...])
        high, low = split2(panel)
        done = dot(
            jnp.concatenate([inv_high, inv_high, inv_low], axis=1),
            jnp.concatenate([high, low, high], axis=0),
            1,
            0,
        )
        full_ref[lo : lo + BLK, lo : lo + BLK] = jnp.where(col_id >= row_id, done[:, 0:BLK], 0.0)
        if k + 1 < nb:
            full_ref[lo : lo + BLK, lo + BLK :] = done[:, BLK : n - lo]
            high, low = split2(done[:, BLK:])
            right_ref[3 * lo : 3 * lo + BLK, lo + BLK :] = high
            right_ref[3 * lo + BLK : 3 * lo + 2 * BLK, lo + BLK :] = low
            right_ref[3 * lo + 2 * BLK : 3 * lo + 3 * BLK, lo + BLK :] = high
            for j in range(k + 1, nb):
                high, low = split2(done[:, (j - k) * BLK : (j - k + 1) * BLK].T)
                left_ref[j * BLK : (j + 1) * BLK, 3 * lo : 3 * lo + 3 * BLK] = jnp.concatenate(
                    [high, high, low], axis=1
                )
        z_cast = done[:, n - lo + width :]
        z_all[:, lo : lo + BLK] = z_cast.T[0:1, :]
        for at in range(0, width, BLK):
            part = jnp.sum(done[:, n - lo + at : n - lo + at + BLK] * z_cast, axis=0, keepdims=True)
            if k:
                part = part + x_ref[:, at : at + BLK]
            x_ref[:, at : at + BLK] = part

    rows = pl.ds(pl.multiple_of(me * out_rows, 8), out_rows)
    lanes = pl.ds(pl.multiple_of(core * width, BLK), width)
    r_ref[...] = full_ref[rows, lanes]
    z_ref[...] = z_all[:, lanes]


def per_device(
    whitening,
    sensor_states,
    sensor_coefficients,
    sensor_readings,
    conduit_endpoints,
    conductance,
    balance_right_side,
    prior_root_factor,
    prior_information,
    transition,
):
    n = prior_root_factor.shape[1]
    rows, cols = lax.axis_size("rows"), lax.axis_size("cols")
    plan = Plan(n, rows, cols)
    radix = plan.radix
    params = pltpu.CompilerParams(vmem_limit_bytes=VMEM_LIMIT)
    block_rows, bal_rows = whitening.shape[0], conductance.shape[0]
    depth = block_rows + bal_rows + BLK

    def piece_type(size):
        return jax.ShapeDtypeStruct((size, BLK), F32)

    parts = pl.pallas_call(
        functools.partial(assemble_kernel, plan),
        out_shape=[piece_type(plan.span(0))] * radix[0],
        scratch_shapes=[
            pltpu.VMEM((n + 16, 3 * block_rows), BF16),
            pltpu.VMEM((n + 16, 3 * depth), BF16),
            pltpu.VMEM((n, 3 * depth), BF16),
            pltpu.VMEM((BLK, n), F32),
            pltpu.VMEM((plan.total, BLK), F32),
        ],
        compiler_params=params,
        name="assemble",
    )(
        whitening,
        sensor_states.T,
        sensor_coefficients.T,
        sensor_readings[None, :],
        conduit_endpoints.T,
        conductance[None, :],
        balance_right_side[None, :],
        prior_root_factor,
        prior_information[None, :],
    )

    def exchange(stage, rel, block):
        flip = rel * plan.stride[stage]
        return lax.ppermute(block, "rows", [(i, i ^ flip) for i in range(rows)])

    for stage in range(len(radix)):
        got = [parts[0]] + [exchange(stage, d, parts[d]) for d in range(1, radix[stage])]
        if stage + 1 < len(radix):
            parts = pl.pallas_call(
                functools.partial(sum_kernel, plan, stage + 1),
                out_shape=[piece_type(plan.span(stage + 1))] * radix[stage + 1],
                compiler_params=params,
                name="partial_sums",
            )(*got)
        else:
            block = functools.reduce(jnp.add, got)
    for stage in reversed(range(len(radix))):
        got = [block] + [exchange(stage, d, block) for d in range(1, radix[stage])]
        if stage:
            block = jnp.concatenate(got, axis=0)
    swap = [(i, i ^ 1) for i in range(cols)]
    both = got + [lax.ppermute(block, "cols", swap) for block in got]

    width = n // cols
    out_rows = n // rows
    wide = n + width + BLK
    anywhere = pl.BlockSpec(memory_space=pl.ANY)
    vmem = pl.BlockSpec(memory_space=pltpu.VMEM)
    r_post, z_post, x_next = pl.pallas_call(
        functools.partial(factor_kernel, plan, out_rows),
        out_shape=[
            jax.ShapeDtypeStruct((out_rows, width), F32),
            jax.ShapeDtypeStruct((1, width), F32),
            jax.ShapeDtypeStruct((1, width), F32),
        ],
        in_specs=[anywhere] * len(both) + [vmem],
        scratch_shapes=[
            pltpu.VMEM((plan.total, BLK), F32),
            pltpu.VMEM((BLK, BLK), F32),
            pltpu.VMEM((BLK, BLK), F32),
            pltpu.VMEM((MIC * MIC, BLK), F32),
            pltpu.VMEM((MIC, BLK), F32),
            pltpu.VMEM((MIC, BLK), F32),
            pltpu.VMEM((n, 3 * n), BF16),
            pltpu.VMEM((3 * n, wide), BF16),
            pltpu.VMEM((n, n), F32),
            pltpu.VMEM((1, n), F32),
            pltpu.SemaphoreType.DMA((rows * cols,)),
        ],
        compiler_params=params,
        name="factor",
    )(*both, transition.T)
    return (r_post, z_post[0], x_next[0])


def solution(mesh):
    in_specs = (
        P("rows", None),
        P("rows", None),
        P("rows", None),
        P("rows"),
        P("rows", None),
        P("rows"),
        P("rows"),
        P("rows", None),
        P("rows"),
        P("cols", None),
    )
    out_specs = (P("rows", "cols"), P("cols"), P("cols"))
    return jax.shard_map(
        per_device, mesh=mesh, in_specs=in_specs, out_specs=out_specs, check_vma=False
    )
```

time: 567 us -> 113 us (0.20); the launches traced: 557 us -> 112 us
  other arithmetic: 263 us -> 0.93 us
  waiting for transfers between devices: 129 us -> 34.4 us
  matrix products: 60.2 us -> 0 us
  Pallas kernels: 0 us -> 54.8 us
  local copies, waits for them, and re-layouts: 44.4 us -> 4.06 us
  blocking collectives: 40.1 us -> 0 us
  between operations: 20 us -> 0.93 us
  starting transfers between devices: 0.08 us -> 17.4 us
    another operation x33 -> x0, other arithmetic: 257 us -> none  [the longest x30 172 us: per_device(): lower_factor = jnp.linalg.cholesky(gram)]
    psum x1 -> x0, waiting for transfers between devices: 129 us -> none  [per_device(): gram_sum, moment = lax.psum((gram_part, moment_part), 'rows')]
    pallas_call x0 -> x3, Pallas kernels: none -> 54.8 us  [the longest x1 45.1 us: per_device(): pl.pallas_call(functools.partial(factor_kernel, plan, out_rows), out_shap...]
    another operation x44 -> x0, matrix products: 43.2 us -> none  [the longest x14 22.7 us: per_device(): lower_factor = jnp.linalg.cholesky(gram)]
    psum x1 -> x0, blocking collectives: 40.1 us -> none  [per_device(): gram_sum, moment = lax.psum((gram_part, moment_part), 'rows')]
    ppermute x0 -> x16, waiting for transfers between devices: none -> 34.4 us  [the longest x12 34.4 us: exchange(): return lax.ppermute(block, 'rows', [(i, i ^ flip) for i in range(rows)])]
    another operation x39 -> x0, local copies, waits for them, and re-layouts: 31.4 us -> none
    ppermute x0 -> x16, starting transfers between devices: none -> 17.4 us  [the longest x12 16.9 us: exchange(): return lax.ppermute(block, 'rows', [(i, i ^ flip) for i in range(rows)])]
  transfers between devices with their start and end apart: 2 -> 16, of which waited for: 1 -> 9; matrix products, arithmetic and copies ran while one was open for 1% -> 2% of each run, Pallas kernels for 0% -> 0%
where the time goes in v1:
time: 113 us; the launch traced here: 112 us
  Pallas kernels  54.8 us (48%)
  waiting for transfers between devices  34.4 us (30%)
  starting transfers between devices  17.4 us (15%)
  local copies, waits for them, and re-layouts  4.06 us (4%)
    pallas_call x1, Pallas kernels, per_device(): pl.pallas_call(functools.partial(factor_kernel, plan, out_rows), out_shap...  45.1 us
    ppermute x12, waiting for transfers between devices, exchange(): return lax.ppermute(block, 'rows', [(i, i ^ flip) for i in range(rows)])  34.4 us
    ppermute x12, starting transfers between devices, exchange(): return lax.ppermute(block, 'rows', [(i, i ^ flip) for i in range(rows)])  16.9 us
    pallas_call x1, Pallas kernels, per_device(): pl.pallas_call(functools.partial(assemble_kernel, plan), out_shape=[piece...  7.68 us
    unnamed x17, local copies, waits for them, and re-layouts  2.67 us
  transfers between devices with their start and end apart: 16, of which 9 were waited for; matrix products, arithmetic and copies ran while one was open for 2% of the time, Pallas kernels for 0%

profile of v1, /device:TPU:0, one launch (start us, length us, event | category | flops | bytes accessed | tf_op | source)
XLA Modules:
  0.0 112.5 jit_solution(8331853589063623869)
XLA Ops:
  0.6 0.0 copy-start
  0.6 1.4 %broadcast_in_dim.12.readings_ref = f32[1,384]{1,0:T(1,128)} reshape(f32[384]{0:T(512)} %param.13) | data formatting | bytes 3072 | tf_op jit(solution)/shard_map/broadcast_in_dim | solution.py:348
  2.0 7.7 %assemble.1 = (f32[608,128]{1,0:T(8,128)}, f32[608,128]{1,0:T(8,128)}, f32[608,128]{1,0:T(8,128)}, f32[608,128]{1,0:T(8,128)}) custom-call(f32[384,384]{1,0:T(8,128)} %white_ref.1, s32[4,384]{1,0:T(4,128)} %bitcast.10, f32[4,384]{1,0:T(4,128)} %bitcast.11, f32[1,384]{1,0:T(1,128)} %broadcast_in_dim.12.readings_ref, s32[2,128]{1,0:T(2,128)} %bitcast.12, ...), custom_call_target="tpu_custom_call" | custom-call | tf_op jit(solution)/shard_map/assemble/pallas_call | solution.py:332
  9.7 2.9 %collective-permute-start = (f32[608,128]{1,0:T(8,128)}, f32[608,128]{1,0:T(8,128)S(1)}, u32[]{:S(2)}, u32[]{:S(2)}) collective-permute-start(f32[608,128]{1,0:T(8,128)} %get-tuple-element.15), channel_id=1, source_target_pairs={{0,2},{2,0},{4,6},{6,4},{8,10},{10,8},{12,14},{14,12},{16,18},{18,... | collective-permute-start | bytes 933896 | tf_op jit(solution)/shard_map/ppermute | solution.py:358
  12.7 1.5 %collective-permute-start.1 = (f32[608,128]{1,0:T(8,128)}, f32[608,128]{1,0:T(8,128)S(1)}, u32[]{:S(2)}, u32[]{:S(2)}) collective-permute-start(f32[608,128]{1,0:T(8,128)} %get-tuple-element.16), channel_id=1, source_target_pairs={{0,4},{2,6},{4,0},{6,2},{8,12},{10,14},{12,8},{14,10},{16,20},{18,... | collective-permute-start | bytes 933896 | tf_op jit(solution)/shard_map/ppermute | solution.py:358
  14.2 0.0 collective-permute-start.2
  14.2 6.9 %collective-permute-done.refs_1_ = f32[608,128]{1,0:T(8,128)S(1)} collective-permute-done((f32[608,128]{1,0:T(8,128)}, f32[608,128]{1,0:T(8,128)S(1)}, u32[]{:S(2)}, u32[]{:S(2)}) %collective-permute-start) | collective-permute-done | bytes 311328 | tf_op jit(solution)/shard_map/ppermute | solution.py:358
  21.1 0.0 copy-start.5
  21.1 7.3 %collective-permute-done.1.refs_2_ = f32[608,128]{1,0:T(8,128)S(1)} collective-permute-done((f32[608,128]{1,0:T(8,128)}, f32[608,128]{1,0:T(8,128)S(1)}, u32[]{:S(2)}, u32[]{:S(2)}) %collective-permute-start.1) | collective-permute-done | bytes 311328 | tf_op jit(solution)/shard_map/ppermute | solution.py:358
  28.4 0.0 copy-start.6
  28.4 0.0 collective-permute-done.2.refs_3_
  28.4 0.0 copy-start.7
  28.4 0.0 copy-done.5
  28.4 0.7 copy-done.6
  29.1 0.1 copy-done.7
  29.2 2.0 %partial_sums.1 = (f32[152,128]{1,0:T(8,128)}, f32[152,128]{1,0:T(8,128)}, f32[152,128]{1,0:T(8,128)}, f32[152,128]{1,0:T(8,128)}) custom-call(f32[608,128]{1,0:T(8,128)} %get-tuple-element.14.refs_0_, f32[608,128]{1,0:T(8,128)} %copy-done.5, f32[608,128]{1,0:T(8,128)} %copy-done.6, f32[608,128]{1,0:T(8,128)} %copy-done.7), custom_call_target="tpu_custom_call" | custom-call | tf_op jit(solution)/shard_map/partial_sums/pallas_call | solution.py:363
  31.2 1.6 %collective-permute-start.3 = (f32[152,128]{1,0:T(8,128)}, f32[152,128]{1,0:T(8,128)S(1)}, u32[]{:S(2)}, u32[]{:S(2)}) collective-permute-start(f32[152,128]{1,0:T(8,128)} %get-tuple-element.19), channel_id=1, source_target_pairs={{0,8},{2,10},{4,12},{6,14},{8,0},{10,2},{12,4},{14,6},{16,24},{18,... | collective-permute-start | bytes 233480 | tf_op jit(solution)/shard_map/ppermute | solution.py:358
  32.8 2.6 %collective-permute-start.4 = (f32[152,128]{1,0:T(8,128)}, f32[152,128]{1,0:T(8,128)S(1)}, u32[]{:S(2)}, u32[]{:S(2)}) collective-permute-start(f32[152,128]{1,0:T(8,128)} %get-tuple-element.20), channel_id=1, source_target_pairs={{0,16},{2,18},{4,20},{6,22},{8,24},{10,26},{12,28},{14,30},{16,0},... | collective-permute-start | bytes 233480 | tf_op jit(solution)/shard_map/ppermute | solution.py:358
  35.4 0.2 collective-permute-start.5
  35.6 0.9 collective-permute-done.3
  36.4 3.5 %collective-permute-done.4 = f32[152,128]{1,0:T(8,128)S(1)} collective-permute-done((f32[152,128]{1,0:T(8,128)}, f32[152,128]{1,0:T(8,128)S(1)}, u32[]{:S(2)}, u32[]{:S(2)}) %collective-permute-start.4) | collective-permute-done | bytes 77856 | tf_op jit(solution)/shard_map/ppermute | solution.py:358
  39.9 1.9 %collective-permute-done.5 = f32[152,128]{1,0:T(8,128)S(1)} collective-permute-done((f32[152,128]{1,0:T(8,128)}, f32[152,128]{1,0:T(8,128)S(1)}, u32[]{:S(2)}, u32[]{:S(2)}) %collective-permute-start.5) | collective-permute-done | bytes 77856 | tf_op jit(solution)/shard_map/ppermute | solution.py:358
  41.8 0.9 add_add_fusion
  42.8 1.5 %collective-permute-start.8 = (f32[152,128]{1,0:T(8,128)S(1)}, f32[152,128]{1,0:T(8,128)S(1)}, u32[]{:S(2)}, u32[]{:S(2)}) collective-permute-start(f32[152,128]{1,0:T(8,128)S(1)} %add_add_fusion), channel_id=1, source_target_pairs={{0,24},{2,26},{4,28},{6,30},{8,16},{10,18},{12,20},{14,22},{16,8},... | collective-permute-start | bytes 233480 | tf_op jit(solution)/shard_map/ppermute | solution.py:358
  44.3 0.7 collective-permute-start.7
  45.0 2.3 %collective-permute-start.6 = (f32[152,128]{1,0:T(8,128)S(1)}, f32[152,128]{1,0:T(8,128)S(1)}, u32[]{:S(2)}, u32[]{:S(2)}) collective-permute-start(f32[152,128]{1,0:T(8,128)S(1)} %add_add_fusion), channel_id=1, source_target_pairs={{0,8},{2,10},{4,12},{6,14},{8,0},{10,2},{12,4},{14,6},{16,24},{18,... | collective-permute-start | bytes 233480 | tf_op jit(solution)/shard_map/ppermute | solution.py:358
  47.2 1.9 %collective-permute-done.8 = f32[152,128]{1,0:T(8,128)S(1)} collective-permute-done((f32[152,128]{1,0:T(8,128)S(1)}, f32[152,128]{1,0:T(8,128)S(1)}, u32[]{:S(2)}, u32[]{:S(2)}) %collective-permute-start.8) | collective-permute-done | bytes 77856 | tf_op jit(solution)/shard_map/ppermute | solution.py:358
  49.1 1.6 %collective-permute-done.7 = f32[152,128]{1,0:T(8,128)S(1)} collective-permute-done((f32[152,128]{1,0:T(8,128)S(1)}, f32[152,128]{1,0:T(8,128)S(1)}, u32[]{:S(2)}, u32[]{:S(2)}) %collective-permute-start.7) | collective-permute-done | bytes 77856 | tf_op jit(solution)/shard_map/ppermute | solution.py:358
  50.7 0.0 collective-permute-done.6
  50.7 0.0 copy-start.1
  50.7 1.6 %collective-permute-start.11 = (f32[608,128]{1,0:T(8,128)S(1)}, f32[608,128]{1,0:T(8,128)S(1)}, u32[]{:S(2)}, u32[]{:S(2)}) collective-permute-start(f32[608,128]{1,0:T(8,128)S(1)} %pad_maximum_fusion.refs_0_), channel_id=1, source_target_pairs={{0,6},{2,4},{4,2},{6,0},{8,14},{10,12},{12,10},{14,8},{16,22},{18,... | collective-permute-start | bytes 933896 | tf_op jit(solution)/shard_map/ppermute | solution.py:358
  52.3 1.1 collective-permute-start.10
  53.4 0.9 collective-permute-start.9
  54.3 0.0 collective-permute-start.12
  54.3 7.3 %collective-permute-done.11.refs_3_ = f32[608,128]{1,0:T(8,128)S(1)} collective-permute-done((f32[608,128]{1,0:T(8,128)S(1)}, f32[608,128]{1,0:T(8,128)S(1)}, u32[]{:S(2)}, u32[]{:S(2)}) %collective-permute-start.11) | collective-permute-done | bytes 311328 | tf_op jit(solution)/shard_map/ppermute | solution.py:358
  61.5 0.0 copy-start.2
  61.5 0.0 collective-permute-start.15
  61.5 3.2 %collective-permute-done.10.refs_2_ = f32[608,128]{1,0:T(8,128)S(1)} collective-permute-done((f32[608,128]{1,0:T(8,128)S(1)}, f32[608,128]{1,0:T(8,128)S(1)}, u32[]{:S(2)}, u32[]{:S(2)}) %collective-permute-start.10) | collective-permute-done | bytes 311328 | tf_op jit(solution)/shard_map/ppermute | solution.py:358
  64.8 0.0 copy-start.3
  64.8 0.0 collective-permute-start.14
  64.8 0.0 collective-permute-done.9.refs_1_
  64.8 0.0 copy-start.4
  64.8 0.5 collective-permute-start.13
  65.3 0.0 copy-done
  65.3 1.8 %copy.13 = f32[512,1024]{0,1:T(8,128)} copy(f32[512,1024]{1,0:T(8,128)S(1)} %copy-done) | data formatting | bytes 4194304 | tf_op args[9]
  67.1 0.0 collective-permute-done.12.refs_4_
  67.1 0.0 collective-permute-done.15.refs_7_
  67.1 0.0 collective-permute-done.14.refs_6_
  67.1 0.0 collective-permute-done.13.refs_5_
  67.1 0.0 copy-done.1
  67.2 0.0 copy-done.2
  67.2 0.0 copy-done.3
  67.2 0.0 copy-done.4
  67.2 45.1 %factor.1 = (f32[64,512]{1,0:T(8,128)}, f32[1,512]{1,0:T(1,128)}, f32[1,512]{1,0:T(1,128)}) custom-call(f32[608,128]{1,0:T(8,128)} %copy-done.1, f32[608,128]{1,0:T(8,128)} %copy-done.4, f32[608,128]{1,0:T(8,128)} %copy-done.3, f32[608,128]{1,0:T(8,128)} %copy-done.2, f32[608,128]{1,0:T(8,128)} %collective-permute-done.12.refs_4_, ...), custom_call_target="tpu_custom_call" | custom-call | tf_op jit(solution)/shard_map/factor/pallas_call | solution.py:383
  (1 shorter events, 0.0 us)
Async XLA Ops:
  0.6 64.7 %copy-start = (f32[512,1024]{1,0:T(8,128)S(1)}, f32[512,1024]{1,0:T(8,128)}, u32[]{:S(2)}) copy-start(f32[512,1024]{1,0:T(8,128)} %param.19) | copy-start | bytes 6291460
  9.7 11.3 %collective-permute-start = (f32[608,128]{1,0:T(8,128)}, f32[608,128]{1,0:T(8,128)S(1)}, u32[]{:S(2)}, u32[]{:S(2)}) collective-permute-start(f32[608,128]{1,0:T(8,128)} %get-tuple-element.15), channel_id=1, source_target_pairs={{0,2},{2,0},{4,6},{6,4},{8,10},{10,8},{12,14},{14,12},{16,18},{18,... | collective-permute-start | bytes 933896 | tf_op jit(solution)/shard_map/ppermute | solution.py:358
  12.7 15.7 %collective-permute-start.1 = (f32[608,128]{1,0:T(8,128)}, f32[608,128]{1,0:T(8,128)S(1)}, u32[]{:S(2)}, u32[]{:S(2)}) collective-permute-start(f32[608,128]{1,0:T(8,128)} %get-tuple-element.16), channel_id=1, source_target_pairs={{0,4},{2,6},{4,0},{6,2},{8,12},{10,14},{12,8},{14,10},{16,20},{18,... | collective-permute-start | bytes 933896 | tf_op jit(solution)/shard_map/ppermute | solution.py:358
  14.2 14.2 %collective-permute-start.2 = (f32[608,128]{1,0:T(8,128)}, f32[608,128]{1,0:T(8,128)S(1)}, u32[]{:S(2)}, u32[]{:S(2)}) collective-permute-start(f32[608,128]{1,0:T(8,128)} %get-tuple-element.17), channel_id=1, source_target_pairs={{0,6},{2,4},{4,2},{6,0},{8,14},{10,12},{12,10},{14,8},{16,22},{18,... | collective-permute-start | bytes 933896 | tf_op jit(solution)/shard_map/ppermute | solution.py:358
  21.1 7.3 %copy-start.5 = (f32[608,128]{1,0:T(8,128)}, f32[608,128]{1,0:T(8,128)S(1)}, u32[]{:S(2)}) copy-start(f32[608,128]{1,0:T(8,128)S(1)} %collective-permute-done.refs_1_) | copy-start | bytes 933892
  28.4 0.7 copy-start.6
  28.4 0.8 copy-start.7
  31.2 5.2 %collective-permute-start.3 = (f32[152,128]{1,0:T(8,128)}, f32[152,128]{1,0:T(8,128)S(1)}, u32[]{:S(2)}, u32[]{:S(2)}) collective-permute-start(f32[152,128]{1,0:T(8,128)} %get-tuple-element.19), channel_id=1, source_target_pairs={{0,8},{2,10},{4,12},{6,14},{8,0},{10,2},{12,4},{14,6},{16,24},{18,... | collective-permute-start | bytes 233480 | tf_op jit(solution)/shard_map/ppermute | solution.py:358
  32.8 7.2 %collective-permute-start.4 = (f32[152,128]{1,0:T(8,128)}, f32[152,128]{1,0:T(8,128)S(1)}, u32[]{:S(2)}, u32[]{:S(2)}) collective-permute-start(f32[152,128]{1,0:T(8,128)} %get-tuple-element.20), channel_id=1, source_target_pairs={{0,16},{2,18},{4,20},{6,22},{8,24},{10,26},{12,28},{14,30},{16,0},... | collective-permute-start | bytes 233480 | tf_op jit(solution)/shard_map/ppermute | solution.py:358
  35.4 6.5 %collective-permute-start.5 = (f32[152,128]{1,0:T(8,128)}, f32[152,128]{1,0:T(8,128)S(1)}, u32[]{:S(2)}, u32[]{:S(2)}) collective-permute-start(f32[152,128]{1,0:T(8,128)} %get-tuple-element.21), channel_id=1, source_target_pairs={{0,24},{2,26},{4,28},{6,30},{8,16},{10,18},{12,20},{14,22},{16,8},... | collective-permute-start | bytes 233480 | tf_op jit(solution)/shard_map/ppermute | solution.py:358
  42.8 6.3 %collective-permute-start.8 = (f32[152,128]{1,0:T(8,128)S(1)}, f32[152,128]{1,0:T(8,128)S(1)}, u32[]{:S(2)}, u32[]{:S(2)}) collective-permute-start(f32[152,128]{1,0:T(8,128)S(1)} %add_add_fusion), channel_id=1, source_target_pairs={{0,24},{2,26},{4,28},{6,30},{8,16},{10,18},{12,20},{14,22},{16,8},... | collective-permute-start | bytes 233480 | tf_op jit(solution)/shard_map/ppermute | solution.py:358
  44.3 6.4 %collective-permute-start.7 = (f32[152,128]{1,0:T(8,128)S(1)}, f32[152,128]{1,0:T(8,128)S(1)}, u32[]{:S(2)}, u32[]{:S(2)}) collective-permute-start(f32[152,128]{1,0:T(8,128)S(1)} %add_add_fusion), channel_id=1, source_target_pairs={{0,16},{2,18},{4,20},{6,22},{8,24},{10,26},{12,28},{14,30},{16,0},... | collective-permute-start | bytes 233480 | tf_op jit(solution)/shard_map/ppermute | solution.py:358
  45.0 5.7 %collective-permute-start.6 = (f32[152,128]{1,0:T(8,128)S(1)}, f32[152,128]{1,0:T(8,128)S(1)}, u32[]{:S(2)}, u32[]{:S(2)}) collective-permute-start(f32[152,128]{1,0:T(8,128)S(1)} %add_add_fusion), channel_id=1, source_target_pairs={{0,8},{2,10},{4,12},{6,14},{8,0},{10,2},{12,4},{14,6},{16,24},{18,... | collective-permute-start | bytes 233480 | tf_op jit(solution)/shard_map/ppermute | solution.py:358
  50.7 16.4 %copy-start.1 = (f32[608,128]{1,0:T(8,128)}, f32[608,128]{1,0:T(8,128)S(1)}, u32[]{:S(2)}) copy-start(f32[608,128]{1,0:T(8,128)S(1)} %pad_maximum_fusion.refs_0_) | copy-start | bytes 933892
  50.7 10.8 %collective-permute-start.11 = (f32[608,128]{1,0:T(8,128)S(1)}, f32[608,128]{1,0:T(8,128)S(1)}, u32[]{:S(2)}, u32[]{:S(2)}) collective-permute-start(f32[608,128]{1,0:T(8,128)S(1)} %pad_maximum_fusion.refs_0_), channel_id=1, source_target_pairs={{0,6},{2,4},{4,2},{6,0},{8,14},{10,12},{12,10},{14,8},{16,22},{18,... | collective-permute-start | bytes 933896 | tf_op jit(solution)/shard_map/ppermute | solution.py:358
  52.3 12.5 %collective-permute-start.10 = (f32[608,128]{1,0:T(8,128)S(1)}, f32[608,128]{1,0:T(8,128)S(1)}, u32[]{:S(2)}, u32[]{:S(2)}) collective-permute-start(f32[608,128]{1,0:T(8,128)S(1)} %pad_maximum_fusion.refs_0_), channel_id=1, source_target_pairs={{0,4},{2,6},{4,0},{6,2},{8,12},{10,14},{12,8},{14,10},{16,20},{18,... | collective-permute-start | bytes 933896 | tf_op jit(solution)/shard_map/ppermute | solution.py:358
  53.4 11.4 %collective-permute-start.9 = (f32[608,128]{1,0:T(8,128)S(1)}, f32[608,128]{1,0:T(8,128)S(1)}, u32[]{:S(2)}, u32[]{:S(2)}) collective-permute-start(f32[608,128]{1,0:T(8,128)S(1)} %pad_maximum_fusion.refs_0_), channel_id=1, source_target_pairs={{0,2},{2,0},{4,6},{6,4},{8,10},{10,8},{12,14},{14,12},{16,18},{18,... | collective-permute-start | bytes 933896 | tf_op jit(solution)/shard_map/ppermute | solution.py:358
  54.3 12.8 %collective-permute-start.12 = (f32[608,128]{1,0:T(8,128)S(1)}, f32[608,128]{1,0:T(8,128)}, u32[]{:S(2)}, u32[]{:S(2)}) collective-permute-start(f32[608,128]{1,0:T(8,128)S(1)} %pad_maximum_fusion.refs_0_), channel_id=1, source_target_pairs={{0,1},{1,0},{2,3},{3,2},{4,5},{5,4},{6,7},{7,6},{8,9},{9,8},{10,11... | collective-permute-start | bytes 933896 | tf_op jit(solution)/shard_map/ppermute | solution.py:376
  61.5 5.6 %copy-start.2 = (f32[608,128]{1,0:T(8,128)}, f32[608,128]{1,0:T(8,128)S(1)}, u32[]{:S(2)}) copy-start(f32[608,128]{1,0:T(8,128)S(1)} %collective-permute-done.11.refs_3_) | copy-start | bytes 933892
  61.5 5.6 %collective-permute-start.15 = (f32[608,128]{1,0:T(8,128)S(1)}, f32[608,128]{1,0:T(8,128)}, u32[]{:S(2)}, u32[]{:S(2)}) collective-permute-start(f32[608,128]{1,0:T(8,128)S(1)} %collective-permute-done.11.refs_3_), channel_id=1, source_target_pairs={{0,1},{1,0},{2,3},{3,2},{4,5},{5,4},{6,7},{7,6},{8,9},{9,8},{10,11... | collective-permute-start | bytes 933896 | tf_op jit(solution)/shard_map/ppermute | solution.py:376
  64.8 2.4 %copy-start.3 = (f32[608,128]{1,0:T(8,128)}, f32[608,128]{1,0:T(8,128)S(1)}, u32[]{:S(2)}) copy-start(f32[608,128]{1,0:T(8,128)S(1)} %collective-permute-done.10.refs_2_) | copy-start | bytes 933892
  64.8 2.3 %collective-permute-start.14 = (f32[608,128]{1,0:T(8,128)S(1)}, f32[608,128]{1,0:T(8,128)}, u32[]{:S(2)}, u32[]{:S(2)}) collective-permute-start(f32[608,128]{1,0:T(8,128)S(1)} %collective-permute-done.10.refs_2_), channel_id=1, source_target_pairs={{0,1},{1,0},{2,3},{3,2},{4,5},{5,4},{6,7},{7,6},{8,9},{9,8},{10,11... | collective-permute-start | bytes 933896 | tf_op jit(solution)/shard_map/ppermute | solution.py:376
  64.8 2.4 %copy-start.4 = (f32[608,128]{1,0:T(8,128)}, f32[608,128]{1,0:T(8,128)S(1)}, u32[]{:S(2)}) copy-start(f32[608,128]{1,0:T(8,128)S(1)} %collective-permute-done.9.refs_1_) | copy-start | bytes 933892
  64.8 2.3 %collective-permute-start.13 = (f32[608,128]{1,0:T(8,128)S(1)}, f32[608,128]{1,0:T(8,128)}, u32[]{:S(2)}, u32[]{:S(2)}) collective-permute-start(f32[608,128]{1,0:T(8,128)S(1)} %collective-permute-done.9.refs_1_), channel_id=1, source_target_pairs={{0,1},{1,0},{2,3},{3,2},{4,5},{5,4},{6,7},{7,6},{8,9},{9,8},{10,11... | collective-permute-start | bytes 933896 | tf_op jit(solution)/shard_map/ppermute | solution.py:376

commit v2 on v0

v2 whole, which is shorter than its diff:
```python
import functools

import jax
import jax.numpy as jnp
from jax import lax
from jax.experimental import pallas as pl
from jax.experimental.pallas import tpu as pltpu
from jax.sharding import PartitionSpec as P

BLK = 128
MIC = 32
GRP = 8
F32 = jnp.float32
BF16 = jnp.bfloat16
VMEM_LIMIT = 48 * 1024 * 1024
ASSEMBLE_VMEM = 63 * 1024 * 1024


def split2(value):
    high = value.astype(BF16)
    low = (value - high.astype(F32)).astype(BF16)
    return high, low


def dot(left, right, left_dim=1, right_dim=0):
    return lax.dot_general(
        left, right, (((left_dim,), (right_dim,)), ((), ())), preferred_element_type=F32
    )


def dot3(left, right, left_dim=1, right_dim=0):
    total = dot(left[0], right[1], left_dim, right_dim) + dot(left[1], right[0], left_dim, right_dim)
    return total + dot(left[0], right[0], left_dim, right_dim)


def radices(count):
    found = []
    while count > 1:
        found.append(4 if count % 4 == 0 else 2)
        count //= found[-1]
    return tuple(found)


class Plan:
    def __init__(self, state_total, rows, cols):
        self.state_total = state_total
        self.blocks = nb = state_total // BLK
        self.rows, self.cols = rows, cols
        self.radix = radices(rows)
        self.stride = []
        step = 1
        for f in self.radix:
            self.stride.append(step)
            step *= f
        self.tiles = nb * (nb + 1) // 2
        unit = 8 * rows * cols
        self.total = -(-self.tiles * BLK // unit) * unit
        self.piece = self.total // (rows * cols)
        self.moment_rows = state_total // 64

    def tile(self, i, j):
        return (sum(self.blocks - k for k in range(i)) + j - i) * BLK


def assemble_kernel(plan, *refs):
    ins, (out_ref, *scratch) = refs[:9], refs[9:]
    here, (sens_hi, sens_lo, at_hi, at_lo, prior_pad, packed, sems) = scratch[:9], scratch[9:]
    copies = [pltpu.make_async_copy(a, b, sems.at[i]) for i, (a, b) in enumerate(zip(ins, here))]
    for copy in copies:
        copy.start()
    (
        white_ref,
        states_ref,
        coeffs_ref,
        readings_ref,
        ends_ref,
        conductance_ref,
        balance_rhs_ref,
        prior_ref,
        prior_info_ref,
    ) = here
    n = plan.state_total
    block_rows = white_ref.shape[0]
    bal_rows = conductance_ref.shape[1]
    prior_rows = prior_ref.shape[0]
    head = 16
    step = 64

    def put(high_ref, low_ref, row, col, value):
        high, low = split2(value)
        high_ref[row : row + value.shape[0], col : col + value.shape[1]] = high
        low_ref[row : row + value.shape[0], col : col + value.shape[1]] = low

    def head_rows(row):
        top = lax.broadcasted_iota(jnp.int32, (head, row.shape[1]), 0) == 0
        return jnp.where(top, jnp.broadcast_to(row, (head, row.shape[1])), 0.0)

    prior_pad[...] = jnp.zeros_like(prior_pad)
    if plan.tiles * BLK < plan.total:
        packed[plan.tiles * BLK :, :] = jnp.zeros((plan.total - plan.tiles * BLK, BLK), F32)
    for copy in copies:
        copy.wait()

    readings = jnp.concatenate(
        [readings_ref[k : k + 1, :] for k in range(readings_ref.shape[0])], axis=1
    )
    put(sens_hi, sens_lo, 0, 0, head_rows(readings))
    for at in range(0, n, step):
        ids = lax.broadcasted_iota(jnp.int32, (step, block_rows), 0) + at
        summed = jnp.zeros((step, block_rows), F32)
        for k in range(states_ref.shape[0]):
            summed = summed + jnp.where(ids == states_ref[k : k + 1, :], coeffs_ref[k : k + 1, :], 0.0)
        put(sens_hi, sens_lo, head + at, 0, summed)
    white = split2(white_ref[...])
    whitened = dot3((sens_hi[...], sens_lo[...]), white, 1, 1)
    for at in range(0, n + head, step):
        size = min(step, n + head - at)
        put(at_hi, at_lo, at, 0, whitened[at : at + size, :])

    conductance = conductance_ref[...]
    put(at_hi, at_lo, 0, block_rows, head_rows(conductance * balance_rhs_ref[...]))
    for at in range(0, n, step):
        ids = lax.broadcasted_iota(jnp.int32, (step, bal_rows), 0) + at
        value = jnp.where(ids == ends_ref[0:1, :], conductance, 0.0)
        value = value + jnp.where(ids == ends_ref[1:2, :], -conductance, 0.0)
        put(at_hi, at_lo, head + at, block_rows, value)

    prior_col = block_rows + bal_rows
    prior_pad[0:prior_rows, :] = prior_ref[...]
    info = jnp.concatenate([prior_info_ref[...], jnp.zeros((1, BLK - prior_rows), F32)], axis=1)
    put(at_hi, at_lo, 0, prior_col, head_rows(info))
    for at in range(0, n, BLK):
        put(at_hi, at_lo, head + at, prior_col, prior_pad[:, at : at + BLK].T)

    wide = 2 * BLK
    moments = []
    for at in range(0, n, wide):
        stop = head + at + wide
        out = dot3(
            (at_hi[0:stop, :], at_lo[0:stop, :]),
            (at_hi[head + at : stop, :], at_lo[head + at : stop, :]),
            1,
            1,
        )
        moments.append(out[0:1, :])
        for part in range(2):
            j = at // BLK + part
            for i in range(j + 1):
                row = plan.tile(i, j)
                packed[row : row + BLK, :] = out[
                    head + i * BLK : head + (i + 1) * BLK, part * BLK : (part + 1) * BLK
                ]
    for k in range(plan.moment_rows):
        row = BLK - plan.moment_rows + k
        source = moments[k * 64 // wide][:, k * 64 % wide : k * 64 % wide + 64]
        packed[row : row + 1, 0:64] = source

    size = plan.rows * plan.piece
    at = lax.axis_index("cols") * size
    out_ref[...] = packed[pl.ds(pl.multiple_of(at, 8), size), :]


def eliminate(s, rows):
    u = [[None] * GRP for _ in range(GRP)]
    pairs, done = [], []
    for p in range(0, GRP, 2):
        a, b, c = s[p][p], s[p + 1][p], s[p + 1][p + 1]
        det = a * c - b * b
        root_det = lax.rsqrt(det)
        root_a = lax.rsqrt(a)
        second = root_a * root_det
        inv = root_det * root_det
        u[p + 1][p] = b * root_a
        left = {}
        for i in range(p + 2, GRP):
            one, two = s[i][p], s[i][p + 1]
            cross = a * two - b * one
            left[i] = (c * one - b * two, cross)
            u[i][p] = one * root_a
            u[i][p + 1] = cross * second
        for c_at in range(p + 2, GRP):
            for i in range(c_at, GRP):
                fall = left[i][0] * s[c_at][p] + left[i][1] * s[c_at][p + 1]
                s[i][c_at] = s[i][c_at] - fall * inv
        pairs.append((a, b, root_a, second))
        done.append(rows[p] * root_a)
        done.append((a * rows[p + 1] - b * rows[p]) * second)
        for i in range(p + 2, GRP):
            rows[i] = rows[i] - (u[i][p] * done[p] + u[i][p + 1] * done[p + 1])
    return u, pairs, done


def factor_block(d_ref, inv_ref, cast_ref, times_ref, strip_ref, row_ref, queue):
    lane = lax.broadcasted_iota(jnp.int32, (MIC, BLK), 1)
    sub = lax.broadcasted_iota(jnp.int32, (MIC, BLK), 0)
    groups = MIC // GRP
    slots = groups * (BLK // MIC)
    share = -(-len(queue) // slots)

    def background():
        for _ in range(min(share, len(queue))):
            queue.pop(0)()

    for m in range(BLK // MIC):
        r0 = m * MIC
        strip = d_ref[r0 : r0 + MIC, :]
        inside = (lane >= r0) & (lane < r0 + MIC)
        ready = jnp.where(inside, jnp.where(lane == r0 + sub, 1.0, 0.0), strip)
        low, rest = [], []
        for g in range(groups):
            part = strip[g * GRP : (g + 1) * GRP, :]
            low.append(
                [
                    jnp.broadcast_to(part[:, r0 + c : r0 + c + 1], (GRP, BLK))
                    for c in range((g + 1) * GRP)
                ]
            )
            rest.append(ready[g * GRP : (g + 1) * GRP, :])
        for s in range(groups):
            base = s * GRP * GRP
            for c in range(GRP):
                cast_ref[base + GRP * c : base + GRP * (c + 1), :] = low[s][s * GRP + c]
            strip_ref[s * GRP : (s + 1) * GRP, :] = rest[s]
            splats = [
                [
                    cast_ref[base + GRP * c + i : base + GRP * c + i + 1, :] if i >= c else None
                    for c in range(GRP)
                ]
                for i in range(GRP)
            ]
            background()
            u, pairs, done = eliminate(
                splats, [strip_ref[s * GRP + i : s * GRP + i + 1, :] for i in range(GRP)]
            )
            for j in range(GRP):
                row_ref[s * GRP + j : s * GRP + j + 1, :] = done[j]
            for g in range(s + 1, groups):
                mine = low[g][s * GRP : (s + 1) * GRP]
                for p in range(0, GRP, 2):
                    a, b, root_a, second = pairs[p // 2]
                    one, two = mine[p], mine[p + 1]
                    mine[p] = one * root_a
                    mine[p + 1] = (a * two - b * one) * second
                    for c in range(p + 2, GRP):
                        mine[c] = mine[c] - (mine[p] * u[c][p] + mine[p + 1] * u[c][p + 1])
                times = (s * groups + g) * GRP * GRP
                for j in range(GRP):
                    times_ref[times + GRP * j : times + GRP * (j + 1), :] = mine[j]
                    rest[g] = rest[g] - mine[j] * done[j]
                for h in range(s + 1, g + 1):
                    other = (s * groups + h) * GRP * GRP
                    for c in range(GRP):
                        total = low[g][h * GRP + c]
                        for j in range(0, GRP, 2):
                            at = other + GRP * j + c
                            total = total - (
                                mine[j] * times_ref[at : at + 1, :]
                                + mine[j + 1] * times_ref[at + GRP : at + GRP + 1, :]
                            )
                        low[g][h * GRP + c] = total
        solved = row_ref[...]
        inv_ref[r0 : r0 + MIC, :] = jnp.where(lane < r0 + MIC, solved, 0.0)
        if r0 + MIC < BLK:
            high, low_part = split2(solved)
            fix = dot(
                jnp.concatenate([high, high, low_part], axis=0),
                jnp.concatenate([high, low_part, high], axis=0),
                0,
                0,
            )
            lanes = lax.broadcasted_iota(jnp.int32, (BLK - r0 - MIC, BLK), 1)
            keep = (lanes < r0) | (lanes >= r0 + MIC)
            left = jnp.where(keep, d_ref[r0 + MIC :, :], 0.0)
            d_ref[r0 + MIC :, :] = left - fix[r0 + MIC :, :]
    while queue:
        queue.pop(0)()


def factor_kernel(plan, out_rows, width, *refs):
    radix0, cols, n, nb = plan.radix[0], plan.cols, plan.state_total, plan.blocks
    ins, (trans_hbm, r_ref, z_ref, x_ref, *scratch) = refs[: radix0 * cols], refs[radix0 * cols :]
    (
        packed,
        d_ref,
        inv_ref,
        cast_ref,
        times_ref,
        strip_ref,
        row_ref,
        panel_ref,
        full_ref,
        trans_ref,
        col_ref,
        root_ref,
        *state,
        sems,
        trans_sem,
    ) = scratch
    left, right, z_all = state[:2], state[2:4], state[4]
    me, core = lax.axis_index("rows"), lax.axis_index("cols")

    copies = []
    inner = plan.rows // radix0
    piece = plan.piece
    for e in range(cols):
        for d0 in range(radix0):
            for f in range(inner):
                flip = d0 * plan.stride[0]
                rest, size = f, inner
                for stage in range(1, len(plan.radix)):
                    size //= plan.radix[stage]
                    flip += rest // size * plan.stride[stage]
                    rest %= size
                place = (core ^ e) * plan.rows + (me ^ flip)
                copies.append(
                    pltpu.make_async_copy(
                        ins[e * radix0 + d0].at[pl.ds(f * piece, piece), :],
                        packed.at[pl.ds(pl.multiple_of(place * piece, 8), piece), :],
                        sems.at[len(copies)],
                    )
                )
    trans_copy = pltpu.make_async_copy(trans_hbm, trans_ref, trans_sem)
    for copy in copies:
        copy.start()
    trans_copy.start()
    full_ref[...] = jnp.zeros_like(full_ref)
    for copy in copies:
        copy.wait()

    row_id = lax.broadcasted_iota(jnp.int32, (BLK, BLK), 0)
    col_id = lax.broadcasted_iota(jnp.int32, (BLK, BLK), 1)

    def turned(row):
        return jnp.broadcast_to(row, (BLK, BLK)).T

    tile = packed[0:BLK, :]
    hidden = (row_id >= BLK - plan.moment_rows) & (col_id < 64)
    moments = []
    for k in range(nb):
        at = BLK - plan.moment_rows + 2 * k
        moments.append(jnp.concatenate([tile[at : at + 1, 0:64], tile[at + 1 : at + 2, 0:64]], axis=1))
    packed[0:BLK, :] = jnp.where(hidden, tile.T, tile)

    scales = []
    for k in range(nb):
        row = plan.tile(k, k)
        diagonal = jnp.sum(
            jnp.where(row_id == col_id, packed[row : row + BLK, :], 0.0), axis=0, keepdims=True
        )
        scales.append(lax.rsqrt(diagonal))
        root_ref[k : k + 1, :] = diagonal * scales[k]
        col_ref[k] = turned(scales[k])
    trans_copy.wait()

    def base(k, j):
        if j < nb:
            row = plan.tile(k, j)
            return packed[row : row + BLK, :] * col_ref[k] * scales[j]
        if j < nb + width // BLK:
            at = (j - nb) * BLK
            return trans_ref[k * BLK : (k + 1) * BLK, at : at + BLK] * col_ref[k]
        return turned(moments[k] * scales[k])

    last = nb + width // BLK

    def lanes_of(tiles):
        return slice(tiles[0] * BLK, (tiles[-1] + 1) * BLK)

    def updated(k, tiles):
        value = base(k, tiles[0])
        if len(tiles) > 1:
            value = jnp.concatenate([base(k, j) for j in tiles], axis=1)
        if k:
            rows, done = slice(k * BLK, (k + 1) * BLK), slice(0, k * BLK)
            value = value - dot3(
                [ref[rows, done] for ref in left], [ref[done, lanes_of(tiles)] for ref in right]
            )
        return value

    def prepare(k, tiles):
        panel_ref[k % 2, :, lanes_of(tiles)] = updated(k, tiles)

    z_tile = [None]

    def finish(k, tiles, inverse):
        rows, lanes = slice(k * BLK, (k + 1) * BLK), lanes_of(tiles)
        high, low = split2(panel_ref[k % 2, :, lanes])
        value = dot(inverse, jnp.concatenate([high, low, high], axis=0))
        if k + 1 < nb and tiles[0] > k:
            high, low = split2(value)
            right[0][rows, lanes] = high
            right[1][rows, lanes] = low
        for at, j in enumerate(tiles):
            one = value[:, at * BLK : (at + 1) * BLK]
            if j < nb:
                kept = one * root_ref[j : j + 1, :]
                if j == k:
                    kept = jnp.where(col_id >= row_id, kept, 0.0)
                else:
                    high, low = split2(one.T)
                    left[0][j * BLK : (j + 1) * BLK, rows] = high
                    left[1][j * BLK : (j + 1) * BLK, rows] = low
                full_ref[rows, j * BLK : (j + 1) * BLK] = kept
            elif j < last:
                at_x = (j - nb) * BLK
                part_x = jnp.sum(one * z_tile[0], axis=0, keepdims=True)
                if k:
                    part_x = part_x + x_ref[:, at_x : at_x + BLK]
                x_ref[:, at_x : at_x + BLK] = part_x
            else:
                z_tile[0] = one
                z_all[:, rows] = one.T[0:1, :]

    def groups(first_tile):
        found = [[last]]
        at = first_tile
        while at < last:
            size = 1 if at % 2 or at + 1 >= last or (at < nb <= at + 1) else 2
            found.append(list(range(at, at + size)))
            at += size
        return found

    queue = []
    for k in range(nb):
        d_ref[...] = updated(k, [k])
        panel_ref[k % 2, :, k * BLK : (k + 1) * BLK] = d_ref[...]
        queue += [functools.partial(prepare, k, tiles) for tiles in groups(k + 1)]
        factor_block(d_ref, inv_ref, cast_ref, times_ref, strip_ref, row_ref, queue)
        inv_high, inv_low = split2(inv_ref[...])
        inverse = jnp.concatenate([inv_high, inv_high, inv_low], axis=1)
        if k + 1 < nb:
            finish(k, [k + 1], inverse)
        queue += [functools.partial(finish, k, tiles, inverse) for tiles in groups(min(k + 2, nb))]
        queue.append(functools.partial(finish, k, [k], inverse))
    while queue:
        queue.pop(0)()

    rows = pl.ds(pl.multiple_of(me * out_rows, 8), out_rows)
    lanes = pl.ds(pl.multiple_of(core * width, BLK), width)
    r_ref[...] = full_ref[rows, lanes]
    z_ref[...] = z_all[:, lanes]


def per_device(
    whitening,
    sensor_states,
    sensor_coefficients,
    sensor_readings,
    conduit_endpoints,
    conductance,
    balance_right_side,
    prior_root_factor,
    prior_information,
    transition,
):
    n = prior_root_factor.shape[1]
    rows, cols = lax.axis_size("rows"), lax.axis_size("cols")
    plan = Plan(n, rows, cols)
    radix = plan.radix
    params = pltpu.CompilerParams(vmem_limit_bytes=VMEM_LIMIT)
    block_rows, bal_rows = whitening.shape[0], conductance.shape[0]
    depth = block_rows + bal_rows + BLK
    anywhere = pl.BlockSpec(memory_space=pl.ANY)
    hbm = pl.BlockSpec(memory_space=pltpu.HBM)
    vmem = pl.BlockSpec(memory_space=pltpu.VMEM)

    def typed(*shape):
        return jax.ShapeDtypeStruct(shape, F32)

    inputs = (
        whitening,
        sensor_states.T,
        sensor_coefficients.T,
        sensor_readings.reshape(-1, BLK),
        conduit_endpoints.T,
        conductance[None, :],
        balance_right_side[None, :],
        prior_root_factor,
        prior_information[None, :],
    )
    mine = pl.pallas_call(
        functools.partial(assemble_kernel, plan),
        out_shape=typed(rows * plan.piece, BLK),
        in_specs=[hbm] * len(inputs),
        out_specs=vmem,
        scratch_shapes=[pltpu.VMEM(x.shape, x.dtype) for x in inputs]
        + [
            pltpu.VMEM((n + 16, block_rows), BF16),
            pltpu.VMEM((n + 16, block_rows), BF16),
            pltpu.VMEM((n + 16, depth), BF16),
            pltpu.VMEM((n + 16, depth), BF16),
            pltpu.VMEM((BLK, n), F32),
            pltpu.VMEM((plan.total, BLK), F32),
            pltpu.SemaphoreType.DMA((len(inputs),)),
        ],
        compiler_params=pltpu.CompilerParams(vmem_limit_bytes=ASSEMBLE_VMEM),
        name="assemble",
    )(*inputs)

    spread = lax.all_to_all(
        mine.reshape(rows, plan.piece, BLK), "rows", split_axis=0, concat_axis=0
    )
    block = jnp.sum(spread, axis=0)

    def exchange(stage, rel, block):
        flip = rel * plan.stride[stage]
        return lax.ppermute(block, "rows", [(i, i ^ flip) for i in range(rows)])

    for stage in reversed(range(len(radix))):
        got = [block] + [exchange(stage, d, block) for d in range(1, radix[stage])]
        if stage:
            block = jnp.concatenate(got, axis=0)
    swap = [(i, i ^ 1) for i in range(cols)]
    both = got + [lax.ppermute(block, "cols", swap) for block in got]

    width = n // cols
    out_rows = n // rows
    wide = n + width + BLK
    r_post, z_post, x_next = pl.pallas_call(
        functools.partial(factor_kernel, plan, out_rows, width),
        out_shape=[typed(out_rows, width), typed(1, width), typed(1, width)],
        in_specs=[anywhere] * (len(both) + 1),
        out_specs=[vmem] * 3,
        scratch_shapes=[
            pltpu.VMEM((plan.total, BLK), F32),
            pltpu.VMEM((BLK, BLK), F32),
            pltpu.VMEM((BLK, BLK), F32),
            pltpu.VMEM((MIC * GRP, BLK), F32),
            pltpu.VMEM((MIC * MIC, BLK), F32),
            pltpu.VMEM((MIC, BLK), F32),
            pltpu.VMEM((MIC, BLK), F32),
            pltpu.VMEM((2, BLK, wide), F32),
            pltpu.VMEM((n, n), F32),
            pltpu.VMEM((n, width), F32),
            pltpu.VMEM((plan.blocks, BLK, BLK), F32),
            pltpu.VMEM((plan.blocks, BLK), F32),
            pltpu.VMEM((n, n), BF16),
            pltpu.VMEM((n, n), BF16),
            pltpu.VMEM((n, wide), BF16),
            pltpu.VMEM((n, wide), BF16),
            pltpu.VMEM((1, n), F32),
            pltpu.SemaphoreType.DMA((rows * cols,)),
            pltpu.SemaphoreType.DMA,
        ],
        compiler_params=params,
        name="factor",
    )(*both, transition.T)
    return (r_post, z_post[0], x_next[0])


def solution(mesh):
    in_specs = (
        P("rows", None),
        P("rows", None),
        P("rows", None),
        P("rows"),
        P("rows", None),
        P("rows"),
        P("rows"),
        P("rows", None),
        P("rows"),
        P("cols", None),
    )
    out_specs = (P("rows", "cols"), P("cols"), P("cols"))
    return jax.shard_map(
        per_device, mesh=mesh, in_specs=in_specs, out_specs=out_specs, check_vma=False
    )
```

time: 567 us -> 107 us (0.19); the launches traced: 557 us -> 107 us
  other arithmetic: 263 us -> 0.08 us
  waiting for transfers between devices: 129 us -> 15.6 us
  matrix products: 60.2 us -> 0 us
  local copies, waits for them, and re-layouts: 44.4 us -> 1.92 us
  Pallas kernels: 0 us -> 41.5 us
  between operations: 20 us -> 0.88 us
  starting transfers between devices: 0.08 us -> 8.51 us
    another operation x33 -> x0, other arithmetic: 257 us -> none  [the longest x30 172 us: per_device(): lower_factor = jnp.linalg.cholesky(gram)]
    psum x1 -> x0, waiting for transfers between devices: 129 us -> none  [per_device(): gram_sum, moment = lax.psum((gram_part, moment_part), 'rows')]
    another operation x44 -> x0, matrix products: 43.2 us -> none  [the longest x14 22.7 us: per_device(): lower_factor = jnp.linalg.cholesky(gram)]
    pallas_call x0 -> x2, Pallas kernels: none -> 41.5 us  [the longest x1 32.3 us: per_device(): pl.pallas_call(functools.partial(factor_kernel, plan, out_rows, width), o...]
    psum x1 -> x0, blocking collectives: 40.1 us -> none  [per_device(): gram_sum, moment = lax.psum((gram_part, moment_part), 'rows')]
    all_to_all x0 -> x1, blocking collectives: none -> 38.4 us  [per_device(): lax.all_to_all(mine.reshape(rows, plan.piece, BLK), 'rows', split_axis=0,...]
    another operation x39 -> x0, local copies, waits for them, and re-layouts: 31.4 us -> none
    dot_general x5 -> x0, matrix products: 17 us -> none  [the longest x1 6.57 us: per_device(): lax.dot_general(stacked_system, stacked_cols, (((0,), (0,)), ((), ())), p...]
  transfers between devices with their start and end apart: 2 -> 10, of which waited for: 1 -> 4; matrix products, arithmetic and copies ran while one was open for 1% -> 2% of each run, Pallas kernels for 0% -> 0%
where the time goes in v2:
time: 107 us
  Pallas kernels  41.5 us (39%)
  blocking collectives  38.4 us (36%)
  waiting for transfers between devices  15.6 us (15%)
  starting transfers between devices  8.51 us (8%)
  local copies, waits for them, and re-layouts  1.92 us (2%)
    all_to_all x1, blocking collectives, per_device(): lax.all_to_all(mine.reshape(rows, plan.piece, BLK), 'rows', split_axis=0,...  38.4 us
    pallas_call x1, Pallas kernels, per_device(): pl.pallas_call(functools.partial(factor_kernel, plan, out_rows, width), o...  32.3 us
    ppermute x6, waiting for transfers between devices, exchange(): return lax.ppermute(block, 'rows', [(i, i ^ flip) for i in range(rows)])  15.6 us
    pallas_call x1, Pallas kernels, per_device(): pl.pallas_call(functools.partial(assemble_kernel, plan), out_shape=typed(...  9.2 us
    ppermute x6, starting transfers between devices, exchange(): return lax.ppermute(block, 'rows', [(i, i ^ flip) for i in range(rows)])  8.01 us
  transfers between devices with their start and end apart: 10, of which 4 were waited for; matrix products, arithmetic and copies ran while one was open for 2% of the time, Pallas kernels for 0%

profile of v2, /device:TPU:0, one launch (start us, length us, event | category | flops | bytes accessed | tf_op | source)
XLA Modules:
  0.0 107.0 jit_solution(5647254879830691488)
XLA Ops:
  0.6 9.2 %assemble.1 = f32[2304,128]{1,0:T(8,128)} custom-call(f32[384,384]{1,0:T(8,128)} %refs_0_.1, s32[4,384]{1,0:T(4,128)} %bitcast.13, f32[4,384]{1,0:T(4,128)} %bitcast.14, f32[3,128]{1,0:T(4,128)} %bitcast.15, s32[2,128]{1,0:T(2,128)} %bitcast.16, f32[1,128]{1,0:T(1,128)} %bitcast.17, f32[1,128]{1,0:T(1,128)} %bitcast.18, f32[64,1024]{1,0:T(8,128)} %refs_7_.1, ...), custom_call_target="tpu_custom_call" | custom-call | tf_op jit(solution)/shard_map/assemble/pallas_call | solution.py:481
  9.8 38.4 %all_to_all.5 = f32[16,144,128]{2,1,0:T(8,128)S(1)} all-to-all(f32[16,144,128]{2,1,0:T(8,128)} %bitcast.12), channel_id=1, replica_groups=mesh['rows'=16,'cols'=2] {'rows'}, dimensions={0} | all-to-all | bytes 2359296 | tf_op jit(solution)/shard_map/all_to_all | solution.py:500
  48.3 0.1 reduce_sum.9
  48.4 1.6 %collective-permute-start.2 = (f32[144,128]{1,0:T(8,128)S(1)}, f32[144,128]{1,0:T(8,128)S(1)}, u32[]{:S(2)}, u32[]{:S(2)}) collective-permute-start(f32[144,128]{1,0:T(8,128)S(1)} %reduce_sum.9), channel_id=1, source_target_pairs={{0,24},{2,26},{4,28},{6,30},{8,16},{10,18},{12,20},{14,22},{16,8},... | collective-permute-start | bytes 221192 | tf_op jit(solution)/shard_map/ppermute | solution.py:507
  50.0 0.7 collective-permute-start.1
  50.6 2.2 %collective-permute-start = (f32[144,128]{1,0:T(8,128)S(1)}, f32[144,128]{1,0:T(8,128)S(1)}, u32[]{:S(2)}, u32[]{:S(2)}) collective-permute-start(f32[144,128]{1,0:T(8,128)S(1)} %reduce_sum.9), channel_id=1, source_target_pairs={{0,8},{2,10},{4,12},{6,14},{8,0},{10,2},{12,4},{14,6},{16,24},{18,... | collective-permute-start | bytes 221192 | tf_op jit(solution)/shard_map/ppermute | solution.py:507
  52.8 2.4 %collective-permute-done.2 = f32[144,128]{1,0:T(8,128)S(1)} collective-permute-done((f32[144,128]{1,0:T(8,128)S(1)}, f32[144,128]{1,0:T(8,128)S(1)}, u32[]{:S(2)}, u32[]{:S(2)}) %collective-permute-start.2) | collective-permute-done | bytes 73760 | tf_op jit(solution)/shard_map/ppermute | solution.py:507
  55.2 1.7 %collective-permute-done.1 = f32[144,128]{1,0:T(8,128)S(1)} collective-permute-done((f32[144,128]{1,0:T(8,128)S(1)}, f32[144,128]{1,0:T(8,128)S(1)}, u32[]{:S(2)}, u32[]{:S(2)}) %collective-permute-start.1) | collective-permute-done | bytes 73760 | tf_op jit(solution)/shard_map/ppermute | solution.py:507
  56.9 0.0 collective-permute-done
  56.9 0.8 collective-permute-start.5
  57.7 1.3 %collective-permute-start.4 = (f32[576,128]{1,0:T(8,128)S(1)}, f32[576,128]{1,0:T(8,128)S(1)}, u32[]{:S(2)}, u32[]{:S(2)}) collective-permute-start(f32[576,128]{1,0:T(8,128)S(1)} %pad_maximum_fusion.refs_0_), channel_id=1, source_target_pairs={{0,4},{2,6},{4,0},{6,2},{8,12},{10,14},{12,8},{14,10},{16,20},{18,... | collective-permute-start | bytes 884744 | tf_op jit(solution)/shard_map/ppermute | solution.py:507
  59.0 1.5 %collective-permute-start.3 = (f32[576,128]{1,0:T(8,128)S(1)}, f32[576,128]{1,0:T(8,128)S(1)}, u32[]{:S(2)}, u32[]{:S(2)}) collective-permute-start(f32[576,128]{1,0:T(8,128)S(1)} %pad_maximum_fusion.refs_0_), channel_id=1, source_target_pairs={{0,2},{2,0},{4,6},{6,4},{8,10},{10,8},{12,14},{14,12},{16,18},{18,... | collective-permute-start | bytes 884744 | tf_op jit(solution)/shard_map/ppermute | solution.py:507
  60.5 0.0 collective-permute-start.6
  60.5 7.4 %collective-permute-done.5.refs_3_ = f32[576,128]{1,0:T(8,128)S(1)} collective-permute-done((f32[576,128]{1,0:T(8,128)S(1)}, f32[576,128]{1,0:T(8,128)S(1)}, u32[]{:S(2)}, u32[]{:S(2)}) %collective-permute-start.5) | collective-permute-done | bytes 294944 | tf_op jit(solution)/shard_map/ppermute | solution.py:507
  67.8 0.0 collective-permute-start.9
  67.8 4.2 %collective-permute-done.4.refs_2_ = f32[576,128]{1,0:T(8,128)S(1)} collective-permute-done((f32[576,128]{1,0:T(8,128)S(1)}, f32[576,128]{1,0:T(8,128)S(1)}, u32[]{:S(2)}, u32[]{:S(2)}) %collective-permute-start.4) | collective-permute-done | bytes 294944 | tf_op jit(solution)/shard_map/ppermute | solution.py:507
  72.0 0.0 collective-permute-start.8
  72.0 0.0 collective-permute-done.3.refs_1_
  72.0 0.5 collective-permute-start.7
  72.5 1.9 %copy.13 = f32[512,1024]{0,1:T(8,128)S(1)} copy(f32[512,1024]{1,0:T(8,128)} %param.19) | data formatting | bytes 4194304 | tf_op args[9]
  74.5 0.0 collective-permute-done.6.refs_4_
  74.5 0.0 collective-permute-done.9.refs_7_
  74.5 0.0 collective-permute-done.8.refs_6_
  74.5 0.0 collective-permute-done.7.refs_5_
  74.5 32.3 %factor.1 = (f32[64,512]{1,0:T(8,128)}, f32[1,512]{1,0:T(1,128)}, f32[1,512]{1,0:T(1,128)}) custom-call(f32[576,128]{1,0:T(8,128)S(1)} %pad_maximum_fusion.refs_0_, f32[576,128]{1,0:T(8,128)S(1)} %collective-permute-done.3.refs_1_, f32[576,128]{1,0:T(8,128)S(1)} %collective-permute-done.4.refs_2_, f32[576,128]{1,0:T(8,128)S(1)} %collective-permute-done.5.refs_3_, ...), custom_call_target="tpu_custom_call" | custom-call | tf_op jit(solution)/shard_map/factor/pallas_call | solution.py:519
  (1 shorter events, 0.0 us)
Async XLA Ops:
  48.4 6.9 %collective-permute-start.2 = (f32[144,128]{1,0:T(8,128)S(1)}, f32[144,128]{1,0:T(8,128)S(1)}, u32[]{:S(2)}, u32[]{:S(2)}) collective-permute-start(f32[144,128]{1,0:T(8,128)S(1)} %reduce_sum.9), channel_id=1, source_target_pairs={{0,24},{2,26},{4,28},{6,30},{8,16},{10,18},{12,20},{14,22},{16,8},... | collective-permute-start | bytes 221192 | tf_op jit(solution)/shard_map/ppermute | solution.py:507
  50.0 6.9 %collective-permute-start.1 = (f32[144,128]{1,0:T(8,128)S(1)}, f32[144,128]{1,0:T(8,128)S(1)}, u32[]{:S(2)}, u32[]{:S(2)}) collective-permute-start(f32[144,128]{1,0:T(8,128)S(1)} %reduce_sum.9), channel_id=1, source_target_pairs={{0,16},{2,18},{4,20},{6,22},{8,24},{10,26},{12,28},{14,30},{16,0},... | collective-permute-start | bytes 221192 | tf_op jit(solution)/shard_map/ppermute | solution.py:507
  50.6 6.3 %collective-permute-start = (f32[144,128]{1,0:T(8,128)S(1)}, f32[144,128]{1,0:T(8,128)S(1)}, u32[]{:S(2)}, u32[]{:S(2)}) collective-permute-start(f32[144,128]{1,0:T(8,128)S(1)} %reduce_sum.9), channel_id=1, source_target_pairs={{0,8},{2,10},{4,12},{6,14},{8,0},{10,2},{12,4},{14,6},{16,24},{18,... | collective-permute-start | bytes 221192 | tf_op jit(solution)/shard_map/ppermute | solution.py:507
  56.9 10.9 %collective-permute-start.5 = (f32[576,128]{1,0:T(8,128)S(1)}, f32[576,128]{1,0:T(8,128)S(1)}, u32[]{:S(2)}, u32[]{:S(2)}) collective-permute-start(f32[576,128]{1,0:T(8,128)S(1)} %pad_maximum_fusion.refs_0_), channel_id=1, source_target_pairs={{0,6},{2,4},{4,2},{6,0},{8,14},{10,12},{12,10},{14,8},{16,22},{18,... | collective-permute-start | bytes 884744 | tf_op jit(solution)/shard_map/ppermute | solution.py:507
  57.7 14.3 %collective-permute-start.4 = (f32[576,128]{1,0:T(8,128)S(1)}, f32[576,128]{1,0:T(8,128)S(1)}, u32[]{:S(2)}, u32[]{:S(2)}) collective-permute-start(f32[576,128]{1,0:T(8,128)S(1)} %pad_maximum_fusion.refs_0_), channel_id=1, source_target_pairs={{0,4},{2,6},{4,0},{6,2},{8,12},{10,14},{12,8},{14,10},{16,20},{18,... | collective-permute-start | bytes 884744 | tf_op jit(solution)/shard_map/ppermute | solution.py:507
  59.0 13.1 %collective-permute-start.3 = (f32[576,128]{1,0:T(8,128)S(1)}, f32[576,128]{1,0:T(8,128)S(1)}, u32[]{:S(2)}, u32[]{:S(2)}) collective-permute-start(f32[576,128]{1,0:T(8,128)S(1)} %pad_maximum_fusion.refs_0_), channel_id=1, source_target_pairs={{0,2},{2,0},{4,6},{6,4},{8,10},{10,8},{12,14},{14,12},{16,18},{18,... | collective-permute-start | bytes 884744 | tf_op jit(solution)/shard_map/ppermute | solution.py:507
  60.5 14.0 %collective-permute-start.6 = (f32[576,128]{1,0:T(8,128)S(1)}, f32[576,128]{1,0:T(8,128)}, u32[]{:S(2)}, u32[]{:S(2)}) collective-permute-start(f32[576,128]{1,0:T(8,128)S(1)} %pad_maximum_fusion.refs_0_), channel_id=1, source_target_pairs={{0,1},{1,0},{2,3},{3,2},{4,5},{5,4},{6,7},{7,6},{8,9},{9,8},{10,11... | collective-permute-start | bytes 884744 | tf_op jit(solution)/shard_map/ppermute | solution.py:514
  67.8 6.7 %collective-permute-start.9 = (f32[576,128]{1,0:T(8,128)S(1)}, f32[576,128]{1,0:T(8,128)}, u32[]{:S(2)}, u32[]{:S(2)}) collective-permute-start(f32[576,128]{1,0:T(8,128)S(1)} %collective-permute-done.5.refs_3_), channel_id=1, source_target_pairs={{0,1},{1,0},{2,3},{3,2},{4,5},{5,4},{6,7},{7,6},{8,9},{9,8},{10,11... | collective-permute-start | bytes 884744 | tf_op jit(solution)/shard_map/ppermute | solution.py:514
  72.0 2.5 %collective-permute-start.8 = (f32[576,128]{1,0:T(8,128)S(1)}, f32[576,128]{1,0:T(8,128)}, u32[]{:S(2)}, u32[]{:S(2)}) collective-permute-start(f32[576,128]{1,0:T(8,128)S(1)} %collective-permute-done.4.refs_2_), channel_id=1, source_target_pairs={{0,1},{1,0},{2,3},{3,2},{4,5},{5,4},{6,7},{7,6},{8,9},{9,8},{10,11... | collective-permute-start | bytes 884744 | tf_op jit(solution)/shard_map/ppermute | solution.py:514
  72.0 2.5 %collective-permute-start.7 = (f32[576,128]{1,0:T(8,128)S(1)}, f32[576,128]{1,0:T(8,128)}, u32[]{:S(2)}, u32[]{:S(2)}) collective-permute-start(f32[576,128]{1,0:T(8,128)S(1)} %collective-permute-done.3.refs_1_), channel_id=1, source_target_pairs={{0,1},{1,0},{2,3},{3,2},{4,5},{5,4},{6,7},{7,6},{8,9},{9,8},{10,11... | collective-permute-start | bytes 884744 | tf_op jit(solution)/shard_map/ppermute | solution.py:514

commit v3 on v2

--- a/solution.py
+++ b/solution.py
@@ -13,7 +13,7 @@
 F32 = jnp.float32
 BF16 = jnp.bfloat16
 VMEM_LIMIT = 48 * 1024 * 1024
-ASSEMBLE_VMEM = 63 * 1024 * 1024
+WHOLE_VMEM = 63 * 1024 * 1024
 
 
 def split2(value):
@@ -58,12 +58,28 @@
         self.piece = self.total // (rows * cols)
         self.moment_rows = state_total // 64
 
+    def digit(self, index, stage):
+        return lax.rem(index // self.stride[stage], self.radix[stage])
+
+    def span(self, stage):
+        size = self.piece
+        for f in self.radix[stage + 1 :]:
+            size *= f
+        return size
+
+    def place(self, index, core):
+        found = core
+        for stride, f in zip(self.stride, self.radix):
+            found = found * f + index // stride % f
+        return found
+
     def tile(self, i, j):
         return (sum(self.blocks - k for k in range(i)) + j - i) * BLK
 
 
 def assemble_kernel(plan, *refs):
-    ins, (out_ref, *scratch) = refs[:9], refs[9:]
+    first = plan.radix[0]
+    ins, outs, scratch = refs[:9], refs[9 : 9 + first], refs[9 + first :]
     here, (sens_hi, sens_lo, at_hi, at_lo, prior_pad, packed, sems) = scratch[:9], scratch[9:]
     copies = [pltpu.make_async_copy(a, b, sems.at[i]) for i, (a, b) in enumerate(zip(ins, here))]
     for copy in copies:
@@ -155,9 +171,24 @@
         source = moments[k * 64 // wide][:, k * 64 % wide : k * 64 % wide + 64]
         packed[row : row + 1, 0:64] = source
 
-    size = plan.rows * plan.piece
-    at = lax.axis_index("cols") * size
-    out_ref[...] = packed[pl.ds(pl.multiple_of(at, 8), size), :]
+    me, core = lax.axis_index("rows"), lax.axis_index("cols")
+    span = plan.span(0)
+    for d in range(first):
+        at = (core * first + (plan.digit(me, 0) ^ d)) * span
+        outs[d][...] = packed[pl.ds(pl.multiple_of(at, 8), span), :]
+
+
+def sum_kernel(plan, stage, *refs):
+    before, after = plan.radix[stage - 1], plan.radix[stage]
+    ins, outs = refs[:before], refs[before:]
+    mine = plan.digit(lax.axis_index("rows"), stage)
+    span = plan.span(stage)
+    for d in range(after):
+        rows = pl.ds(pl.multiple_of((mine ^ d) * span, 8), span)
+        total = ins[0][rows, :]
+        for other in ins[1:]:
+            total = total + other[rows, :]
+        outs[d][...] = total
 
 
 def eliminate(s, rows):
@@ -277,8 +308,8 @@
 
 
 def factor_kernel(plan, out_rows, width, *refs):
-    radix0, cols, n, nb = plan.radix[0], plan.cols, plan.state_total, plan.blocks
-    ins, (trans_hbm, r_ref, z_ref, x_ref, *scratch) = refs[: radix0 * cols], refs[radix0 * cols :]
+    n, nb = plan.state_total, plan.blocks
+    gathered, trans_hbm, r_ref, z_ref, x_ref, *scratch = refs
     (
         packed,
         d_ref,
@@ -300,25 +331,17 @@
     me, core = lax.axis_index("rows"), lax.axis_index("cols")
 
     copies = []
-    inner = plan.rows // radix0
-    piece = plan.piece
-    for e in range(cols):
-        for d0 in range(radix0):
-            for f in range(inner):
-                flip = d0 * plan.stride[0]
-                rest, size = f, inner
-                for stage in range(1, len(plan.radix)):
-                    size //= plan.radix[stage]
-                    flip += rest // size * plan.stride[stage]
-                    rest %= size
-                place = (core ^ e) * plan.rows + (me ^ flip)
-                copies.append(
-                    pltpu.make_async_copy(
-                        ins[e * radix0 + d0].at[pl.ds(f * piece, piece), :],
-                        packed.at[pl.ds(pl.multiple_of(place * piece, 8), piece), :],
-                        sems.at[len(copies)],
-                    )
+    for index in range(plan.rows):
+        for e in range(plan.cols):
+            source = (index * plan.cols + e) * plan.piece
+            target = plan.place(index, e) * plan.piece
+            copies.append(
+                pltpu.make_async_copy(
+                    gathered.at[pl.ds(source, plan.piece), :],
+                    packed.at[pl.ds(target, plan.piece), :],
+                    sems.at[len(copies)],
                 )
+            )
     trans_copy = pltpu.make_async_copy(trans_hbm, trans_ref, trans_sem)
     for copy in copies:
         copy.start()
@@ -358,7 +381,7 @@
             return packed[row : row + BLK, :] * col_ref[k] * scales[j]
         if j < nb + width // BLK:
             at = (j - nb) * BLK
-            return trans_ref[k * BLK : (k + 1) * BLK, at : at + BLK] * col_ref[k]
+            return trans_ref[at : at + BLK, k * BLK : (k + 1) * BLK].T * col_ref[k]
         return turned(moments[k] * scales[k])
 
     last = nb + width // BLK
@@ -478,11 +501,11 @@
         prior_root_factor,
         prior_information[None, :],
     )
-    mine = pl.pallas_call(
+    parts = pl.pallas_call(
         functools.partial(assemble_kernel, plan),
-        out_shape=typed(rows * plan.piece, BLK),
+        out_shape=[typed(plan.span(0), BLK)] * radix[0],
         in_specs=[hbm] * len(inputs),
-        out_specs=vmem,
+        out_specs=[vmem] * radix[0],
         scratch_shapes=[pltpu.VMEM(x.shape, x.dtype) for x in inputs]
         + [
             pltpu.VMEM((n + 16, block_rows), BF16),
@@ -493,25 +516,25 @@
             pltpu.VMEM((plan.total, BLK), F32),
             pltpu.SemaphoreType.DMA((len(inputs),)),
         ],
-        compiler_params=pltpu.CompilerParams(vmem_limit_bytes=ASSEMBLE_VMEM),
+        compiler_params=pltpu.CompilerParams(vmem_limit_bytes=WHOLE_VMEM),
         name="assemble",
     )(*inputs)
-
-    spread = lax.all_to_all(
-        mine.reshape(rows, plan.piece, BLK), "rows", split_axis=0, concat_axis=0
-    )
-    block = jnp.sum(spread, axis=0)
 
     def exchange(stage, rel, block):
         flip = rel * plan.stride[stage]
         return lax.ppermute(block, "rows", [(i, i ^ flip) for i in range(rows)])
 
-    for stage in reversed(range(len(radix))):
-        got = [block] + [exchange(stage, d, block) for d in range(1, radix[stage])]
-        if stage:
-            block = jnp.concatenate(got, axis=0)
-    swap = [(i, i ^ 1) for i in range(cols)]
-    both = got + [lax.ppermute(block, "cols", swap) for block in got]
+    for stage in range(len(radix)):
+        got = [parts[0]] + [exchange(stage, d, parts[d]) for d in range(1, radix[stage])]
+        if stage + 1 < len(radix):
+            parts = pl.pallas_call(
+                functools.partial(sum_kernel, plan, stage + 1),
+                out_shape=[typed(plan.span(stage + 1), BLK)] * radix[stage + 1],
+                compiler_params=params,
+                name="partial_sums",
+            )(*got)
+    block = functools.reduce(jnp.add, got)
+    gathered = lax.all_gather(block, ("rows", "cols"), axis=0, tiled=True)
 
     width = n // cols
     out_rows = n // rows
@@ -519,7 +542,7 @@
     r_post, z_post, x_next = pl.pallas_call(
         functools.partial(factor_kernel, plan, out_rows, width),
         out_shape=[typed(out_rows, width), typed(1, width), typed(1, width)],
-        in_specs=[anywhere] * (len(both) + 1),
+        in_specs=[anywhere] * 2,
         out_specs=[vmem] * 3,
         scratch_shapes=[
             pltpu.VMEM((plan.total, BLK), F32),
@@ -531,7 +554,7 @@
             pltpu.VMEM((MIC, BLK), F32),
             pltpu.VMEM((2, BLK, wide), F32),
             pltpu.VMEM((n, n), F32),
-            pltpu.VMEM((n, width), F32),
+            pltpu.VMEM((width, n), F32),
             pltpu.VMEM((plan.blocks, BLK, BLK), F32),
             pltpu.VMEM((plan.blocks, BLK), F32),
             pltpu.VMEM((n, n), BF16),
@@ -542,9 +565,9 @@
             pltpu.SemaphoreType.DMA((rows * cols,)),
             pltpu.SemaphoreType.DMA,
         ],
-        compiler_params=params,
+        compiler_params=pltpu.CompilerParams(vmem_limit_bytes=WHOLE_VMEM),
         name="factor",
-    )(*both, transition.T)
+    )(gathered, transition)
     return (r_post, z_post[0], x_next[0])
 
 

time: 107 us -> 140 us (1.31)
  waiting for transfers between devices: 15.6 us -> 74.9 us
  blocking collectives: 38.4 us -> 0 us
  between operations: 0.88 us -> 14.1 us
    all_gather x0 -> x1, waiting for transfers between devices: none -> 55.5 us  [per_device(): gathered = lax.all_gather(block, ('rows', 'cols'), axis=0, tiled=True)]
    all_to_all x1 -> x0, blocking collectives: 38.4 us -> none  [per_device(): lax.all_to_all(mine.reshape(rows, plan.piece, BLK), 'rows', split_axis=0,...]
    ppermute x6, waiting for transfers between devices: 15.6 us -> 19.4 us  [exchange(): return lax.ppermute(block, 'rows', [(i, i ^ flip) for i in range(rows)])]
    pallas_call x1 -> x2, Pallas kernels: 9.2 us -> 9.19 us  [the longest x1 9.13 us: per_device(): pl.pallas_call(functools.partial(assemble_kernel, plan), out_shape=[typed...]
  transfers between devices with their start and end apart: 10 -> 7, of which waited for: 4 -> 6; matrix products, arithmetic and copies ran while one was open for 2% -> 0% of each run, Pallas kernels for 0% -> 0%
where the time goes in v3:
time: 140 us
  waiting for transfers between devices  74.9 us (54%)
  Pallas kernels  40.6 us (29%)
  between operations  14.1 us (10%)
  starting transfers between devices  9.03 us (6%)
    all_gather x1, waiting for transfers between devices, per_device(): gathered = lax.all_gather(block, ('rows', 'cols'), axis=0, tiled=True)  55.5 us
    pallas_call x1, Pallas kernels, per_device(): pl.pallas_call(functools.partial(factor_kernel, plan, out_rows, width), o...  31.5 us
    ppermute x6, waiting for transfers between devices, exchange(): return lax.ppermute(block, 'rows', [(i, i ^ flip) for i in range(rows)])  19.4 us
    pallas_call x1, Pallas kernels, per_device(): pl.pallas_call(functools.partial(assemble_kernel, plan), out_shape=[typed...  9.13 us
    ppermute x6, starting transfers between devices, exchange(): return lax.ppermute(block, 'rows', [(i, i ^ flip) for i in range(rows)])  8.99 us
  transfers between devices with their start and end apart: 7, of which 6 were waited for; matrix products, arithmetic and copies ran while one was open for 0% of the time, Pallas kernels for 0%

profile of v3, /device:TPU:0, one launch (start us, length us, event | category | flops | bytes accessed | tf_op | source)
XLA Modules:
  0.0 140.2 jit_solution(808483410801965350)
XLA Ops:
  7.2 0.0 all-gather.2.cloned.1.call-start
  7.2 9.1 %assemble.1 = (f32[576,128]{1,0:T(8,128)}, f32[576,128]{1,0:T(8,128)}, f32[576,128]{1,0:T(8,128)}, f32[576,128]{1,0:T(8,128)}) custom-call(f32[384,384]{1,0:T(8,128)} %refs_0_.1, s32[4,384]{1,0:T(4,128)} %bitcast.9, f32[4,384]{1,0:T(4,128)} %bitcast.10, f32[3,128]{1,0:T(4,128)} %bitcast.11, s32[2,128]{1,0:T(2,128)} %bitcast.12, f32[1,128]{1,0:T(1,128)} %bitcast.13, ...), custom_call_target="tpu_custom_call" | custom-call | tf_op jit(solution)/shard_map/assemble/pallas_call | solution.py:504
  16.4 3.0 %collective-permute-start = (f32[576,128]{1,0:T(8,128)}, f32[576,128]{1,0:T(8,128)S(1)}, u32[]{:S(2)}, u32[]{:S(2)}) collective-permute-start(f32[576,128]{1,0:T(8,128)} %get-tuple-element.15), channel_id=1, source_target_pairs={{0,2},{2,0},{4,6},{6,4},{8,10},{10,8},{12,14},{14,12},{16,18},{18,... | collective-permute-start | bytes 884744 | tf_op jit(solution)/shard_map/ppermute | solution.py:525
  19.4 1.5 %collective-permute-start.1 = (f32[576,128]{1,0:T(8,128)}, f32[576,128]{1,0:T(8,128)S(1)}, u32[]{:S(2)}, u32[]{:S(2)}) collective-permute-start(f32[576,128]{1,0:T(8,128)} %get-tuple-element.16), channel_id=1, source_target_pairs={{0,4},{2,6},{4,0},{6,2},{8,12},{10,14},{12,8},{14,10},{16,20},{18,... | collective-permute-start | bytes 884744 | tf_op jit(solution)/shard_map/ppermute | solution.py:525
  20.9 0.0 collective-permute-start.2
  20.9 6.5 %collective-permute-done.refs_1_ = f32[576,128]{1,0:T(8,128)S(1)} collective-permute-done((f32[576,128]{1,0:T(8,128)}, f32[576,128]{1,0:T(8,128)S(1)}, u32[]{:S(2)}, u32[]{:S(2)}) %collective-permute-start) | collective-permute-done | bytes 294944 | tf_op jit(solution)/shard_map/ppermute | solution.py:525
  27.4 7.0 %collective-permute-done.1.refs_2_ = f32[576,128]{1,0:T(8,128)S(1)} collective-permute-done((f32[576,128]{1,0:T(8,128)}, f32[576,128]{1,0:T(8,128)S(1)}, u32[]{:S(2)}, u32[]{:S(2)}) %collective-permute-start.1) | collective-permute-done | bytes 294944 | tf_op jit(solution)/shard_map/ppermute | solution.py:525
  34.4 0.0 collective-permute-done.2.refs_3_
  34.4 0.0 copy-start
  34.4 1.0 copy-done
  35.3 0.1 partial_sums.1
  35.4 1.6 %collective-permute-start.3 = (f32[144,128]{1,0:T(8,128)S(1)}, f32[144,128]{1,0:T(8,128)S(1)}, u32[]{:S(2)}, u32[]{:S(2)}) collective-permute-start(f32[144,128]{1,0:T(8,128)S(1)} %get-tuple-element.19), channel_id=1, source_target_pairs={{0,8},{2,10},{4,12},{6,14},{8,0},{10,2},{12,4},{14,6},{16,24},{18,... | collective-permute-start | bytes 221192 | tf_op jit(solution)/shard_map/ppermute | solution.py:525
  37.0 2.6 %collective-permute-start.4 = (f32[144,128]{1,0:T(8,128)S(1)}, f32[144,128]{1,0:T(8,128)S(1)}, u32[]{:S(2)}, u32[]{:S(2)}) collective-permute-start(f32[144,128]{1,0:T(8,128)S(1)} %get-tuple-element.20), channel_id=1, source_target_pairs={{0,16},{2,18},{4,20},{6,22},{8,24},{10,26},{12,28},{14,30},{16,0},... | collective-permute-start | bytes 221192 | tf_op jit(solution)/shard_map/ppermute | solution.py:525
  39.6 0.2 collective-permute-start.5
  39.8 0.7 collective-permute-done.3
  40.5 3.4 %collective-permute-done.4 = f32[144,128]{1,0:T(8,128)S(1)} collective-permute-done((f32[144,128]{1,0:T(8,128)S(1)}, f32[144,128]{1,0:T(8,128)S(1)}, u32[]{:S(2)}, u32[]{:S(2)}) %collective-permute-start.4) | collective-permute-done | bytes 73760 | tf_op jit(solution)/shard_map/ppermute | solution.py:525
  43.9 1.9 %collective-permute-done.5 = f32[144,128]{1,0:T(8,128)S(1)} collective-permute-done((f32[144,128]{1,0:T(8,128)S(1)}, f32[144,128]{1,0:T(8,128)S(1)}, u32[]{:S(2)}, u32[]{:S(2)}) %collective-permute-start.5) | collective-permute-done | bytes 73760 | tf_op jit(solution)/shard_map/ppermute | solution.py:525
  45.8 0.7 add_add_fusion
  46.4 0.0 all-gather.2.cloned.1.call-update
  46.4 55.5 %all-gather.2.cloned.1.call-done.refs_0_ = f32[4608,128]{1,0:T(8,128)} async-done(((f32[144,128]{1,0:T(8,128)}), f32[4608,128]{1,0:T(8,128)}) %all-gather.2.cloned.1.call-update) | async-done | bytes 2359312 | tf_op jit(solution)/shard_map/all_gather | solution.py:537
  101.9 31.5 %factor.1 = (f32[64,512]{1,0:T(8,128)}, f32[1,512]{1,0:T(1,128)}, f32[1,512]{1,0:T(1,128)}) custom-call(f32[4608,128]{1,0:T(8,128)} %all-gather.2.cloned.1.call-done.refs_0_, f32[512,1024]{1,0:T(8,128)} %refs_1_.1), custom_call_target="tpu_custom_call" | custom-call | tf_op jit(solution)/shard_map/factor/pallas_call | solution.py:542
Async XLA Ops:
  7.2 94.7 %all-gather.2.cloned.1.call-start = ((), (), s32[]{:S(2)}) async-start(), calls=%async_computation | async-start | bytes 2433024 | tf_op jit(solution)/shard_map/all_gather | solution.py:537
  16.4 11.1 %collective-permute-start = (f32[576,128]{1,0:T(8,128)}, f32[576,128]{1,0:T(8,128)S(1)}, u32[]{:S(2)}, u32[]{:S(2)}) collective-permute-start(f32[576,128]{1,0:T(8,128)} %get-tuple-element.15), channel_id=1, source_target_pairs={{0,2},{2,0},{4,6},{6,4},{8,10},{10,8},{12,14},{14,12},{16,18},{18,... | collective-permute-start | bytes 884744 | tf_op jit(solution)/shard_map/ppermute | solution.py:525
  19.4 15.0 %collective-permute-start.1 = (f32[576,128]{1,0:T(8,128)}, f32[576,128]{1,0:T(8,128)S(1)}, u32[]{:S(2)}, u32[]{:S(2)}) collective-permute-start(f32[576,128]{1,0:T(8,128)} %get-tuple-element.16), channel_id=1, source_target_pairs={{0,4},{2,6},{4,0},{6,2},{8,12},{10,14},{12,8},{14,10},{16,20},{18,... | collective-permute-start | bytes 884744 | tf_op jit(solution)/shard_map/ppermute | solution.py:525
  20.9 13.5 %collective-permute-start.2 = (f32[576,128]{1,0:T(8,128)}, f32[576,128]{1,0:T(8,128)S(1)}, u32[]{:S(2)}, u32[]{:S(2)}) collective-permute-start(f32[576,128]{1,0:T(8,128)} %get-tuple-element.17), channel_id=1, source_target_pairs={{0,6},{2,4},{4,2},{6,0},{8,14},{10,12},{12,10},{14,8},{16,22},{18,... | collective-permute-start | bytes 884744 | tf_op jit(solution)/shard_map/ppermute | solution.py:525
  34.4 1.0 copy-start
  35.4 5.1 %collective-permute-start.3 = (f32[144,128]{1,0:T(8,128)S(1)}, f32[144,128]{1,0:T(8,128)S(1)}, u32[]{:S(2)}, u32[]{:S(2)}) collective-permute-start(f32[144,128]{1,0:T(8,128)S(1)} %get-tuple-element.19), channel_id=1, source_target_pairs={{0,8},{2,10},{4,12},{6,14},{8,0},{10,2},{12,4},{14,6},{16,24},{18,... | collective-permute-start | bytes 221192 | tf_op jit(solution)/shard_map/ppermute | solution.py:525
  37.0 6.8 %collective-permute-start.4 = (f32[144,128]{1,0:T(8,128)S(1)}, f32[144,128]{1,0:T(8,128)S(1)}, u32[]{:S(2)}, u32[]{:S(2)}) collective-permute-start(f32[144,128]{1,0:T(8,128)S(1)} %get-tuple-element.20), channel_id=1, source_target_pairs={{0,16},{2,18},{4,20},{6,22},{8,24},{10,26},{12,28},{14,30},{16,0},... | collective-permute-start | bytes 221192 | tf_op jit(solution)/shard_map/ppermute | solution.py:525
  39.6 6.2 %collective-permute-start.5 = (f32[144,128]{1,0:T(8,128)S(1)}, f32[144,128]{1,0:T(8,128)S(1)}, u32[]{:S(2)}, u32[]{:S(2)}) collective-permute-start(f32[144,128]{1,0:T(8,128)S(1)} %get-tuple-element.21), channel_id=1, source_target_pairs={{0,24},{2,26},{4,28},{6,30},{8,16},{10,18},{12,20},{14,22},{16,8},... | collective-permute-start | bytes 221192 | tf_op jit(solution)/shard_map/ppermute | solution.py:525
Sparse Core Ops, SparseCore 0:
  46.6 55.2 all-gather.1

commit v4 on v2

--- a/solution.py
+++ b/solution.py
@@ -13,7 +13,7 @@
 F32 = jnp.float32
 BF16 = jnp.bfloat16
 VMEM_LIMIT = 48 * 1024 * 1024
-ASSEMBLE_VMEM = 63 * 1024 * 1024
+WHOLE_VMEM = 63 * 1024 * 1024
 
 
 def split2(value):
@@ -52,18 +52,42 @@
         for f in self.radix:
             self.stride.append(step)
             step *= f
-        self.tiles = nb * (nb + 1) // 2
-        unit = 8 * rows * cols
-        self.total = -(-self.tiles * BLK // unit) * unit
-        self.piece = self.total // (rows * cols)
+        stages = list(range(len(self.radix)))
+        self.orders = (stages, stages[::-1])
+        tiles = [(i, j) for i in range(nb) for j in range(i, nb)]
+        share = -(-len(tiles) // cols)
+        piece = -(-share * BLK // (8 * rows)) * 8
+        small = max(8, piece // 24 * 8)
+        self.pieces = (piece - small, small)
+        self.half = rows * piece
+        self.local = {}
+        for index, tile in enumerate(tiles):
+            self.local[tile] = (index // share, index % share * BLK)
         self.moment_rows = state_total // 64
 
     def tile(self, i, j):
-        return (sum(self.blocks - k for k in range(i)) + j - i) * BLK
+        core, row = self.local[i, j]
+        return core * self.half + row
+
+    def digit(self, index, stage):
+        return lax.rem(index // self.stride[stage], self.radix[stage])
+
+    def base(self, flow):
+        return self.rows * self.pieces[0] * flow
+
+    def span(self, flow, step):
+        size = self.pieces[flow]
+        for stage in self.orders[flow][step + 1 :]:
+            size *= self.radix[stage]
+        return size
+
+    def fan(self, flow, step):
+        return self.radix[self.orders[flow][step]]
 
 
 def assemble_kernel(plan, *refs):
-    ins, (out_ref, *scratch) = refs[:9], refs[9:]
+    fans = [plan.fan(flow, 0) for flow in range(2)]
+    ins, outs, scratch = refs[:9], refs[9 : 9 + sum(fans)], refs[9 + sum(fans) :]
     here, (sens_hi, sens_lo, at_hi, at_lo, prior_pad, packed, sems) = scratch[:9], scratch[9:]
     copies = [pltpu.make_async_copy(a, b, sems.at[i]) for i, (a, b) in enumerate(zip(ins, here))]
     for copy in copies:
@@ -96,8 +120,9 @@
         return jnp.where(top, jnp.broadcast_to(row, (head, row.shape[1])), 0.0)
 
     prior_pad[...] = jnp.zeros_like(prior_pad)
-    if plan.tiles * BLK < plan.total:
-        packed[plan.tiles * BLK :, :] = jnp.zeros((plan.total - plan.tiles * BLK, BLK), F32)
+    used = max(row for _, row in plan.local.values()) + BLK
+    if used < plan.half:
+        packed[used:, :] = jnp.zeros((plan.half - used, BLK), F32)
     for copy in copies:
         copy.wait()
 
@@ -132,32 +157,55 @@
     for at in range(0, n, BLK):
         put(at_hi, at_lo, head + at, prior_col, prior_pad[:, at : at + BLK].T)
 
-    wide = 2 * BLK
-    moments = []
-    for at in range(0, n, wide):
-        stop = head + at + wide
-        out = dot3(
-            (at_hi[0:stop, :], at_lo[0:stop, :]),
-            (at_hi[head + at : stop, :], at_lo[head + at : stop, :]),
-            1,
-            1,
-        )
-        moments.append(out[0:1, :])
-        for part in range(2):
-            j = at // BLK + part
-            for i in range(j + 1):
-                row = plan.tile(i, j)
-                packed[row : row + BLK, :] = out[
-                    head + i * BLK : head + (i + 1) * BLK, part * BLK : (part + 1) * BLK
-                ]
-    for k in range(plan.moment_rows):
-        row = BLK - plan.moment_rows + k
-        source = moments[k * 64 // wide][:, k * 64 % wide : k * 64 % wide + 64]
-        packed[row : row + 1, 0:64] = source
-
-    size = plan.rows * plan.piece
-    at = lax.axis_index("cols") * size
-    out_ref[...] = packed[pl.ds(pl.multiple_of(at, 8), size), :]
+    me, core = lax.axis_index("rows"), lax.axis_index("cols")
+
+    def tiles_of(part):
+        moments = []
+        for at in range(0, plan.blocks, 2):
+            wanted = [(i, j) for (i, j), (c, _) in plan.local.items() if c == part and j // 2 == at // 2]
+            if not wanted:
+                continue
+            low, high = min(i for i, _ in wanted), max(i for i, _ in wanted) + 1
+            top = head + low * BLK if low else 0
+            rows = slice(top, head + high * BLK)
+            cols = slice(head + at * BLK, head + (at + 2) * BLK)
+            out = dot3((at_hi[rows, :], at_lo[rows, :]), (at_hi[cols, :], at_lo[cols, :]), 1, 1)
+            if not low:
+                moments += [out[0:1, k * 64 : k * 64 + 64] for k in range(2 * BLK // 64)]
+            for i, j in wanted:
+                row, col = plan.local[i, j][1], (j - at) * BLK
+                where = head + i * BLK - top
+                packed[row : row + BLK, :] = out[where : where + BLK, col : col + BLK]
+        for k, value in enumerate(moments):
+            row = plan.local[0, 0][1] + BLK - plan.moment_rows + k
+            packed[row : row + 1, 0:64] = value
+
+    for part in range(plan.cols):
+        pl.when(core == part)(functools.partial(tiles_of, part))
+
+    outs = list(outs)
+    for flow in range(2):
+        span, stage = plan.span(flow, 0), plan.orders[flow][0]
+        for d in range(fans[flow]):
+            at = plan.base(flow) + (plan.digit(me, stage) ^ d) * span
+            outs.pop(0)[...] = packed[pl.ds(pl.multiple_of(at, 8), span), :]
+
+
+def sum_kernel(plan, step, *refs):
+    me = lax.axis_index("rows")
+    refs = list(refs)
+    ins = [[refs.pop(0) for _ in range(plan.fan(flow, step))] for flow in range(2)]
+    last = step + 1 == len(plan.radix)
+    for flow in range(2):
+        count = 1 if last else plan.fan(flow, step + 1)
+        span = plan.span(flow, step + 1)
+        for d in range(count):
+            at = 0 if last else (plan.digit(me, plan.orders[flow][step + 1]) ^ d) * span
+            rows = pl.ds(pl.multiple_of(at, 8), span)
+            total = ins[flow][0][rows, :]
+            for other in ins[flow][1:]:
+                total = total + other[rows, :]
+            refs.pop(0)[...] = total
 
 
 def eliminate(s, rows):
@@ -277,8 +325,9 @@
 
 
 def factor_kernel(plan, out_rows, width, *refs):
-    radix0, cols, n, nb = plan.radix[0], plan.cols, plan.state_total, plan.blocks
-    ins, (trans_hbm, r_ref, z_ref, x_ref, *scratch) = refs[: radix0 * cols], refs[radix0 * cols :]
+    n, nb = plan.state_total, plan.blocks
+    slots = max(plan.fan(flow, 0) for flow in range(2))
+    ins, (trans_hbm, r_ref, z_ref, x_ref, *scratch) = refs[: slots * plan.cols], refs[slots * plan.cols :]
     (
         packed,
         d_ref,
@@ -300,25 +349,28 @@
     me, core = lax.axis_index("rows"), lax.axis_index("cols")
 
     copies = []
-    inner = plan.rows // radix0
-    piece = plan.piece
-    for e in range(cols):
-        for d0 in range(radix0):
-            for f in range(inner):
-                flip = d0 * plan.stride[0]
-                rest, size = f, inner
-                for stage in range(1, len(plan.radix)):
-                    size //= plan.radix[stage]
-                    flip += rest // size * plan.stride[stage]
-                    rest %= size
-                place = (core ^ e) * plan.rows + (me ^ flip)
-                copies.append(
-                    pltpu.make_async_copy(
-                        ins[e * radix0 + d0].at[pl.ds(f * piece, piece), :],
-                        packed.at[pl.ds(pl.multiple_of(place * piece, 8), piece), :],
-                        sems.at[len(copies)],
+    for e in range(plan.cols):
+        offsets = [0] * slots
+        for flow in range(2):
+            piece, order = plan.pieces[flow], plan.orders[flow]
+            inner = plan.span(flow, 0) // piece
+            for d in range(plan.fan(flow, 0)):
+                for f in range(inner):
+                    place = plan.digit(me, order[0]) ^ d
+                    rest, size = f, inner
+                    for stage in order[1:]:
+                        size //= plan.radix[stage]
+                        place = place * plan.radix[stage] + (plan.digit(me, stage) ^ (rest // size))
+                        rest %= size
+                    target = (core ^ e) * plan.half + plan.base(flow) + place * piece
+                    copies.append(
+                        pltpu.make_async_copy(
+                            ins[e * slots + d].at[pl.ds(offsets[d] + f * piece, piece), :],
+                            packed.at[pl.ds(pl.multiple_of(target, 8), piece), :],
+                            sems.at[len(copies)],
+                        )
                     )
-                )
+                offsets[d] += inner * piece
     trans_copy = pltpu.make_async_copy(trans_hbm, trans_ref, trans_sem)
     for copy in copies:
         copy.start()
@@ -333,13 +385,14 @@
     def turned(row):
         return jnp.broadcast_to(row, (BLK, BLK)).T
 
-    tile = packed[0:BLK, :]
+    corner = plan.tile(0, 0)
+    tile = packed[corner : corner + BLK, :]
     hidden = (row_id >= BLK - plan.moment_rows) & (col_id < 64)
     moments = []
     for k in range(nb):
         at = BLK - plan.moment_rows + 2 * k
         moments.append(jnp.concatenate([tile[at : at + 1, 0:64], tile[at + 1 : at + 2, 0:64]], axis=1))
-    packed[0:BLK, :] = jnp.where(hidden, tile.T, tile)
+    packed[corner : corner + BLK, :] = jnp.where(hidden, tile.T, tile)
 
     scales = []
     for k in range(nb):
@@ -358,7 +411,7 @@
             return packed[row : row + BLK, :] * col_ref[k] * scales[j]
         if j < nb + width // BLK:
             at = (j - nb) * BLK
-            return trans_ref[k * BLK : (k + 1) * BLK, at : at + BLK] * col_ref[k]
+            return trans_ref[at : at + BLK, k * BLK : (k + 1) * BLK].T * col_ref[k]
         return turned(moments[k] * scales[k])
 
     last = nb + width // BLK
@@ -478,11 +531,11 @@
         prior_root_factor,
         prior_information[None, :],
     )
-    mine = pl.pallas_call(
+    parts = pl.pallas_call(
         functools.partial(assemble_kernel, plan),
-        out_shape=typed(rows * plan.piece, BLK),
+        out_shape=[typed(plan.span(f, 0), BLK) for f in range(2) for _ in range(plan.fan(f, 0))],
         in_specs=[hbm] * len(inputs),
-        out_specs=vmem,
+        out_specs=[vmem] * sum(plan.fan(f, 0) for f in range(2)),
         scratch_shapes=[pltpu.VMEM(x.shape, x.dtype) for x in inputs]
         + [
             pltpu.VMEM((n + 16, block_rows), BF16),
@@ -490,28 +543,51 @@
             pltpu.VMEM((n + 16, depth), BF16),
             pltpu.VMEM((n + 16, depth), BF16),
             pltpu.VMEM((BLK, n), F32),
-            pltpu.VMEM((plan.total, BLK), F32),
+            pltpu.VMEM((plan.half, BLK), F32),
             pltpu.SemaphoreType.DMA((len(inputs),)),
         ],
-        compiler_params=pltpu.CompilerParams(vmem_limit_bytes=ASSEMBLE_VMEM),
+        compiler_params=pltpu.CompilerParams(vmem_limit_bytes=WHOLE_VMEM),
         name="assemble",
     )(*inputs)
-
-    spread = lax.all_to_all(
-        mine.reshape(rows, plan.piece, BLK), "rows", split_axis=0, concat_axis=0
-    )
-    block = jnp.sum(spread, axis=0)
 
     def exchange(stage, rel, block):
         flip = rel * plan.stride[stage]
         return lax.ppermute(block, "rows", [(i, i ^ flip) for i in range(rows)])
 
-    for stage in reversed(range(len(radix))):
-        got = [block] + [exchange(stage, d, block) for d in range(1, radix[stage])]
-        if stage:
-            block = jnp.concatenate(got, axis=0)
+    steps = len(radix)
+    for step in range(steps):
+        parts = list(parts)
+        got = []
+        for flow in range(2):
+            fan, stage = plan.fan(flow, step), plan.orders[flow][step]
+            mine = [parts.pop(0) for _ in range(fan)]
+            got += mine[:1] + [exchange(stage, d, mine[d]) for d in range(1, fan)]
+        last = step + 1 == steps
+        shapes = [
+            typed(plan.span(flow, step + 1), BLK)
+            for flow in range(2)
+            for _ in range(1 if last else plan.fan(flow, step + 1))
+        ]
+        parts = pl.pallas_call(
+            functools.partial(sum_kernel, plan, step),
+            out_shape=shapes,
+            compiler_params=params,
+            name="partial_sums",
+        )(*got)
+    blocks = list(parts)
+    for step in reversed(range(steps)):
+        got = []
+        for flow in range(2):
+            fan, stage = plan.fan(flow, step), plan.orders[flow][step]
+            got.append([blocks[flow]] + [exchange(stage, d, blocks[flow]) for d in range(1, fan)])
+        if step:
+            blocks = [jnp.concatenate(found, axis=0) for found in got]
     swap = [(i, i ^ 1) for i in range(cols)]
-    both = got + [lax.ppermute(block, "cols", swap) for block in got]
+    joined = [
+        jnp.concatenate([found[d] for found in got if d < len(found)], axis=0)
+        for d in range(max(len(found) for found in got))
+    ]
+    both = joined + [lax.ppermute(block, "cols", swap) for block in joined]
 
     width = n // cols
     out_rows = n // rows
@@ -522,7 +598,7 @@
         in_specs=[anywhere] * (len(both) + 1),
         out_specs=[vmem] * 3,
         scratch_shapes=[
-            pltpu.VMEM((plan.total, BLK), F32),
+            pltpu.VMEM((cols * plan.half, BLK), F32),
             pltpu.VMEM((BLK, BLK), F32),
             pltpu.VMEM((BLK, BLK), F32),
             pltpu.VMEM((MIC * GRP, BLK), F32),
@@ -531,7 +607,7 @@
             pltpu.VMEM((MIC, BLK), F32),
             pltpu.VMEM((2, BLK, wide), F32),
             pltpu.VMEM((n, n), F32),
-            pltpu.VMEM((n, width), F32),
+            pltpu.VMEM((width, n), F32),
             pltpu.VMEM((plan.blocks, BLK, BLK), F32),
             pltpu.VMEM((plan.blocks, BLK), F32),
             pltpu.VMEM((n, n), BF16),
@@ -539,12 +615,12 @@
             pltpu.VMEM((n, wide), BF16),
             pltpu.VMEM((n, wide), BF16),
             pltpu.VMEM((1, n), F32),
-            pltpu.SemaphoreType.DMA((rows * cols,)),
+            pltpu.SemaphoreType.DMA((2 * rows * cols,)),
             pltpu.SemaphoreType.DMA,
         ],
         compiler_params=params,
         name="factor",
-    )(*both, transition.T)
+    )(*both, transition)
     return (r_post, z_post[0], x_next[0])
 
 

time: 107 us -> 107 us (level)
  blocking collectives: 38.4 us -> 0 us
  starting transfers between devices: 8.51 us -> 33.1 us
  waiting for transfers between devices: 15.6 us -> 29.9 us
    all_to_all x1 -> x0, blocking collectives: 38.4 us -> none  [per_device(): lax.all_to_all(mine.reshape(rows, plan.piece, BLK), 'rows', split_axis=0,...]
    ppermute x6 -> x24, starting transfers between devices: 8.01 us -> 32.4 us  [exchange(): return lax.ppermute(block, 'rows', [(i, i ^ flip) for i in range(rows)])]
    ppermute x6 -> x24, waiting for transfers between devices: 15.6 us -> 28.2 us  [exchange(): return lax.ppermute(block, 'rows', [(i, i ^ flip) for i in range(rows)])]
    pallas_call x1 -> x3, Pallas kernels: 9.2 us -> 6.79 us  [the longest x1 6.7 us: per_device(): pl.pallas_call(functools.partial(assemble_kernel, plan), out_shape=[typed...]
    pallas_call x1, Pallas kernels: 32.3 us -> 34 us  [per_device(): pl.pallas_call(functools.partial(factor_kernel, plan, out_rows, width), o...]
    ppermute x4, waiting for transfers between devices: 0.01 us -> 1.66 us  [per_device(): both = joined + [lax.ppermute(block, 'cols', swap) for block in joined]]
  transfers between devices with their start and end apart: 10 -> 28, of which waited for: 4 -> 10; matrix products, arithmetic and copies ran while one was open for 2% -> 0% of each run, Pallas kernels for 0% -> 0%
where the time goes in v4:
time: 107 us
  Pallas kernels  40.8 us (38%)
  starting transfers between devices  33.1 us (31%)
  waiting for transfers between devices  29.9 us (28%)
  local copies, waits for them, and re-layouts  1.94 us (2%)
    pallas_call x1, Pallas kernels, per_device(): pl.pallas_call(functools.partial(factor_kernel, plan, out_rows, width), o...  34 us
    ppermute x24, starting transfers between devices, exchange(): return lax.ppermute(block, 'rows', [(i, i ^ flip) for i in range(rows)])  32.4 us
    ppermute x24, waiting for transfers between devices, exchange(): return lax.ppermute(block, 'rows', [(i, i ^ flip) for i in range(rows)])  28.2 us
    pallas_call x1, Pallas kernels, per_device(): pl.pallas_call(functools.partial(assemble_kernel, plan), out_shape=[typed...  6.7 us
  transfers between devices with their start and end apart: 28, of which 10 were waited for; matrix products, arithmetic and copies ran while one was open for 0% of the time, Pallas kernels for 0%

profile of v4, /device:TPU:0, one launch (start us, length us, event | category | flops | bytes accessed | tf_op | source)
XLA Modules:
  0.0 106.7 jit_solution(7138642160058281473)
XLA Ops:
  0.6 6.7 %assemble.1 = (f32[384,128]{1,0:T(8,128)}, f32[384,128]{1,0:T(8,128)}, f32[384,128]{1,0:T(8,128)}, f32[384,128]{1,0:T(8,128)}, f32[192,128]{1,0:T(8,128)}, /*ind...) custom-call(f32[384,384]{1,0:T(8,128)} %refs_0_.1, s32[4,384]{1,0:T(4,128)} %bitcast.9, f32[4,384]{1,0:T(4,128)} %bitcast.10, ...), custom_call_target="tpu_custom_call" | custom-call | tf_op jit(solution)/shard_map/assemble/pallas_call | solution.py:534
  7.3 0.0 copy-start
  7.4 3.1 %collective-permute-start.3 = (f32[192,128]{1,0:T(8,128)}, f32[192,128]{1,0:T(8,128)S(1)}, u32[]{:S(2)}, u32[]{:S(2)}) collective-permute-start(f32[192,128]{1,0:T(8,128)} %get-tuple-element.29), channel_id=1, source_target_pairs={{0,8},{2,10},{4,12},{6,14},{8,0},{10,2},{12,4},{14,6},{16,24},{18,... | collective-permute-start | bytes 294920 | tf_op jit(solution)/shard_map/ppermute | solution.py:555
  10.4 1.5 %collective-permute-start = (f32[384,128]{1,0:T(8,128)}, f32[384,128]{1,0:T(8,128)S(1)}, u32[]{:S(2)}, u32[]{:S(2)}) collective-permute-start(f32[384,128]{1,0:T(8,128)} %get-tuple-element.25), channel_id=1, source_target_pairs={{0,2},{2,0},{4,6},{6,4},{8,10},{10,8},{12,14},{14,12},{16,18},{18,... | collective-permute-start | bytes 589832 | tf_op jit(solution)/shard_map/ppermute | solution.py:555
  11.9 1.5 %collective-permute-start.1 = (f32[384,128]{1,0:T(8,128)}, f32[384,128]{1,0:T(8,128)S(1)}, u32[]{:S(2)}, u32[]{:S(2)}) collective-permute-start(f32[384,128]{1,0:T(8,128)} %get-tuple-element.26), channel_id=1, source_target_pairs={{0,4},{2,6},{4,0},{6,2},{8,12},{10,14},{12,8},{14,10},{16,20},{18,... | collective-permute-start | bytes 589832 | tf_op jit(solution)/shard_map/ppermute | solution.py:555
  13.5 0.5 collective-permute-start.2
  13.9 2.6 %collective-permute-start.4 = (f32[192,128]{1,0:T(8,128)}, f32[192,128]{1,0:T(8,128)S(1)}, u32[]{:S(2)}, u32[]{:S(2)}) collective-permute-start(f32[192,128]{1,0:T(8,128)} %get-tuple-element.30), channel_id=1, source_target_pairs={{0,16},{2,18},{4,20},{6,22},{8,24},{10,26},{12,28},{14,30},{16,0},... | collective-permute-start | bytes 294920 | tf_op jit(solution)/shard_map/ppermute | solution.py:555
  16.5 0.0 collective-permute-done.3.refs_5_
  16.5 0.9 collective-permute-start.5
  17.4 6.2 %collective-permute-done.4.refs_6_ = f32[192,128]{1,0:T(8,128)S(1)} collective-permute-done((f32[192,128]{1,0:T(8,128)}, f32[192,128]{1,0:T(8,128)S(1)}, u32[]{:S(2)}, u32[]{:S(2)}) %collective-permute-start.4) | collective-permute-done | bytes 98336 | tf_op jit(solution)/shard_map/ppermute | solution.py:555
  23.6 0.0 collective-permute-done.5.refs_7_
  23.6 0.0 collective-permute-done.refs_1_
  23.6 0.0 collective-permute-done.1.refs_2_
  23.6 0.0 collective-permute-done.2.refs_3_
  23.6 0.0 copy-start.1
  23.6 0.9 copy-done.1
  24.6 0.9 copy-done.2
  25.4 0.1 partial_sums.2
  25.5 1.8 %collective-permute-start.9 = (f32[48,128]{1,0:T(8,128)S(1)}, f32[48,128]{1,0:T(8,128)S(1)}, u32[]{:S(2)}, u32[]{:S(2)}) collective-permute-start(f32[48,128]{1,0:T(8,128)S(1)} %get-tuple-element.37), channel_id=1, source_target_pairs={{0,2},{2,0},{4,6},{6,4},{8,10},{10,8},{12,14},{14,12},{16,18},{18,... | collective-permute-start | bytes 73736 | tf_op jit(solution)/shard_map/ppermute | solution.py:555
  27.3 1.6 %collective-permute-start.6 = (f32[96,128]{1,0:T(8,128)S(1)}, f32[96,128]{1,0:T(8,128)S(1)}, u32[]{:S(2)}, u32[]{:S(2)}) collective-permute-start(f32[96,128]{1,0:T(8,128)S(1)} %get-tuple-element.33), channel_id=1, source_target_pairs={{0,8},{2,10},{4,12},{6,14},{8,0},{10,2},{12,4},{14,6},{16,24},{18,... | collective-permute-start | bytes 147464 | tf_op jit(solution)/shard_map/ppermute | solution.py:555
  28.9 1.5 %collective-permute-start.7 = (f32[96,128]{1,0:T(8,128)S(1)}, f32[96,128]{1,0:T(8,128)S(1)}, u32[]{:S(2)}, u32[]{:S(2)}) collective-permute-start(f32[96,128]{1,0:T(8,128)S(1)} %get-tuple-element.34), channel_id=1, source_target_pairs={{0,16},{2,18},{4,20},{6,22},{8,24},{10,26},{12,28},{14,30},{16,0},... | collective-permute-start | bytes 147464 | tf_op jit(solution)/shard_map/ppermute | solution.py:555
  30.4 1.2 %collective-permute-start.8 = (f32[96,128]{1,0:T(8,128)S(1)}, f32[96,128]{1,0:T(8,128)S(1)}, u32[]{:S(2)}, u32[]{:S(2)}) collective-permute-start(f32[96,128]{1,0:T(8,128)S(1)} %get-tuple-element.35), channel_id=1, source_target_pairs={{0,24},{2,26},{4,28},{6,30},{8,16},{10,18},{12,20},{14,22},{16,8},... | collective-permute-start | bytes 147464 | tf_op jit(solution)/shard_map/ppermute | solution.py:555
  31.6 1.5 %collective-permute-start.10 = (f32[48,128]{1,0:T(8,128)S(1)}, f32[48,128]{1,0:T(8,128)S(1)}, u32[]{:S(2)}, u32[]{:S(2)}) collective-permute-start(f32[48,128]{1,0:T(8,128)S(1)} %get-tuple-element.38), channel_id=1, source_target_pairs={{0,4},{2,6},{4,0},{6,2},{8,12},{10,14},{12,8},{14,10},{16,20},{18,... | collective-permute-start | bytes 73736 | tf_op jit(solution)/shard_map/ppermute | solution.py:555
  33.2 0.0 collective-permute-done.9.refs_5_
  33.2 0.3 collective-permute-start.11
  33.5 2.0 %collective-permute-done.10.refs_6_ = f32[48,128]{1,0:T(8,128)S(1)} collective-permute-done((f32[48,128]{1,0:T(8,128)S(1)}, f32[48,128]{1,0:T(8,128)S(1)}, u32[]{:S(2)}, u32[]{:S(2)}) %collective-permute-start.10) | collective-permute-done | bytes 24608 | tf_op jit(solution)/shard_map/ppermute | solution.py:555
  35.5 2.5 %collective-permute-done.11.refs_7_ = f32[48,128]{1,0:T(8,128)S(1)} collective-permute-done((f32[48,128]{1,0:T(8,128)S(1)}, f32[48,128]{1,0:T(8,128)S(1)}, u32[]{:S(2)}, u32[]{:S(2)}) %collective-permute-start.11) | collective-permute-done | bytes 24608 | tf_op jit(solution)/shard_map/ppermute | solution.py:555
  38.0 0.0 collective-permute-done.6.refs_1_
  38.0 0.0 collective-permute-done.7.refs_2_
  38.0 0.0 collective-permute-done.8.refs_3_
  38.0 0.2 collective-permute-start.17
  38.3 1.7 %collective-permute-start.16 = (f32[48,128]{1,0:T(8,128)S(1)}, f32[48,128]{1,0:T(8,128)S(1)}, u32[]{:S(2)}, u32[]{:S(2)}) collective-permute-start(f32[48,128]{1,0:T(8,128)S(1)} %get-tuple-element.41), channel_id=1, source_target_pairs={{0,4},{2,6},{4,0},{6,2},{8,12},{10,14},{12,8},{14,10},{16,20},{18,... | collective-permute-start | bytes 73736 | tf_op jit(solution)/shard_map/ppermute | solution.py:555
  40.0 1.6 %collective-permute-start.15 = (f32[48,128]{1,0:T(8,128)S(1)}, f32[48,128]{1,0:T(8,128)S(1)}, u32[]{:S(2)}, u32[]{:S(2)}) collective-permute-start(f32[48,128]{1,0:T(8,128)S(1)} %get-tuple-element.41), channel_id=1, source_target_pairs={{0,2},{2,0},{4,6},{6,4},{8,10},{10,8},{12,14},{14,12},{16,18},{18,... | collective-permute-start | bytes 73736 | tf_op jit(solution)/shard_map/ppermute | solution.py:555
  41.6 2.6 %collective-permute-start.14 = (f32[96,128]{1,0:T(8,128)S(1)}, f32[96,128]{1,0:T(8,128)S(1)}, u32[]{:S(2)}, u32[]{:S(2)}) collective-permute-start(f32[96,128]{1,0:T(8,128)S(1)} %get-tuple-element.40), channel_id=1, source_target_pairs={{0,24},{2,26},{4,28},{6,30},{8,16},{10,18},{12,20},{14,22},{16,8},... | collective-permute-start | bytes 147464 | tf_op jit(solution)/shard_map/ppermute | solution.py:555
  44.2 0.0 collective-permute-start.12
  44.2 4.1 %collective-permute-done.12 = f32[96,128]{1,0:T(8,128)S(1)} collective-permute-done((f32[96,128]{1,0:T(8,128)S(1)}, f32[96,128]{1,0:T(8,128)S(1)}, u32[]{:S(2)}, u32[]{:S(2)}) %collective-permute-start.12) | collective-permute-done | bytes 49184 | tf_op jit(solution)/shard_map/ppermute | solution.py:555
  48.3 0.3 collective-permute-start.13
  48.6 7.7 %collective-permute-done.13 = f32[96,128]{1,0:T(8,128)S(1)} collective-permute-done((f32[96,128]{1,0:T(8,128)S(1)}, f32[96,128]{1,0:T(8,128)S(1)}, u32[]{:S(2)}, u32[]{:S(2)}) %collective-permute-start.13) | collective-permute-done | bytes 49184 | tf_op jit(solution)/shard_map/ppermute | solution.py:555
  56.3 0.0 collective-permute-done.14
  56.3 0.6 collective-permute-start.18
  56.9 0.0 collective-permute-done.15
  56.9 0.0 collective-permute-done.16
  57.0 0.0 collective-permute-done.17
  57.0 1.2 %collective-permute-start.23 = (f32[192,128]{1,0:T(8,128)S(1)}, f32[192,128]{1,0:T(8,128)S(1)}, u32[]{:S(2)}, u32[]{:S(2)}) collective-permute-start(f32[192,128]{1,0:T(8,128)S(1)} %get-tuple-element.53), channel_id=1, source_target_pairs={{0,24},{2,26},{4,28},{6,30},{8,16},{10,18},{12,20},{14,22},{16,8},... | collective-permute-start | bytes 294920 | tf_op jit(solution)/shard_map/ppermute | solution.py:555
  58.2 0.0 collective-permute-start.21
  58.2 3.2 %collective-permute-start.19 = (f32[192,128]{1,0:T(8,128)S(1)}, f32[192,128]{1,0:T(8,128)S(1)}, u32[]{:S(2)}, u32[]{:S(2)}) collective-permute-start(f32[192,128]{1,0:T(8,128)S(1)} %get-tuple-element.53), channel_id=1, source_target_pairs={{0,8},{2,10},{4,12},{6,14},{8,0},{10,2},{12,4},{14,6},{16,24},{18,... | collective-permute-start | bytes 294920 | tf_op jit(solution)/shard_map/ppermute | solution.py:555
  61.4 1.2 %collective-permute-start.22 = (f32[384,128]{1,0:T(8,128)S(1)}, f32[384,128]{1,0:T(8,128)S(1)}, u32[]{:S(2)}, u32[]{:S(2)}) collective-permute-start(f32[384,128]{1,0:T(8,128)S(1)} %get-tuple-element.45), channel_id=1, source_target_pairs={{0,6},{2,4},{4,2},{6,0},{8,14},{10,12},{12,10},{14,8},{16,22},{18,... | collective-permute-start | bytes 589832 | tf_op jit(solution)/shard_map/ppermute | solution.py:555
  62.7 0.0 collective-permute-done.18
  62.7 1.7 %collective-permute-start.20 = (f32[384,128]{1,0:T(8,128)S(1)}, f32[384,128]{1,0:T(8,128)S(1)}, u32[]{:S(2)}, u32[]{:S(2)}) collective-permute-start(f32[384,128]{1,0:T(8,128)S(1)} %get-tuple-element.45), channel_id=1, source_target_pairs={{0,4},{2,6},{4,0},{6,2},{8,12},{10,14},{12,8},{14,10},{16,20},{18,... | collective-permute-start | bytes 589832 | tf_op jit(solution)/shard_map/ppermute | solution.py:555
  64.4 0.2 collective-permute-done.19
  64.6 0.0 collective-permute-start.24
  64.6 5.5 %collective-permute-done.20 = f32[384,128]{1,0:T(8,128)S(1)} collective-permute-done((f32[384,128]{1,0:T(8,128)S(1)}, f32[384,128]{1,0:T(8,128)S(1)}, u32[]{:S(2)}, u32[]{:S(2)}) %collective-permute-start.20) | collective-permute-done | bytes 196640 | tf_op jit(solution)/shard_map/ppermute | solution.py:555
  70.1 0.0 collective-permute-start.25
  70.1 0.0 collective-permute-done.21
  70.2 0.6 collective-permute-start.26
  70.7 0.0 collective-permute-done.22
  70.8 0.0 collective-permute-done.23
  70.8 0.1 collective-permute-start.27
  70.9 0.0 collective-permute-done.24.refs_4_
  70.9 0.8 collective-permute-done.25.refs_5_
  71.7 0.4 collective-permute-done.26.refs_6_
  72.1 0.4 collective-permute-done.27.refs_7_
  72.6 0.0 copy-done
  72.6 34.0 %factor.1 = (f32[64,512]{1,0:T(8,128)}, f32[1,512]{1,0:T(1,128)}, f32[1,512]{1,0:T(1,128)}) custom-call(f32[576,128]{1,0:T(8,128)S(1)} %get-tuple-element.54.refs_0_, f32[576,128]{1,0:T(8,128)S(1)} %constant_dynamic-update-slice_fusion.16.refs_1_, f32[576,128]{1,0:T(8,128)S(1)} %constant_dynamic-update-slice_fusion.18.refs_2_, ...), custom_call_target="tpu_custom_call" | custom-call | tf_op jit(solution)/shard_map/factor/pallas_call | solution.py:595
  (16 shorter events, 0.2 us)
Async XLA Ops:
  7.3 65.2 %copy-start = (f32[512,1024]{1,0:T(8,128)S(1)}, f32[512,1024]{1,0:T(8,128)}, u32[]{:S(2)}) copy-start(f32[512,1024]{1,0:T(8,128)} %refs_8_.1) | copy-start | bytes 6291460
  7.4 9.2 %collective-permute-start.3 = (f32[192,128]{1,0:T(8,128)}, f32[192,128]{1,0:T(8,128)S(1)}, u32[]{:S(2)}, u32[]{:S(2)}) collective-permute-start(f32[192,128]{1,0:T(8,128)} %get-tuple-element.29), channel_id=1, source_target_pairs={{0,8},{2,10},{4,12},{6,14},{8,0},{10,2},{12,4},{14,6},{16,24},{18,... | collective-permute-start | bytes 294920 | tf_op jit(solution)/shard_map/ppermute | solution.py:555
  10.4 13.2 %collective-permute-start = (f32[384,128]{1,0:T(8,128)}, f32[384,128]{1,0:T(8,128)S(1)}, u32[]{:S(2)}, u32[]{:S(2)}) collective-permute-start(f32[384,128]{1,0:T(8,128)} %get-tuple-element.25), channel_id=1, source_target_pairs={{0,2},{2,0},{4,6},{6,4},{8,10},{10,8},{12,14},{14,12},{16,18},{18,... | collective-permute-start | bytes 589832 | tf_op jit(solution)/shard_map/ppermute | solution.py:555
  11.9 11.7 %collective-permute-start.1 = (f32[384,128]{1,0:T(8,128)}, f32[384,128]{1,0:T(8,128)S(1)}, u32[]{:S(2)}, u32[]{:S(2)}) collective-permute-start(f32[384,128]{1,0:T(8,128)} %get-tuple-element.26), channel_id=1, source_target_pairs={{0,4},{2,6},{4,0},{6,2},{8,12},{10,14},{12,8},{14,10},{16,20},{18,... | collective-permute-start | bytes 589832 | tf_op jit(solution)/shard_map/ppermute | solution.py:555
  13.5 10.2 %collective-permute-start.2 = (f32[384,128]{1,0:T(8,128)}, f32[384,128]{1,0:T(8,128)S(1)}, u32[]{:S(2)}, u32[]{:S(2)}) collective-permute-start(f32[384,128]{1,0:T(8,128)} %get-tuple-element.27), channel_id=1, source_target_pairs={{0,6},{2,4},{4,2},{6,0},{8,14},{10,12},{12,10},{14,8},{16,22},{18,... | collective-permute-start | bytes 589832 | tf_op jit(solution)/shard_map/ppermute | solution.py:555
  13.9 9.7 %collective-permute-start.4 = (f32[192,128]{1,0:T(8,128)}, f32[192,128]{1,0:T(8,128)S(1)}, u32[]{:S(2)}, u32[]{:S(2)}) collective-permute-start(f32[192,128]{1,0:T(8,128)} %get-tuple-element.30), channel_id=1, source_target_pairs={{0,16},{2,18},{4,20},{6,22},{8,24},{10,26},{12,28},{14,30},{16,0},... | collective-permute-start | bytes 294920 | tf_op jit(solution)/shard_map/ppermute | solution.py:555
  16.5 7.1 %collective-permute-start.5 = (f32[192,128]{1,0:T(8,128)}, f32[192,128]{1,0:T(8,128)S(1)}, u32[]{:S(2)}, u32[]{:S(2)}) collective-permute-start(f32[192,128]{1,0:T(8,128)} %get-tuple-element.31), channel_id=1, source_target_pairs={{0,24},{2,26},{4,28},{6,30},{8,16},{10,18},{12,20},{14,22},{16,8},... | collective-permute-start | bytes 294920 | tf_op jit(solution)/shard_map/ppermute | solution.py:555
  23.6 0.9 copy-start.1
  24.5 0.9 copy-start.2
  25.5 7.7 %collective-permute-start.9 = (f32[48,128]{1,0:T(8,128)S(1)}, f32[48,128]{1,0:T(8,128)S(1)}, u32[]{:S(2)}, u32[]{:S(2)}) collective-permute-start(f32[48,128]{1,0:T(8,128)S(1)} %get-tuple-element.37), channel_id=1, source_target_pairs={{0,2},{2,0},{4,6},{6,4},{8,10},{10,8},{12,14},{14,12},{16,18},{18,... | collective-permute-start | bytes 73736 | tf_op jit(solution)/shard_map/ppermute | solution.py:555
  27.3 10.7 %collective-permute-start.6 = (f32[96,128]{1,0:T(8,128)S(1)}, f32[96,128]{1,0:T(8,128)S(1)}, u32[]{:S(2)}, u32[]{:S(2)}) collective-permute-start(f32[96,128]{1,0:T(8,128)S(1)} %get-tuple-element.33), channel_id=1, source_target_pairs={{0,8},{2,10},{4,12},{6,14},{8,0},{10,2},{12,4},{14,6},{16,24},{18,... | collective-permute-start | bytes 147464 | tf_op jit(solution)/shard_map/ppermute | solution.py:555
  28.9 9.1 %collective-permute-start.7 = (f32[96,128]{1,0:T(8,128)S(1)}, f32[96,128]{1,0:T(8,128)S(1)}, u32[]{:S(2)}, u32[]{:S(2)}) collective-permute-start(f32[96,128]{1,0:T(8,128)S(1)} %get-tuple-element.34), channel_id=1, source_target_pairs={{0,16},{2,18},{4,20},{6,22},{8,24},{10,26},{12,28},{14,30},{16,0},... | collective-permute-start | bytes 147464 | tf_op jit(solution)/shard_map/ppermute | solution.py:555
  30.4 7.6 %collective-permute-start.8 = (f32[96,128]{1,0:T(8,128)S(1)}, f32[96,128]{1,0:T(8,128)S(1)}, u32[]{:S(2)}, u32[]{:S(2)}) collective-permute-start(f32[96,128]{1,0:T(8,128)S(1)} %get-tuple-element.35), channel_id=1, source_target_pairs={{0,24},{2,26},{4,28},{6,30},{8,16},{10,18},{12,20},{14,22},{16,8},... | collective-permute-start | bytes 147464 | tf_op jit(solution)/shard_map/ppermute | solution.py:555
  31.6 3.8 %collective-permute-start.10 = (f32[48,128]{1,0:T(8,128)S(1)}, f32[48,128]{1,0:T(8,128)S(1)}, u32[]{:S(2)}, u32[]{:S(2)}) collective-permute-start(f32[48,128]{1,0:T(8,128)S(1)} %get-tuple-element.38), channel_id=1, source_target_pairs={{0,4},{2,6},{4,0},{6,2},{8,12},{10,14},{12,8},{14,10},{16,20},{18,... | collective-permute-start | bytes 73736 | tf_op jit(solution)/shard_map/ppermute | solution.py:555
  33.2 4.8 %collective-permute-start.11 = (f32[48,128]{1,0:T(8,128)S(1)}, f32[48,128]{1,0:T(8,128)S(1)}, u32[]{:S(2)}, u32[]{:S(2)}) collective-permute-start(f32[48,128]{1,0:T(8,128)S(1)} %get-tuple-element.39), channel_id=1, source_target_pairs={{0,6},{2,4},{4,2},{6,0},{8,14},{10,12},{12,10},{14,8},{16,22},{18,... | collective-permute-start | bytes 73736 | tf_op jit(solution)/shard_map/ppermute | solution.py:555
  38.0 18.9 %collective-permute-start.17 = (f32[48,128]{1,0:T(8,128)S(1)}, f32[48,128]{1,0:T(8,128)S(1)}, u32[]{:S(2)}, u32[]{:S(2)}) collective-permute-start(f32[48,128]{1,0:T(8,128)S(1)} %get-tuple-element.41), channel_id=1, source_target_pairs={{0,6},{2,4},{4,2},{6,0},{8,14},{10,12},{12,10},{14,8},{16,22},{18,... | collective-permute-start | bytes 73736 | tf_op jit(solution)/shard_map/ppermute | solution.py:555
  38.3 18.7 %collective-permute-start.16 = (f32[48,128]{1,0:T(8,128)S(1)}, f32[48,128]{1,0:T(8,128)S(1)}, u32[]{:S(2)}, u32[]{:S(2)}) collective-permute-start(f32[48,128]{1,0:T(8,128)S(1)} %get-tuple-element.41), channel_id=1, source_target_pairs={{0,4},{2,6},{4,0},{6,2},{8,12},{10,14},{12,8},{14,10},{16,20},{18,... | collective-permute-start | bytes 73736 | tf_op jit(solution)/shard_map/ppermute | solution.py:555
  40.0 16.9 %collective-permute-start.15 = (f32[48,128]{1,0:T(8,128)S(1)}, f32[48,128]{1,0:T(8,128)S(1)}, u32[]{:S(2)}, u32[]{:S(2)}) collective-permute-start(f32[48,128]{1,0:T(8,128)S(1)} %get-tuple-element.41), channel_id=1, source_target_pairs={{0,2},{2,0},{4,6},{6,4},{8,10},{10,8},{12,14},{14,12},{16,18},{18,... | collective-permute-start | bytes 73736 | tf_op jit(solution)/shard_map/ppermute | solution.py:555
  41.6 14.7 %collective-permute-start.14 = (f32[96,128]{1,0:T(8,128)S(1)}, f32[96,128]{1,0:T(8,128)S(1)}, u32[]{:S(2)}, u32[]{:S(2)}) collective-permute-start(f32[96,128]{1,0:T(8,128)S(1)} %get-tuple-element.40), channel_id=1, source_target_pairs={{0,24},{2,26},{4,28},{6,30},{8,16},{10,18},{12,20},{14,22},{16,8},... | collective-permute-start | bytes 147464 | tf_op jit(solution)/shard_map/ppermute | solution.py:555
  44.2 4.1 %collective-permute-start.12 = (f32[96,128]{1,0:T(8,128)S(1)}, f32[96,128]{1,0:T(8,128)S(1)}, u32[]{:S(2)}, u32[]{:S(2)}) collective-permute-start(f32[96,128]{1,0:T(8,128)S(1)} %get-tuple-element.40), channel_id=1, source_target_pairs={{0,8},{2,10},{4,12},{6,14},{8,0},{10,2},{12,4},{14,6},{16,24},{18,... | collective-permute-start | bytes 147464 | tf_op jit(solution)/shard_map/ppermute | solution.py:555
  48.3 7.9 %collective-permute-start.13 = (f32[96,128]{1,0:T(8,128)S(1)}, f32[96,128]{1,0:T(8,128)S(1)}, u32[]{:S(2)}, u32[]{:S(2)}) collective-permute-start(f32[96,128]{1,0:T(8,128)S(1)} %get-tuple-element.40), channel_id=1, source_target_pairs={{0,16},{2,18},{4,20},{6,22},{8,24},{10,26},{12,28},{14,30},{16,0},... | collective-permute-start | bytes 147464 | tf_op jit(solution)/shard_map/ppermute | solution.py:555
  56.3 6.4 %collective-permute-start.18 = (f32[384,128]{1,0:T(8,128)S(1)}, f32[384,128]{1,0:T(8,128)S(1)}, u32[]{:S(2)}, u32[]{:S(2)}) collective-permute-start(f32[384,128]{1,0:T(8,128)S(1)} %get-tuple-element.45), channel_id=1, source_target_pairs={{0,2},{2,0},{4,6},{6,4},{8,10},{10,8},{12,14},{14,12},{16,18},{18,... | collective-permute-start | bytes 589832 | tf_op jit(solution)/shard_map/ppermute | solution.py:555
  57.0 13.8 %collective-permute-start.23 = (f32[192,128]{1,0:T(8,128)S(1)}, f32[192,128]{1,0:T(8,128)S(1)}, u32[]{:S(2)}, u32[]{:S(2)}) collective-permute-start(f32[192,128]{1,0:T(8,128)S(1)} %get-tuple-element.53), channel_id=1, source_target_pairs={{0,24},{2,26},{4,28},{6,30},{8,16},{10,18},{12,20},{14,22},{16,8},... | collective-permute-start | bytes 294920 | tf_op jit(solution)/shard_map/ppermute | solution.py:555
  58.2 11.9 %collective-permute-start.21 = (f32[192,128]{1,0:T(8,128)S(1)}, f32[192,128]{1,0:T(8,128)S(1)}, u32[]{:S(2)}, u32[]{:S(2)}) collective-permute-start(f32[192,128]{1,0:T(8,128)S(1)} %get-tuple-element.53), channel_id=1, source_target_pairs={{0,16},{2,18},{4,20},{6,22},{8,24},{10,26},{12,28},{14,30},{16,0},... | collective-permute-start | bytes 294920 | tf_op jit(solution)/shard_map/ppermute | solution.py:555
  58.2 6.4 %collective-permute-start.19 = (f32[192,128]{1,0:T(8,128)S(1)}, f32[192,128]{1,0:T(8,128)S(1)}, u32[]{:S(2)}, u32[]{:S(2)}) collective-permute-start(f32[192,128]{1,0:T(8,128)S(1)} %get-tuple-element.53), channel_id=1, source_target_pairs={{0,8},{2,10},{4,12},{6,14},{8,0},{10,2},{12,4},{14,6},{16,24},{18,... | collective-permute-start | bytes 294920 | tf_op jit(solution)/shard_map/ppermute | solution.py:555
  61.4 9.3 %collective-permute-start.22 = (f32[384,128]{1,0:T(8,128)S(1)}, f32[384,128]{1,0:T(8,128)S(1)}, u32[]{:S(2)}, u32[]{:S(2)}) collective-permute-start(f32[384,128]{1,0:T(8,128)S(1)} %get-tuple-element.45), channel_id=1, source_target_pairs={{0,6},{2,4},{4,2},{6,0},{8,14},{10,12},{12,10},{14,8},{16,22},{18,... | collective-permute-start | bytes 589832 | tf_op jit(solution)/shard_map/ppermute | solution.py:555
  62.7 7.4 %collective-permute-start.20 = (f32[384,128]{1,0:T(8,128)S(1)}, f32[384,128]{1,0:T(8,128)S(1)}, u32[]{:S(2)}, u32[]{:S(2)}) collective-permute-start(f32[384,128]{1,0:T(8,128)S(1)} %get-tuple-element.45), channel_id=1, source_target_pairs={{0,4},{2,6},{4,0},{6,2},{8,12},{10,14},{12,8},{14,10},{16,20},{18,... | collective-permute-start | bytes 589832 | tf_op jit(solution)/shard_map/ppermute | solution.py:555
  64.6 6.3 %collective-permute-start.24 = (f32[576,128]{1,0:T(8,128)S(1)}, f32[576,128]{1,0:T(8,128)S(1)}, u32[]{:S(2)}, u32[]{:S(2)}) collective-permute-start(f32[576,128]{1,0:T(8,128)S(1)} %get-tuple-element.54.refs_0_), channel_id=1, source_target_pairs={{0,1},{1,0},{2,3},{3,2},{4,5},{5,4},{6,7},{7,6},{8,9},{9,8},{10,11... | collective-permute-start | bytes 884744 | tf_op jit(solution)/shard_map/ppermute | solution.py:590
  70.1 1.6 %collective-permute-start.25 = (f32[576,128]{1,0:T(8,128)S(1)}, f32[576,128]{1,0:T(8,128)S(1)}, u32[]{:S(2)}, u32[]{:S(2)}) collective-permute-start(f32[576,128]{1,0:T(8,128)S(1)} %constant_dynamic-update-slice_fusion.16.refs_1_), channel_id=1, source_target_pairs={{0,1},{1,0},{2,3},{3,2},{4,5},{5,4},{6,7},{7,6},{8,9},{9,8},{10,11... | collective-permute-start | bytes 884744 | tf_op jit(solution)/shard_map/ppermute | solution.py:590
  70.2 2.0 %collective-permute-start.26 = (f32[576,128]{1,0:T(8,128)S(1)}, f32[576,128]{1,0:T(8,128)S(1)}, u32[]{:S(2)}, u32[]{:S(2)}) collective-permute-start(f32[576,128]{1,0:T(8,128)S(1)} %constant_dynamic-update-slice_fusion.18.refs_2_), channel_id=1, source_target_pairs={{0,1},{1,0},{2,3},{3,2},{4,5},{5,4},{6,7},{7,6},{8,9},{9,8},{10,11... | collective-permute-start | bytes 884744 | tf_op jit(solution)/shard_map/ppermute | solution.py:590
  70.8 1.8 %collective-permute-start.27 = (f32[576,128]{1,0:T(8,128)S(1)}, f32[576,128]{1,0:T(8,128)S(1)}, u32[]{:S(2)}, u32[]{:S(2)}) collective-permute-start(f32[576,128]{1,0:T(8,128)S(1)} %constant_dynamic-update-slice_fusion.20.refs_3_), channel_id=1, source_target_pairs={{0,1},{1,0},{2,3},{3,2},{4,5},{5,4},{6,7},{7,6},{8,9},{9,8},{10,11... | collective-permute-start | bytes 884744 | tf_op jit(solution)/shard_map/ppermute | solution.py:590

commit v5 on v4

--- a/solution.py
+++ b/solution.py
@@ -53,12 +53,11 @@
             self.stride.append(step)
             step *= f
         stages = list(range(len(self.radix)))
-        self.orders = (stages, stages[::-1])
+        self.orders = (stages,)
         tiles = [(i, j) for i in range(nb) for j in range(i, nb)]
         share = -(-len(tiles) // cols)
         piece = -(-share * BLK // (8 * rows)) * 8
-        small = max(8, piece // 24 * 8)
-        self.pieces = (piece - small, small)
+        self.pieces = (piece,)
         self.half = rows * piece
         self.local = {}
         for index, tile in enumerate(tiles):
@@ -86,7 +85,7 @@
 
 
 def assemble_kernel(plan, *refs):
-    fans = [plan.fan(flow, 0) for flow in range(2)]
+    fans = [plan.fan(flow, 0) for flow in range(len(plan.orders))]
     ins, outs, scratch = refs[:9], refs[9 : 9 + sum(fans)], refs[9 + sum(fans) :]
     here, (sens_hi, sens_lo, at_hi, at_lo, prior_pad, packed, sems) = scratch[:9], scratch[9:]
     copies = [pltpu.make_async_copy(a, b, sems.at[i]) for i, (a, b) in enumerate(zip(ins, here))]
@@ -184,7 +183,7 @@
         pl.when(core == part)(functools.partial(tiles_of, part))
 
     outs = list(outs)
-    for flow in range(2):
+    for flow in range(len(plan.orders)):
         span, stage = plan.span(flow, 0), plan.orders[flow][0]
         for d in range(fans[flow]):
             at = plan.base(flow) + (plan.digit(me, stage) ^ d) * span
@@ -194,9 +193,9 @@
 def sum_kernel(plan, step, *refs):
     me = lax.axis_index("rows")
     refs = list(refs)
-    ins = [[refs.pop(0) for _ in range(plan.fan(flow, step))] for flow in range(2)]
+    ins = [[refs.pop(0) for _ in range(plan.fan(flow, step))] for flow in range(len(plan.orders))]
     last = step + 1 == len(plan.radix)
-    for flow in range(2):
+    for flow in range(len(plan.orders)):
         count = 1 if last else plan.fan(flow, step + 1)
         span = plan.span(flow, step + 1)
         for d in range(count):
@@ -309,24 +308,18 @@
         solved = row_ref[...]
         inv_ref[r0 : r0 + MIC, :] = jnp.where(lane < r0 + MIC, solved, 0.0)
         if r0 + MIC < BLK:
-            high, low_part = split2(solved)
-            fix = dot(
-                jnp.concatenate([high, high, low_part], axis=0),
-                jnp.concatenate([high, low_part, high], axis=0),
-                0,
-                0,
-            )
+            fix = dot3(split2(solved.T[r0 + MIC :, :]), split2(solved))
             lanes = lax.broadcasted_iota(jnp.int32, (BLK - r0 - MIC, BLK), 1)
             keep = (lanes < r0) | (lanes >= r0 + MIC)
             left = jnp.where(keep, d_ref[r0 + MIC :, :], 0.0)
-            d_ref[r0 + MIC :, :] = left - fix[r0 + MIC :, :]
+            d_ref[r0 + MIC :, :] = left - fix
     while queue:
         queue.pop(0)()
 
 
 def factor_kernel(plan, out_rows, width, *refs):
     n, nb = plan.state_total, plan.blocks
-    slots = max(plan.fan(flow, 0) for flow in range(2))
+    slots = max(plan.fan(flow, 0) for flow in range(len(plan.orders)))
     ins, (trans_hbm, r_ref, z_ref, x_ref, *scratch) = refs[: slots * plan.cols], refs[slots * plan.cols :]
     (
         packed,
@@ -337,6 +330,8 @@
         strip_ref,
         row_ref,
         panel_ref,
+        turn_ref,
+        next_ref,
         full_ref,
         trans_ref,
         col_ref,
@@ -351,7 +346,7 @@
     copies = []
     for e in range(plan.cols):
         offsets = [0] * slots
-        for flow in range(2):
+        for flow in range(len(plan.orders)):
             piece, order = plan.pieces[flow], plan.orders[flow]
             inner = plan.span(flow, 0) // piece
             for d in range(plan.fan(flow, 0)):
@@ -419,19 +414,43 @@
     def lanes_of(tiles):
         return slice(tiles[0] * BLK, (tiles[-1] + 1) * BLK)
 
-    def updated(k, tiles):
+    def updated(k, tiles, upto=None):
         value = base(k, tiles[0])
         if len(tiles) > 1:
             value = jnp.concatenate([base(k, j) for j in tiles], axis=1)
-        if k:
-            rows, done = slice(k * BLK, (k + 1) * BLK), slice(0, k * BLK)
+        if upto is None:
+            upto = k
+        if upto:
+            rows, done = slice(k * BLK, (k + 1) * BLK), slice(0, upto * BLK)
             value = value - dot3(
                 [ref[rows, done] for ref in left], [ref[done, lanes_of(tiles)] for ref in right]
             )
         return value
 
     def prepare(k, tiles):
-        panel_ref[k % 2, :, lanes_of(tiles)] = updated(k, tiles)
+        value = updated(k, tiles)
+        panel_ref[k % 2, :, lanes_of(tiles)] = value
+        if k + 1 < nb and k + 1 in tiles:
+            at = tiles.index(k + 1) * BLK
+            turn_ref[...] = value[:, at : at + BLK].T
+
+    def prepare_diagonal(k):
+        next_ref[...] = updated(k, [k], k - 1)
+
+    def start_next(k, inverse):
+        rows, lanes = slice(k * BLK, (k + 1) * BLK), lanes_of([k + 1])
+        high, low = split2(panel_ref[k % 2, :, lanes])
+        value = dot(inverse, jnp.concatenate([high, low, high], axis=0))
+        turned_high, turned_low = split2(turn_ref[...])
+        mirror = dot(jnp.concatenate([turned_high, turned_low, turned_high], axis=1), inverse, 1, 1)
+        straight, mirrored = split2(value), split2(mirror)
+        for part in range(2):
+            right[part][rows, lanes] = straight[part]
+            left[part][lanes, rows] = mirrored[part]
+        full_ref[rows, lanes] = value * root_ref[k + 1 : k + 2, :]
+        diagonal = next_ref[...] - dot3(mirrored, straight)
+        d_ref[...] = diagonal
+        panel_ref[(k + 1) % 2, :, lanes] = diagonal
 
     z_tile = [None]
 
@@ -474,15 +493,17 @@
         return found
 
     queue = []
+    d_ref[...] = base(0, 0)
+    panel_ref[0, :, 0:BLK] = d_ref[...]
     for k in range(nb):
-        d_ref[...] = updated(k, [k])
-        panel_ref[k % 2, :, k * BLK : (k + 1) * BLK] = d_ref[...]
         queue += [functools.partial(prepare, k, tiles) for tiles in groups(k + 1)]
+        if k + 1 < nb:
+            queue.append(functools.partial(prepare_diagonal, k + 1))
         factor_block(d_ref, inv_ref, cast_ref, times_ref, strip_ref, row_ref, queue)
         inv_high, inv_low = split2(inv_ref[...])
         inverse = jnp.concatenate([inv_high, inv_high, inv_low], axis=1)
         if k + 1 < nb:
-            finish(k, [k + 1], inverse)
+            start_next(k, inverse)
         queue += [functools.partial(finish, k, tiles, inverse) for tiles in groups(min(k + 2, nb))]
         queue.append(functools.partial(finish, k, [k], inverse))
     while queue:
@@ -533,9 +554,9 @@
     )
     parts = pl.pallas_call(
         functools.partial(assemble_kernel, plan),
-        out_shape=[typed(plan.span(f, 0), BLK) for f in range(2) for _ in range(plan.fan(f, 0))],
+        out_shape=[typed(plan.span(f, 0), BLK) for f in range(len(plan.orders)) for _ in range(plan.fan(f, 0))],
         in_specs=[hbm] * len(inputs),
-        out_specs=[vmem] * sum(plan.fan(f, 0) for f in range(2)),
+        out_specs=[vmem] * sum(plan.fan(f, 0) for f in range(len(plan.orders))),
         scratch_shapes=[pltpu.VMEM(x.shape, x.dtype) for x in inputs]
         + [
             pltpu.VMEM((n + 16, block_rows), BF16),
@@ -558,14 +579,14 @@
     for step in range(steps):
         parts = list(parts)
         got = []
-        for flow in range(2):
+        for flow in range(len(plan.orders)):
             fan, stage = plan.fan(flow, step), plan.orders[flow][step]
             mine = [parts.pop(0) for _ in range(fan)]
             got += mine[:1] + [exchange(stage, d, mine[d]) for d in range(1, fan)]
         last = step + 1 == steps
         shapes = [
             typed(plan.span(flow, step + 1), BLK)
-            for flow in range(2)
+            for flow in range(len(plan.orders))
             for _ in range(1 if last else plan.fan(flow, step + 1))
         ]
         parts = pl.pallas_call(
@@ -577,16 +598,13 @@
     blocks = list(parts)
     for step in reversed(range(steps)):
         got = []
-        for flow in range(2):
+        for flow in range(len(plan.orders)):
             fan, stage = plan.fan(flow, step), plan.orders[flow][step]
             got.append([blocks[flow]] + [exchange(stage, d, blocks[flow]) for d in range(1, fan)])
         if step:
             blocks = [jnp.concatenate(found, axis=0) for found in got]
     swap = [(i, i ^ 1) for i in range(cols)]
-    joined = [
-        jnp.concatenate([found[d] for found in got if d < len(found)], axis=0)
-        for d in range(max(len(found) for found in got))
-    ]
+    (joined,) = got
     both = joined + [lax.ppermute(block, "cols", swap) for block in joined]
 
     width = n // cols
@@ -606,6 +624,8 @@
             pltpu.VMEM((MIC, BLK), F32),
             pltpu.VMEM((MIC, BLK), F32),
             pltpu.VMEM((2, BLK, wide), F32),
+            pltpu.VMEM((BLK, BLK), F32),
+            pltpu.VMEM((BLK, BLK), F32),
             pltpu.VMEM((n, n), F32),
             pltpu.VMEM((width, n), F32),
             pltpu.VMEM((plan.blocks, BLK, BLK), F32),
@@ -615,7 +635,7 @@
             pltpu.VMEM((n, wide), BF16),
             pltpu.VMEM((n, wide), BF16),
             pltpu.VMEM((1, n), F32),
-            pltpu.SemaphoreType.DMA((2 * rows * cols,)),
+            pltpu.SemaphoreType.DMA((rows * cols,)),
             pltpu.SemaphoreType.DMA,
         ],
         compiler_params=params,

time: 107 us -> 94.9 us (0.89)
  starting transfers between devices: 33.1 us -> 17.5 us
  waiting for transfers between devices: 29.9 us -> 33.9 us
    ppermute x24 -> x12, starting transfers between devices: 32.4 us -> 17 us  [exchange(): return lax.ppermute(block, 'rows', [(i, i ^ flip) for i in range(rows)])]
    ppermute x24 -> x12, waiting for transfers between devices: 28.2 us -> 32.4 us  [exchange(): return lax.ppermute(block, 'rows', [(i, i ^ flip) for i in range(rows)])]
  transfers between devices with their start and end apart: 28 -> 16, of which waited for: 10 -> 11; matrix products, arithmetic and copies ran while one was open for 0% -> 0% of each run, Pallas kernels for 0% -> 0%
where the time goes in v5:
time: 94.9 us; the launch traced here: 94.7 us
  Pallas kernels  41.4 us (44%)
  waiting for transfers between devices  33.9 us (36%)
  starting transfers between devices  17.5 us (18%)
  local copies, waits for them, and re-layouts  0.97 us (1%)
    pallas_call x1, Pallas kernels, per_device(): pl.pallas_call(functools.partial(factor_kernel, plan, out_rows, width), o...  34.6 us
    ppermute x12, waiting for transfers between devices, exchange(): return lax.ppermute(block, 'rows', [(i, i ^ flip) for i in range(rows)])  32.4 us
    ppermute x12, starting transfers between devices, exchange(): return lax.ppermute(block, 'rows', [(i, i ^ flip) for i in range(rows)])  17 us
    pallas_call x1, Pallas kernels, per_device(): pl.pallas_call(functools.partial(assemble_kernel, plan), out_shape=[typed...  6.73 us
  transfers between devices with their start and end apart: 16, of which 11 were waited for; matrix products, arithmetic and copies ran while one was open for 0% of the time, Pallas kernels for 0%

profile of v5, /device:TPU:0, one launch (start us, length us, event | category | flops | bytes accessed | tf_op | source)
XLA Modules:
  0.0 94.7 jit_solution(1784413334602087636)
XLA Ops:
  0.6 6.7 %assemble.1 = (f32[576,128]{1,0:T(8,128)}, f32[576,128]{1,0:T(8,128)}, f32[576,128]{1,0:T(8,128)}, f32[576,128]{1,0:T(8,128)}) custom-call(f32[384,384]{1,0:T(8,128)} %refs_0_.1, s32[4,384]{1,0:T(4,128)} %bitcast.9, f32[4,384]{1,0:T(4,128)} %bitcast.10, f32[3,128]{1,0:T(4,128)} %bitcast.11, s32[2,128]{1,0:T(2,128)} %bitcast.12, f32[1,128]{1,0:T(1,128)} %bitcast.13, ...), custom_call_target="tpu_custom_call" | custom-call | tf_op jit(solution)/shard_map/assemble/pallas_call | solution.py:555
  7.4 0.0 copy-start
  7.4 3.0 %collective-permute-start = (f32[576,128]{1,0:T(8,128)}, f32[576,128]{1,0:T(8,128)S(1)}, u32[]{:S(2)}, u32[]{:S(2)}) collective-permute-start(f32[576,128]{1,0:T(8,128)} %get-tuple-element.15), channel_id=1, source_target_pairs={{0,2},{2,0},{4,6},{6,4},{8,10},{10,8},{12,14},{14,12},{16,18},{18,... | collective-permute-start | bytes 884744 | tf_op jit(solution)/shard_map/ppermute | solution.py:576
  10.4 1.5 %collective-permute-start.1 = (f32[576,128]{1,0:T(8,128)}, f32[576,128]{1,0:T(8,128)S(1)}, u32[]{:S(2)}, u32[]{:S(2)}) collective-permute-start(f32[576,128]{1,0:T(8,128)} %get-tuple-element.16), channel_id=1, source_target_pairs={{0,4},{2,6},{4,0},{6,2},{8,12},{10,14},{12,8},{14,10},{16,20},{18,... | collective-permute-start | bytes 884744 | tf_op jit(solution)/shard_map/ppermute | solution.py:576
  11.9 0.0 collective-permute-start.2
  11.9 6.5 %collective-permute-done.refs_1_ = f32[576,128]{1,0:T(8,128)S(1)} collective-permute-done((f32[576,128]{1,0:T(8,128)}, f32[576,128]{1,0:T(8,128)S(1)}, u32[]{:S(2)}, u32[]{:S(2)}) %collective-permute-start) | collective-permute-done | bytes 294944 | tf_op jit(solution)/shard_map/ppermute | solution.py:576
  18.4 7.2 %collective-permute-done.1.refs_2_ = f32[576,128]{1,0:T(8,128)S(1)} collective-permute-done((f32[576,128]{1,0:T(8,128)}, f32[576,128]{1,0:T(8,128)S(1)}, u32[]{:S(2)}, u32[]{:S(2)}) %collective-permute-start.1) | collective-permute-done | bytes 294944 | tf_op jit(solution)/shard_map/ppermute | solution.py:576
  25.6 0.0 collective-permute-done.2.refs_3_
  25.6 0.0 copy-start.1
  25.6 1.0 %copy-done.1 = f32[576,128]{1,0:T(8,128)S(1)} copy-done((f32[576,128]{1,0:T(8,128)S(1)}, f32[576,128]{1,0:T(8,128)}, u32[]{:S(2)}) %copy-start.1) | copy-done | bytes 294936
  26.5 0.1 partial_sums.2
  26.6 1.6 %collective-permute-start.3 = (f32[144,128]{1,0:T(8,128)S(1)}, f32[144,128]{1,0:T(8,128)S(1)}, u32[]{:S(2)}, u32[]{:S(2)}) collective-permute-start(f32[144,128]{1,0:T(8,128)S(1)} %get-tuple-element.19), channel_id=1, source_target_pairs={{0,8},{2,10},{4,12},{6,14},{8,0},{10,2},{12,4},{14,6},{16,24},{18,... | collective-permute-start | bytes 221192 | tf_op jit(solution)/shard_map/ppermute | solution.py:576
  28.2 2.6 %collective-permute-start.4 = (f32[144,128]{1,0:T(8,128)S(1)}, f32[144,128]{1,0:T(8,128)S(1)}, u32[]{:S(2)}, u32[]{:S(2)}) collective-permute-start(f32[144,128]{1,0:T(8,128)S(1)} %get-tuple-element.20), channel_id=1, source_target_pairs={{0,16},{2,18},{4,20},{6,22},{8,24},{10,26},{12,28},{14,30},{16,0},... | collective-permute-start | bytes 221192 | tf_op jit(solution)/shard_map/ppermute | solution.py:576
  30.8 0.2 collective-permute-start.5
  31.0 0.7 collective-permute-done.3.refs_1_
  31.7 3.4 %collective-permute-done.4.refs_2_ = f32[144,128]{1,0:T(8,128)S(1)} collective-permute-done((f32[144,128]{1,0:T(8,128)S(1)}, f32[144,128]{1,0:T(8,128)S(1)}, u32[]{:S(2)}, u32[]{:S(2)}) %collective-permute-start.4) | collective-permute-done | bytes 73760 | tf_op jit(solution)/shard_map/ppermute | solution.py:576
  35.1 1.9 %collective-permute-done.5.refs_3_ = f32[144,128]{1,0:T(8,128)S(1)} collective-permute-done((f32[144,128]{1,0:T(8,128)S(1)}, f32[144,128]{1,0:T(8,128)S(1)}, u32[]{:S(2)}, u32[]{:S(2)}) %collective-permute-start.5) | collective-permute-done | bytes 73760 | tf_op jit(solution)/shard_map/ppermute | solution.py:576
  37.1 2.0 %collective-permute-start.8 = (f32[144,128]{1,0:T(8,128)S(1)}, f32[144,128]{1,0:T(8,128)S(1)}, u32[]{:S(2)}, u32[]{:S(2)}) collective-permute-start(f32[144,128]{1,0:T(8,128)S(1)} %partial_sums.3), channel_id=1, source_target_pairs={{0,24},{2,26},{4,28},{6,30},{8,16},{10,18},{12,20},{14,22},{16,8},... | collective-permute-start | bytes 221192 | tf_op jit(solution)/shard_map/ppermute | solution.py:576
  39.1 0.2 collective-permute-start.7
  39.4 2.2 %collective-permute-start.6 = (f32[144,128]{1,0:T(8,128)S(1)}, f32[144,128]{1,0:T(8,128)S(1)}, u32[]{:S(2)}, u32[]{:S(2)}) collective-permute-start(f32[144,128]{1,0:T(8,128)S(1)} %partial_sums.3), channel_id=1, source_target_pairs={{0,8},{2,10},{4,12},{6,14},{8,0},{10,2},{12,4},{14,6},{16,24},{18,... | collective-permute-start | bytes 221192 | tf_op jit(solution)/shard_map/ppermute | solution.py:576
  41.6 1.8 %collective-permute-done.8 = f32[144,128]{1,0:T(8,128)S(1)} collective-permute-done((f32[144,128]{1,0:T(8,128)S(1)}, f32[144,128]{1,0:T(8,128)S(1)}, u32[]{:S(2)}, u32[]{:S(2)}) %collective-permute-start.8) | collective-permute-done | bytes 73760 | tf_op jit(solution)/shard_map/ppermute | solution.py:576
  43.3 1.8 %collective-permute-done.7 = f32[144,128]{1,0:T(8,128)S(1)} collective-permute-done((f32[144,128]{1,0:T(8,128)S(1)}, f32[144,128]{1,0:T(8,128)S(1)}, u32[]{:S(2)}, u32[]{:S(2)}) %collective-permute-start.7) | collective-permute-done | bytes 73760 | tf_op jit(solution)/shard_map/ppermute | solution.py:576
  45.2 0.0 collective-permute-done.6
  45.2 1.5 %collective-permute-start.11 = (f32[576,128]{1,0:T(8,128)S(1)}, f32[576,128]{1,0:T(8,128)S(1)}, u32[]{:S(2)}, u32[]{:S(2)}) collective-permute-start(f32[576,128]{1,0:T(8,128)S(1)} %pad_maximum_fusion.refs_0_), channel_id=1, source_target_pairs={{0,6},{2,4},{4,2},{6,0},{8,14},{10,12},{12,10},{14,8},{16,22},{18,... | collective-permute-start | bytes 884744 | tf_op jit(solution)/shard_map/ppermute | solution.py:576
  46.7 0.9 collective-permute-start.10
  47.6 1.2 %collective-permute-start.9 = (f32[576,128]{1,0:T(8,128)S(1)}, f32[576,128]{1,0:T(8,128)S(1)}, u32[]{:S(2)}, u32[]{:S(2)}) collective-permute-start(f32[576,128]{1,0:T(8,128)S(1)} %pad_maximum_fusion.refs_0_), channel_id=1, source_target_pairs={{0,2},{2,0},{4,6},{6,4},{8,10},{10,8},{12,14},{14,12},{16,18},{18,... | collective-permute-start | bytes 884744 | tf_op jit(solution)/shard_map/ppermute | solution.py:576
  48.8 0.0 collective-permute-start.12
  48.8 6.1 %collective-permute-done.11.refs_3_ = f32[576,128]{1,0:T(8,128)S(1)} collective-permute-done((f32[576,128]{1,0:T(8,128)S(1)}, f32[576,128]{1,0:T(8,128)S(1)}, u32[]{:S(2)}, u32[]{:S(2)}) %collective-permute-start.11) | collective-permute-done | bytes 294944 | tf_op jit(solution)/shard_map/ppermute | solution.py:576
  54.9 0.0 collective-permute-start.15
  54.9 3.0 %collective-permute-done.10.refs_2_ = f32[576,128]{1,0:T(8,128)S(1)} collective-permute-done((f32[576,128]{1,0:T(8,128)S(1)}, f32[576,128]{1,0:T(8,128)S(1)}, u32[]{:S(2)}, u32[]{:S(2)}) %collective-permute-start.10) | collective-permute-done | bytes 294944 | tf_op jit(solution)/shard_map/ppermute | solution.py:576
  57.9 0.0 collective-permute-start.14
  57.9 0.0 collective-permute-done.9.refs_1_
  57.9 0.5 collective-permute-start.13
  58.4 0.0 collective-permute-done.12.refs_4_
  58.4 0.0 collective-permute-done.15.refs_7_
  58.4 1.1 %collective-permute-done.14.refs_6_ = f32[576,128]{1,0:T(8,128)S(1)} collective-permute-done((f32[576,128]{1,0:T(8,128)S(1)}, f32[576,128]{1,0:T(8,128)S(1)}, u32[]{:S(2)}, u32[]{:S(2)}) %collective-permute-start.14) | collective-permute-done | bytes 294944 | tf_op jit(solution)/shard_map/ppermute | solution.py:608
  59.5 0.4 collective-permute-done.13.refs_5_
  59.9 0.0 copy-done
  59.9 34.6 %factor.1 = (f32[64,512]{1,0:T(8,128)}, f32[1,512]{1,0:T(1,128)}, f32[1,512]{1,0:T(1,128)}) custom-call(f32[576,128]{1,0:T(8,128)S(1)} %pad_maximum_fusion.refs_0_, f32[576,128]{1,0:T(8,128)S(1)} %collective-permute-done.9.refs_1_, f32[576,128]{1,0:T(8,128)S(1)} %collective-permute-done.10.refs_2_, f32[576,128]{1,0:T(8,128)S(1)} %collective-permute-done.11.refs_3_, ...), custom_call_target="tpu_custom_call" | custom-call | tf_op jit(solution)/shard_map/factor/pallas_call | solution.py:613
  (2 shorter events, 0.0 us)
Async XLA Ops:
  7.4 52.5 %copy-start = (f32[512,1024]{1,0:T(8,128)S(1)}, f32[512,1024]{1,0:T(8,128)}, u32[]{:S(2)}) copy-start(f32[512,1024]{1,0:T(8,128)} %refs_8_.1) | copy-start | bytes 6291460
  7.4 11.0 %collective-permute-start = (f32[576,128]{1,0:T(8,128)}, f32[576,128]{1,0:T(8,128)S(1)}, u32[]{:S(2)}, u32[]{:S(2)}) collective-permute-start(f32[576,128]{1,0:T(8,128)} %get-tuple-element.15), channel_id=1, source_target_pairs={{0,2},{2,0},{4,6},{6,4},{8,10},{10,8},{12,14},{14,12},{16,18},{18,... | collective-permute-start | bytes 884744 | tf_op jit(solution)/shard_map/ppermute | solution.py:576
  10.4 15.2 %collective-permute-start.1 = (f32[576,128]{1,0:T(8,128)}, f32[576,128]{1,0:T(8,128)S(1)}, u32[]{:S(2)}, u32[]{:S(2)}) collective-permute-start(f32[576,128]{1,0:T(8,128)} %get-tuple-element.16), channel_id=1, source_target_pairs={{0,4},{2,6},{4,0},{6,2},{8,12},{10,14},{12,8},{14,10},{16,20},{18,... | collective-permute-start | bytes 884744 | tf_op jit(solution)/shard_map/ppermute | solution.py:576
  11.9 13.7 %collective-permute-start.2 = (f32[576,128]{1,0:T(8,128)}, f32[576,128]{1,0:T(8,128)S(1)}, u32[]{:S(2)}, u32[]{:S(2)}) collective-permute-start(f32[576,128]{1,0:T(8,128)} %get-tuple-element.17), channel_id=1, source_target_pairs={{0,6},{2,4},{4,2},{6,0},{8,14},{10,12},{12,10},{14,8},{16,22},{18,... | collective-permute-start | bytes 884744 | tf_op jit(solution)/shard_map/ppermute | solution.py:576
  25.6 1.0 %copy-start.1 = (f32[576,128]{1,0:T(8,128)S(1)}, f32[576,128]{1,0:T(8,128)}, u32[]{:S(2)}) copy-start(f32[576,128]{1,0:T(8,128)} %get-tuple-element.14.refs_0_) | copy-start | bytes 884740
  26.6 5.1 %collective-permute-start.3 = (f32[144,128]{1,0:T(8,128)S(1)}, f32[144,128]{1,0:T(8,128)S(1)}, u32[]{:S(2)}, u32[]{:S(2)}) collective-permute-start(f32[144,128]{1,0:T(8,128)S(1)} %get-tuple-element.19), channel_id=1, source_target_pairs={{0,8},{2,10},{4,12},{6,14},{8,0},{10,2},{12,4},{14,6},{16,24},{18,... | collective-permute-start | bytes 221192 | tf_op jit(solution)/shard_map/ppermute | solution.py:576
  28.2 6.9 %collective-permute-start.4 = (f32[144,128]{1,0:T(8,128)S(1)}, f32[144,128]{1,0:T(8,128)S(1)}, u32[]{:S(2)}, u32[]{:S(2)}) collective-permute-start(f32[144,128]{1,0:T(8,128)S(1)} %get-tuple-element.20), channel_id=1, source_target_pairs={{0,16},{2,18},{4,20},{6,22},{8,24},{10,26},{12,28},{14,30},{16,0},... | collective-permute-start | bytes 221192 | tf_op jit(solution)/shard_map/ppermute | solution.py:576
  30.8 6.3 %collective-permute-start.5 = (f32[144,128]{1,0:T(8,128)S(1)}, f32[144,128]{1,0:T(8,128)S(1)}, u32[]{:S(2)}, u32[]{:S(2)}) collective-permute-start(f32[144,128]{1,0:T(8,128)S(1)} %get-tuple-element.21), channel_id=1, source_target_pairs={{0,24},{2,26},{4,28},{6,30},{8,16},{10,18},{12,20},{14,22},{16,8},... | collective-permute-start | bytes 221192 | tf_op jit(solution)/shard_map/ppermute | solution.py:576
  37.1 6.2 %collective-permute-start.8 = (f32[144,128]{1,0:T(8,128)S(1)}, f32[144,128]{1,0:T(8,128)S(1)}, u32[]{:S(2)}, u32[]{:S(2)}) collective-permute-start(f32[144,128]{1,0:T(8,128)S(1)} %partial_sums.3), channel_id=1, source_target_pairs={{0,24},{2,26},{4,28},{6,30},{8,16},{10,18},{12,20},{14,22},{16,8},... | collective-permute-start | bytes 221192 | tf_op jit(solution)/shard_map/ppermute | solution.py:576
  39.1 6.0 %collective-permute-start.7 = (f32[144,128]{1,0:T(8,128)S(1)}, f32[144,128]{1,0:T(8,128)S(1)}, u32[]{:S(2)}, u32[]{:S(2)}) collective-permute-start(f32[144,128]{1,0:T(8,128)S(1)} %partial_sums.3), channel_id=1, source_target_pairs={{0,16},{2,18},{4,20},{6,22},{8,24},{10,26},{12,28},{14,30},{16,0},... | collective-permute-start | bytes 221192 | tf_op jit(solution)/shard_map/ppermute | solution.py:576
  39.4 5.8 %collective-permute-start.6 = (f32[144,128]{1,0:T(8,128)S(1)}, f32[144,128]{1,0:T(8,128)S(1)}, u32[]{:S(2)}, u32[]{:S(2)}) collective-permute-start(f32[144,128]{1,0:T(8,128)S(1)} %partial_sums.3), channel_id=1, source_target_pairs={{0,8},{2,10},{4,12},{6,14},{8,0},{10,2},{12,4},{14,6},{16,24},{18,... | collective-permute-start | bytes 221192 | tf_op jit(solution)/shard_map/ppermute | solution.py:576
  45.2 9.7 %collective-permute-start.11 = (f32[576,128]{1,0:T(8,128)S(1)}, f32[576,128]{1,0:T(8,128)S(1)}, u32[]{:S(2)}, u32[]{:S(2)}) collective-permute-start(f32[576,128]{1,0:T(8,128)S(1)} %pad_maximum_fusion.refs_0_), channel_id=1, source_target_pairs={{0,6},{2,4},{4,2},{6,0},{8,14},{10,12},{12,10},{14,8},{16,22},{18,... | collective-permute-start | bytes 884744 | tf_op jit(solution)/shard_map/ppermute | solution.py:576
  46.7 11.2 %collective-permute-start.10 = (f32[576,128]{1,0:T(8,128)S(1)}, f32[576,128]{1,0:T(8,128)S(1)}, u32[]{:S(2)}, u32[]{:S(2)}) collective-permute-start(f32[576,128]{1,0:T(8,128)S(1)} %pad_maximum_fusion.refs_0_), channel_id=1, source_target_pairs={{0,4},{2,6},{4,0},{6,2},{8,12},{10,14},{12,8},{14,10},{16,20},{18,... | collective-permute-start | bytes 884744 | tf_op jit(solution)/shard_map/ppermute | solution.py:576
  47.6 10.3 %collective-permute-start.9 = (f32[576,128]{1,0:T(8,128)S(1)}, f32[576,128]{1,0:T(8,128)S(1)}, u32[]{:S(2)}, u32[]{:S(2)}) collective-permute-start(f32[576,128]{1,0:T(8,128)S(1)} %pad_maximum_fusion.refs_0_), channel_id=1, source_target_pairs={{0,2},{2,0},{4,6},{6,4},{8,10},{10,8},{12,14},{14,12},{16,18},{18,... | collective-permute-start | bytes 884744 | tf_op jit(solution)/shard_map/ppermute | solution.py:576
  48.8 9.6 %collective-permute-start.12 = (f32[576,128]{1,0:T(8,128)S(1)}, f32[576,128]{1,0:T(8,128)S(1)}, u32[]{:S(2)}, u32[]{:S(2)}) collective-permute-start(f32[576,128]{1,0:T(8,128)S(1)} %pad_maximum_fusion.refs_0_), channel_id=1, source_target_pairs={{0,1},{1,0},{2,3},{3,2},{4,5},{5,4},{6,7},{7,6},{8,9},{9,8},{10,11... | collective-permute-start | bytes 884744 | tf_op jit(solution)/shard_map/ppermute | solution.py:608
  54.9 3.5 %collective-permute-start.15 = (f32[576,128]{1,0:T(8,128)S(1)}, f32[576,128]{1,0:T(8,128)S(1)}, u32[]{:S(2)}, u32[]{:S(2)}) collective-permute-start(f32[576,128]{1,0:T(8,128)S(1)} %collective-permute-done.11.refs_3_), channel_id=1, source_target_pairs={{0,1},{1,0},{2,3},{3,2},{4,5},{5,4},{6,7},{7,6},{8,9},{9,8},{10,11... | collective-permute-start | bytes 884744 | tf_op jit(solution)/shard_map/ppermute | solution.py:608
  57.9 1.6 %collective-permute-start.14 = (f32[576,128]{1,0:T(8,128)S(1)}, f32[576,128]{1,0:T(8,128)S(1)}, u32[]{:S(2)}, u32[]{:S(2)}) collective-permute-start(f32[576,128]{1,0:T(8,128)S(1)} %collective-permute-done.10.refs_2_), channel_id=1, source_target_pairs={{0,1},{1,0},{2,3},{3,2},{4,5},{5,4},{6,7},{7,6},{8,9},{9,8},{10,11... | collective-permute-start | bytes 884744 | tf_op jit(solution)/shard_map/ppermute | solution.py:608
  57.9 2.0 %collective-permute-start.13 = (f32[576,128]{1,0:T(8,128)S(1)}, f32[576,128]{1,0:T(8,128)S(1)}, u32[]{:S(2)}, u32[]{:S(2)}) collective-permute-start(f32[576,128]{1,0:T(8,128)S(1)} %collective-permute-done.9.refs_1_), channel_id=1, source_target_pairs={{0,1},{1,0},{2,3},{3,2},{4,5},{5,4},{6,7},{7,6},{8,9},{9,8},{10,11... | collective-permute-start | bytes 884744 | tf_op jit(solution)/shard_map/ppermute | solution.py:608

commit v6 on v5

--- a/solution.py
+++ b/solution.py
@@ -308,11 +308,17 @@
         solved = row_ref[...]
         inv_ref[r0 : r0 + MIC, :] = jnp.where(lane < r0 + MIC, solved, 0.0)
         if r0 + MIC < BLK:
-            fix = dot3(split2(solved.T[r0 + MIC :, :]), split2(solved))
+            high, low_part = split2(solved)
+            fix = dot(
+                jnp.concatenate([high, high, low_part], axis=0),
+                jnp.concatenate([high, low_part, high], axis=0),
+                0,
+                0,
+            )
             lanes = lax.broadcasted_iota(jnp.int32, (BLK - r0 - MIC, BLK), 1)
             keep = (lanes < r0) | (lanes >= r0 + MIC)
             left = jnp.where(keep, d_ref[r0 + MIC :, :], 0.0)
-            d_ref[r0 + MIC :, :] = left - fix
+            d_ref[r0 + MIC :, :] = left - fix[r0 + MIC :, :]
     while queue:
         queue.pop(0)()
 
@@ -320,7 +326,7 @@
 def factor_kernel(plan, out_rows, width, *refs):
     n, nb = plan.state_total, plan.blocks
     slots = max(plan.fan(flow, 0) for flow in range(len(plan.orders)))
-    ins, (trans_hbm, r_ref, z_ref, x_ref, *scratch) = refs[: slots * plan.cols], refs[slots * plan.cols :]
+    ins, (trans_ref, r_ref, z_ref, x_ref, *scratch) = refs[: slots * plan.cols], refs[slots * plan.cols :]
     (
         packed,
         d_ref,
@@ -333,17 +339,13 @@
         turn_ref,
         next_ref,
         full_ref,
-        trans_ref,
         col_ref,
         root_ref,
         *state,
-        sems,
-        trans_sem,
     ) = scratch
     left, right, z_all = state[:2], state[2:4], state[4]
     me, core = lax.axis_index("rows"), lax.axis_index("cols")
 
-    copies = []
     for e in range(plan.cols):
         offsets = [0] * slots
         for flow in range(len(plan.orders)):
@@ -358,21 +360,12 @@
                         place = place * plan.radix[stage] + (plan.digit(me, stage) ^ (rest // size))
                         rest %= size
                     target = (core ^ e) * plan.half + plan.base(flow) + place * piece
-                    copies.append(
-                        pltpu.make_async_copy(
-                            ins[e * slots + d].at[pl.ds(offsets[d] + f * piece, piece), :],
-                            packed.at[pl.ds(pl.multiple_of(target, 8), piece), :],
-                            sems.at[len(copies)],
-                        )
-                    )
+                    at = offsets[d] + f * piece
+                    packed[pl.ds(pl.multiple_of(target, 8), piece), :] = ins[e * slots + d][
+                        at : at + piece, :
+                    ]
                 offsets[d] += inner * piece
-    trans_copy = pltpu.make_async_copy(trans_hbm, trans_ref, trans_sem)
-    for copy in copies:
-        copy.start()
-    trans_copy.start()
     full_ref[...] = jnp.zeros_like(full_ref)
-    for copy in copies:
-        copy.wait()
 
     row_id = lax.broadcasted_iota(jnp.int32, (BLK, BLK), 0)
     col_id = lax.broadcasted_iota(jnp.int32, (BLK, BLK), 1)
@@ -398,7 +391,6 @@
         scales.append(lax.rsqrt(diagonal))
         root_ref[k : k + 1, :] = diagonal * scales[k]
         col_ref[k] = turned(scales[k])
-    trans_copy.wait()
 
     def base(k, j):
         if j < nb:
@@ -534,7 +526,6 @@
     params = pltpu.CompilerParams(vmem_limit_bytes=VMEM_LIMIT)
     block_rows, bal_rows = whitening.shape[0], conductance.shape[0]
     depth = block_rows + bal_rows + BLK
-    anywhere = pl.BlockSpec(memory_space=pl.ANY)
     hbm = pl.BlockSpec(memory_space=pltpu.HBM)
     vmem = pl.BlockSpec(memory_space=pltpu.VMEM)
 
@@ -613,7 +604,7 @@
     r_post, z_post, x_next = pl.pallas_call(
         functools.partial(factor_kernel, plan, out_rows, width),
         out_shape=[typed(out_rows, width), typed(1, width), typed(1, width)],
-        in_specs=[anywhere] * (len(both) + 1),
+        in_specs=[vmem] * (len(both) + 1),
         out_specs=[vmem] * 3,
         scratch_shapes=[
             pltpu.VMEM((cols * plan.half, BLK), F32),
@@ -627,7 +618,6 @@
             pltpu.VMEM((BLK, BLK), F32),
             pltpu.VMEM((BLK, BLK), F32),
             pltpu.VMEM((n, n), F32),
-            pltpu.VMEM((width, n), F32),
             pltpu.VMEM((plan.blocks, BLK, BLK), F32),
             pltpu.VMEM((plan.blocks, BLK), F32),
             pltpu.VMEM((n, n), BF16),
@@ -635,8 +625,6 @@
             pltpu.VMEM((n, wide), BF16),
             pltpu.VMEM((n, wide), BF16),
             pltpu.VMEM((1, n), F32),
-            pltpu.SemaphoreType.DMA((rows * cols,)),
-            pltpu.SemaphoreType.DMA,
         ],
         compiler_params=params,
         name="factor",

time: 94.9 us -> 89 us (0.938)
  Pallas kernels: 41.4 us -> 35.7 us
    pallas_call x1, Pallas kernels: 34.6 us -> 28.7 us  [per_device(): pl.pallas_call(functools.partial(factor_kernel, plan, out_rows, width), o...]
where the time goes in v6:
time: 89 us; the launch traced here: 88.8 us
  Pallas kernels  35.7 us (40%)
  waiting for transfers between devices  33.9 us (38%)
  starting transfers between devices  17.5 us (20%)
  local copies, waits for them, and re-layouts  0.97 us (1%)
    ppermute x12, waiting for transfers between devices, exchange(): return lax.ppermute(block, 'rows', [(i, i ^ flip) for i in range(rows)])  32.4 us
    pallas_call x1, Pallas kernels, per_device(): pl.pallas_call(functools.partial(factor_kernel, plan, out_rows, width), o...  28.7 us
    ppermute x12, starting transfers between devices, exchange(): return lax.ppermute(block, 'rows', [(i, i ^ flip) for i in range(rows)])  17 us
    pallas_call x1, Pallas kernels, per_device(): pl.pallas_call(functools.partial(assemble_kernel, plan), out_shape=[typed...  6.91 us
  transfers between devices with their start and end apart: 16, of which 11 were waited for; matrix products, arithmetic and copies ran while one was open for 0% of the time, Pallas kernels for 0%

profile of v6, /device:TPU:0, one launch (start us, length us, event | category | flops | bytes accessed | tf_op | source)
XLA Modules:
  0.0 88.8 jit_solution(2744149814668510485)
XLA Ops:
  0.6 6.9 %assemble.1 = (f32[576,128]{1,0:T(8,128)}, f32[576,128]{1,0:T(8,128)}, f32[576,128]{1,0:T(8,128)}, f32[576,128]{1,0:T(8,128)}) custom-call(f32[384,384]{1,0:T(8,128)} %refs_0_.1, s32[4,384]{1,0:T(4,128)} %bitcast.9, f32[4,384]{1,0:T(4,128)} %bitcast.10, f32[3,128]{1,0:T(4,128)} %bitcast.11, s32[2,128]{1,0:T(2,128)} %bitcast.12, f32[1,128]{1,0:T(1,128)} %bitcast.13, ...), custom_call_target="tpu_custom_call" | custom-call | tf_op jit(solution)/shard_map/assemble/pallas_call | solution.py:546
  7.6 0.0 copy-start
  7.6 3.0 %collective-permute-start = (f32[576,128]{1,0:T(8,128)}, f32[576,128]{1,0:T(8,128)S(1)}, u32[]{:S(2)}, u32[]{:S(2)}) collective-permute-start(f32[576,128]{1,0:T(8,128)} %get-tuple-element.15), channel_id=1, source_target_pairs={{0,2},{2,0},{4,6},{6,4},{8,10},{10,8},{12,14},{14,12},{16,18},{18,... | collective-permute-start | bytes 884744 | tf_op jit(solution)/shard_map/ppermute | solution.py:567
  10.6 1.5 %collective-permute-start.1 = (f32[576,128]{1,0:T(8,128)}, f32[576,128]{1,0:T(8,128)S(1)}, u32[]{:S(2)}, u32[]{:S(2)}) collective-permute-start(f32[576,128]{1,0:T(8,128)} %get-tuple-element.16), channel_id=1, source_target_pairs={{0,4},{2,6},{4,0},{6,2},{8,12},{10,14},{12,8},{14,10},{16,20},{18,... | collective-permute-start | bytes 884744 | tf_op jit(solution)/shard_map/ppermute | solution.py:567
  12.1 0.0 collective-permute-start.2
  12.1 6.5 %collective-permute-done.refs_1_ = f32[576,128]{1,0:T(8,128)S(1)} collective-permute-done((f32[576,128]{1,0:T(8,128)}, f32[576,128]{1,0:T(8,128)S(1)}, u32[]{:S(2)}, u32[]{:S(2)}) %collective-permute-start) | collective-permute-done | bytes 294944 | tf_op jit(solution)/shard_map/ppermute | solution.py:567
  18.6 7.2 %collective-permute-done.1.refs_2_ = f32[576,128]{1,0:T(8,128)S(1)} collective-permute-done((f32[576,128]{1,0:T(8,128)}, f32[576,128]{1,0:T(8,128)S(1)}, u32[]{:S(2)}, u32[]{:S(2)}) %collective-permute-start.1) | collective-permute-done | bytes 294944 | tf_op jit(solution)/shard_map/ppermute | solution.py:567
  25.7 0.0 collective-permute-done.2.refs_3_
  25.7 0.0 copy-start.1
  25.8 1.0 %copy-done.1 = f32[576,128]{1,0:T(8,128)S(1)} copy-done((f32[576,128]{1,0:T(8,128)S(1)}, f32[576,128]{1,0:T(8,128)}, u32[]{:S(2)}) %copy-start.1) | copy-done | bytes 294936
  26.7 0.1 partial_sums.2
  26.8 1.6 %collective-permute-start.3 = (f32[144,128]{1,0:T(8,128)S(1)}, f32[144,128]{1,0:T(8,128)S(1)}, u32[]{:S(2)}, u32[]{:S(2)}) collective-permute-start(f32[144,128]{1,0:T(8,128)S(1)} %get-tuple-element.19), channel_id=1, source_target_pairs={{0,8},{2,10},{4,12},{6,14},{8,0},{10,2},{12,4},{14,6},{16,24},{18,... | collective-permute-start | bytes 221192 | tf_op jit(solution)/shard_map/ppermute | solution.py:567
  28.4 2.6 %collective-permute-start.4 = (f32[144,128]{1,0:T(8,128)S(1)}, f32[144,128]{1,0:T(8,128)S(1)}, u32[]{:S(2)}, u32[]{:S(2)}) collective-permute-start(f32[144,128]{1,0:T(8,128)S(1)} %get-tuple-element.20), channel_id=1, source_target_pairs={{0,16},{2,18},{4,20},{6,22},{8,24},{10,26},{12,28},{14,30},{16,0},... | collective-permute-start | bytes 221192 | tf_op jit(solution)/shard_map/ppermute | solution.py:567
  31.0 0.2 collective-permute-start.5
  31.2 0.7 collective-permute-done.3.refs_1_
  31.9 3.4 %collective-permute-done.4.refs_2_ = f32[144,128]{1,0:T(8,128)S(1)} collective-permute-done((f32[144,128]{1,0:T(8,128)S(1)}, f32[144,128]{1,0:T(8,128)S(1)}, u32[]{:S(2)}, u32[]{:S(2)}) %collective-permute-start.4) | collective-permute-done | bytes 73760 | tf_op jit(solution)/shard_map/ppermute | solution.py:567
  35.3 1.9 %collective-permute-done.5.refs_3_ = f32[144,128]{1,0:T(8,128)S(1)} collective-permute-done((f32[144,128]{1,0:T(8,128)S(1)}, f32[144,128]{1,0:T(8,128)S(1)}, u32[]{:S(2)}, u32[]{:S(2)}) %collective-permute-start.5) | collective-permute-done | bytes 73760 | tf_op jit(solution)/shard_map/ppermute | solution.py:567
  37.3 2.0 %collective-permute-start.8 = (f32[144,128]{1,0:T(8,128)S(1)}, f32[144,128]{1,0:T(8,128)S(1)}, u32[]{:S(2)}, u32[]{:S(2)}) collective-permute-start(f32[144,128]{1,0:T(8,128)S(1)} %partial_sums.3), channel_id=1, source_target_pairs={{0,24},{2,26},{4,28},{6,30},{8,16},{10,18},{12,20},{14,22},{16,8},... | collective-permute-start | bytes 221192 | tf_op jit(solution)/shard_map/ppermute | solution.py:567
  39.3 0.2 collective-permute-start.7
  39.6 2.2 %collective-permute-start.6 = (f32[144,128]{1,0:T(8,128)S(1)}, f32[144,128]{1,0:T(8,128)S(1)}, u32[]{:S(2)}, u32[]{:S(2)}) collective-permute-start(f32[144,128]{1,0:T(8,128)S(1)} %partial_sums.3), channel_id=1, source_target_pairs={{0,8},{2,10},{4,12},{6,14},{8,0},{10,2},{12,4},{14,6},{16,24},{18,... | collective-permute-start | bytes 221192 | tf_op jit(solution)/shard_map/ppermute | solution.py:567
  41.7 1.8 %collective-permute-done.8 = f32[144,128]{1,0:T(8,128)S(1)} collective-permute-done((f32[144,128]{1,0:T(8,128)S(1)}, f32[144,128]{1,0:T(8,128)S(1)}, u32[]{:S(2)}, u32[]{:S(2)}) %collective-permute-start.8) | collective-permute-done | bytes 73760 | tf_op jit(solution)/shard_map/ppermute | solution.py:567
  43.5 1.8 %collective-permute-done.7 = f32[144,128]{1,0:T(8,128)S(1)} collective-permute-done((f32[144,128]{1,0:T(8,128)S(1)}, f32[144,128]{1,0:T(8,128)S(1)}, u32[]{:S(2)}, u32[]{:S(2)}) %collective-permute-start.7) | collective-permute-done | bytes 73760 | tf_op jit(solution)/shard_map/ppermute | solution.py:567
  45.4 0.0 collective-permute-done.6
  45.4 1.4 %collective-permute-start.11 = (f32[576,128]{1,0:T(8,128)S(1)}, f32[576,128]{1,0:T(8,128)S(1)}, u32[]{:S(2)}, u32[]{:S(2)}) collective-permute-start(f32[576,128]{1,0:T(8,128)S(1)} %pad_maximum_fusion.refs_0_), channel_id=1, source_target_pairs={{0,6},{2,4},{4,2},{6,0},{8,14},{10,12},{12,10},{14,8},{16,22},{18,... | collective-permute-start | bytes 884744 | tf_op jit(solution)/shard_map/ppermute | solution.py:567
  46.8 0.9 %collective-permute-start.10 = (f32[576,128]{1,0:T(8,128)S(1)}, f32[576,128]{1,0:T(8,128)S(1)}, u32[]{:S(2)}, u32[]{:S(2)}) collective-permute-start(f32[576,128]{1,0:T(8,128)S(1)} %pad_maximum_fusion.refs_0_), channel_id=1, source_target_pairs={{0,4},{2,6},{4,0},{6,2},{8,12},{10,14},{12,8},{14,10},{16,20},{18,... | collective-permute-start | bytes 884744 | tf_op jit(solution)/shard_map/ppermute | solution.py:567
  47.8 1.2 %collective-permute-start.9 = (f32[576,128]{1,0:T(8,128)S(1)}, f32[576,128]{1,0:T(8,128)S(1)}, u32[]{:S(2)}, u32[]{:S(2)}) collective-permute-start(f32[576,128]{1,0:T(8,128)S(1)} %pad_maximum_fusion.refs_0_), channel_id=1, source_target_pairs={{0,2},{2,0},{4,6},{6,4},{8,10},{10,8},{12,14},{14,12},{16,18},{18,... | collective-permute-start | bytes 884744 | tf_op jit(solution)/shard_map/ppermute | solution.py:567
  49.0 0.0 collective-permute-start.12
  49.0 6.1 %collective-permute-done.11.refs_3_ = f32[576,128]{1,0:T(8,128)S(1)} collective-permute-done((f32[576,128]{1,0:T(8,128)S(1)}, f32[576,128]{1,0:T(8,128)S(1)}, u32[]{:S(2)}, u32[]{:S(2)}) %collective-permute-start.11) | collective-permute-done | bytes 294944 | tf_op jit(solution)/shard_map/ppermute | solution.py:567
  55.1 0.0 collective-permute-start.15
  55.1 3.0 %collective-permute-done.10.refs_2_ = f32[576,128]{1,0:T(8,128)S(1)} collective-permute-done((f32[576,128]{1,0:T(8,128)S(1)}, f32[576,128]{1,0:T(8,128)S(1)}, u32[]{:S(2)}, u32[]{:S(2)}) %collective-permute-start.10) | collective-permute-done | bytes 294944 | tf_op jit(solution)/shard_map/ppermute | solution.py:567
  58.1 0.0 collective-permute-start.14
  58.1 0.0 collective-permute-done.9.refs_1_
  58.1 0.5 collective-permute-start.13
  58.6 0.0 collective-permute-done.12.refs_4_
  58.6 0.0 collective-permute-done.15.refs_7_
  58.6 1.1 %collective-permute-done.14.refs_6_ = f32[576,128]{1,0:T(8,128)S(1)} collective-permute-done((f32[576,128]{1,0:T(8,128)S(1)}, f32[576,128]{1,0:T(8,128)S(1)}, u32[]{:S(2)}, u32[]{:S(2)}) %collective-permute-start.14) | collective-permute-done | bytes 294944 | tf_op jit(solution)/shard_map/ppermute | solution.py:599
  59.7 0.4 collective-permute-done.13.refs_5_
  60.1 0.0 copy-done
  60.1 28.7 %factor.1 = (f32[64,512]{1,0:T(8,128)}, f32[1,512]{1,0:T(1,128)}, f32[1,512]{1,0:T(1,128)}) custom-call(f32[576,128]{1,0:T(8,128)S(1)} %pad_maximum_fusion.refs_0_, f32[576,128]{1,0:T(8,128)S(1)} %collective-permute-done.9.refs_1_, f32[576,128]{1,0:T(8,128)S(1)} %collective-permute-done.10.refs_2_, f32[576,128]{1,0:T(8,128)S(1)} %collective-permute-done.11.refs_3_, ...), custom_call_target="tpu_custom_call" | custom-call | tf_op jit(solution)/shard_map/factor/pallas_call | solution.py:604
  (2 shorter events, 0.0 us)
Async XLA Ops:
  7.6 52.5 %copy-start = (f32[512,1024]{1,0:T(8,128)S(1)}, f32[512,1024]{1,0:T(8,128)}, u32[]{:S(2)}) copy-start(f32[512,1024]{1,0:T(8,128)} %refs_8_.1) | copy-start | bytes 6291460
  7.6 11.0 %collective-permute-start = (f32[576,128]{1,0:T(8,128)}, f32[576,128]{1,0:T(8,128)S(1)}, u32[]{:S(2)}, u32[]{:S(2)}) collective-permute-start(f32[576,128]{1,0:T(8,128)} %get-tuple-element.15), channel_id=1, source_target_pairs={{0,2},{2,0},{4,6},{6,4},{8,10},{10,8},{12,14},{14,12},{16,18},{18,... | collective-permute-start | bytes 884744 | tf_op jit(solution)/shard_map/ppermute | solution.py:567
  10.6 15.2 %collective-permute-start.1 = (f32[576,128]{1,0:T(8,128)}, f32[576,128]{1,0:T(8,128)S(1)}, u32[]{:S(2)}, u32[]{:S(2)}) collective-permute-start(f32[576,128]{1,0:T(8,128)} %get-tuple-element.16), channel_id=1, source_target_pairs={{0,4},{2,6},{4,0},{6,2},{8,12},{10,14},{12,8},{14,10},{16,20},{18,... | collective-permute-start | bytes 884744 | tf_op jit(solution)/shard_map/ppermute | solution.py:567
  12.1 13.7 %collective-permute-start.2 = (f32[576,128]{1,0:T(8,128)}, f32[576,128]{1,0:T(8,128)S(1)}, u32[]{:S(2)}, u32[]{:S(2)}) collective-permute-start(f32[576,128]{1,0:T(8,128)} %get-tuple-element.17), channel_id=1, source_target_pairs={{0,6},{2,4},{4,2},{6,0},{8,14},{10,12},{12,10},{14,8},{16,22},{18,... | collective-permute-start | bytes 884744 | tf_op jit(solution)/shard_map/ppermute | solution.py:567
  25.7 1.0 %copy-start.1 = (f32[576,128]{1,0:T(8,128)S(1)}, f32[576,128]{1,0:T(8,128)}, u32[]{:S(2)}) copy-start(f32[576,128]{1,0:T(8,128)} %get-tuple-element.14.refs_0_) | copy-start | bytes 884740
  26.8 5.1 %collective-permute-start.3 = (f32[144,128]{1,0:T(8,128)S(1)}, f32[144,128]{1,0:T(8,128)S(1)}, u32[]{:S(2)}, u32[]{:S(2)}) collective-permute-start(f32[144,128]{1,0:T(8,128)S(1)} %get-tuple-element.19), channel_id=1, source_target_pairs={{0,8},{2,10},{4,12},{6,14},{8,0},{10,2},{12,4},{14,6},{16,24},{18,... | collective-permute-start | bytes 221192 | tf_op jit(solution)/shard_map/ppermute | solution.py:567
  28.4 6.9 %collective-permute-start.4 = (f32[144,128]{1,0:T(8,128)S(1)}, f32[144,128]{1,0:T(8,128)S(1)}, u32[]{:S(2)}, u32[]{:S(2)}) collective-permute-start(f32[144,128]{1,0:T(8,128)S(1)} %get-tuple-element.20), channel_id=1, source_target_pairs={{0,16},{2,18},{4,20},{6,22},{8,24},{10,26},{12,28},{14,30},{16,0},... | collective-permute-start | bytes 221192 | tf_op jit(solution)/shard_map/ppermute | solution.py:567
  31.0 6.3 %collective-permute-start.5 = (f32[144,128]{1,0:T(8,128)S(1)}, f32[144,128]{1,0:T(8,128)S(1)}, u32[]{:S(2)}, u32[]{:S(2)}) collective-permute-start(f32[144,128]{1,0:T(8,128)S(1)} %get-tuple-element.21), channel_id=1, source_target_pairs={{0,24},{2,26},{4,28},{6,30},{8,16},{10,18},{12,20},{14,22},{16,8},... | collective-permute-start | bytes 221192 | tf_op jit(solution)/shard_map/ppermute | solution.py:567
  37.3 6.2 %collective-permute-start.8 = (f32[144,128]{1,0:T(8,128)S(1)}, f32[144,128]{1,0:T(8,128)S(1)}, u32[]{:S(2)}, u32[]{:S(2)}) collective-permute-start(f32[144,128]{1,0:T(8,128)S(1)} %partial_sums.3), channel_id=1, source_target_pairs={{0,24},{2,26},{4,28},{6,30},{8,16},{10,18},{12,20},{14,22},{16,8},... | collective-permute-start | bytes 221192 | tf_op jit(solution)/shard_map/ppermute | solution.py:567
  39.3 6.0 %collective-permute-start.7 = (f32[144,128]{1,0:T(8,128)S(1)}, f32[144,128]{1,0:T(8,128)S(1)}, u32[]{:S(2)}, u32[]{:S(2)}) collective-permute-start(f32[144,128]{1,0:T(8,128)S(1)} %partial_sums.3), channel_id=1, source_target_pairs={{0,16},{2,18},{4,20},{6,22},{8,24},{10,26},{12,28},{14,30},{16,0},... | collective-permute-start | bytes 221192 | tf_op jit(solution)/shard_map/ppermute | solution.py:567
  39.6 5.8 %collective-permute-start.6 = (f32[144,128]{1,0:T(8,128)S(1)}, f32[144,128]{1,0:T(8,128)S(1)}, u32[]{:S(2)}, u32[]{:S(2)}) collective-permute-start(f32[144,128]{1,0:T(8,128)S(1)} %partial_sums.3), channel_id=1, source_target_pairs={{0,8},{2,10},{4,12},{6,14},{8,0},{10,2},{12,4},{14,6},{16,24},{18,... | collective-permute-start | bytes 221192 | tf_op jit(solution)/shard_map/ppermute | solution.py:567
  45.4 9.7 %collective-permute-start.11 = (f32[576,128]{1,0:T(8,128)S(1)}, f32[576,128]{1,0:T(8,128)S(1)}, u32[]{:S(2)}, u32[]{:S(2)}) collective-permute-start(f32[576,128]{1,0:T(8,128)S(1)} %pad_maximum_fusion.refs_0_), channel_id=1, source_target_pairs={{0,6},{2,4},{4,2},{6,0},{8,14},{10,12},{12,10},{14,8},{16,22},{18,... | collective-permute-start | bytes 884744 | tf_op jit(solution)/shard_map/ppermute | solution.py:567
  46.8 11.3 %collective-permute-start.10 = (f32[576,128]{1,0:T(8,128)S(1)}, f32[576,128]{1,0:T(8,128)S(1)}, u32[]{:S(2)}, u32[]{:S(2)}) collective-permute-start(f32[576,128]{1,0:T(8,128)S(1)} %pad_maximum_fusion.refs_0_), channel_id=1, source_target_pairs={{0,4},{2,6},{4,0},{6,2},{8,12},{10,14},{12,8},{14,10},{16,20},{18,... | collective-permute-start | bytes 884744 | tf_op jit(solution)/shard_map/ppermute | solution.py:567
  47.8 10.3 %collective-permute-start.9 = (f32[576,128]{1,0:T(8,128)S(1)}, f32[576,128]{1,0:T(8,128)S(1)}, u32[]{:S(2)}, u32[]{:S(2)}) collective-permute-start(f32[576,128]{1,0:T(8,128)S(1)} %pad_maximum_fusion.refs_0_), channel_id=1, source_target_pairs={{0,2},{2,0},{4,6},{6,4},{8,10},{10,8},{12,14},{14,12},{16,18},{18,... | collective-permute-start | bytes 884744 | tf_op jit(solution)/shard_map/ppermute | solution.py:567
  49.0 9.7 %collective-permute-start.12 = (f32[576,128]{1,0:T(8,128)S(1)}, f32[576,128]{1,0:T(8,128)S(1)}, u32[]{:S(2)}, u32[]{:S(2)}) collective-permute-start(f32[576,128]{1,0:T(8,128)S(1)} %pad_maximum_fusion.refs_0_), channel_id=1, source_target_pairs={{0,1},{1,0},{2,3},{3,2},{4,5},{5,4},{6,7},{7,6},{8,9},{9,8},{10,11... | collective-permute-start | bytes 884744 | tf_op jit(solution)/shard_map/ppermute | solution.py:599
  55.1 3.5 %collective-permute-start.15 = (f32[576,128]{1,0:T(8,128)S(1)}, f32[576,128]{1,0:T(8,128)S(1)}, u32[]{:S(2)}, u32[]{:S(2)}) collective-permute-start(f32[576,128]{1,0:T(8,128)S(1)} %collective-permute-done.11.refs_3_), channel_id=1, source_target_pairs={{0,1},{1,0},{2,3},{3,2},{4,5},{5,4},{6,7},{7,6},{8,9},{9,8},{10,11... | collective-permute-start | bytes 884744 | tf_op jit(solution)/shard_map/ppermute | solution.py:599
  58.1 1.6 %collective-permute-start.14 = (f32[576,128]{1,0:T(8,128)S(1)}, f32[576,128]{1,0:T(8,128)S(1)}, u32[]{:S(2)}, u32[]{:S(2)}) collective-permute-start(f32[576,128]{1,0:T(8,128)S(1)} %collective-permute-done.10.refs_2_), channel_id=1, source_target_pairs={{0,1},{1,0},{2,3},{3,2},{4,5},{5,4},{6,7},{7,6},{8,9},{9,8},{10,11... | collective-permute-start | bytes 884744 | tf_op jit(solution)/shard_map/ppermute | solution.py:599
  58.1 2.0 %collective-permute-start.13 = (f32[576,128]{1,0:T(8,128)S(1)}, f32[576,128]{1,0:T(8,128)S(1)}, u32[]{:S(2)}, u32[]{:S(2)}) collective-permute-start(f32[576,128]{1,0:T(8,128)S(1)} %collective-permute-done.9.refs_1_), channel_id=1, source_target_pairs={{0,1},{1,0},{2,3},{3,2},{4,5},{5,4},{6,7},{7,6},{8,9},{9,8},{10,11... | collective-permute-start | bytes 884744 | tf_op jit(solution)/shard_map/ppermute | solution.py:599

commit v7 on v6

--- a/solution.py
+++ b/solution.py
@@ -54,19 +54,22 @@
             step *= f
         stages = list(range(len(self.radix)))
         self.orders = (stages,)
-        tiles = [(i, j) for i in range(nb) for j in range(i, nb)]
+        tiles = [(i, j) for i in range(nb) for j in range(i, nb) if i != j or i % 2 == 0]
         share = -(-len(tiles) // cols)
-        piece = -(-share * BLK // (8 * rows)) * 8
+        self.extra = share * BLK
+        piece = -(-(self.extra + nb + nb // 2) // (8 * rows)) * 8
         self.pieces = (piece,)
         self.half = rows * piece
         self.local = {}
         for index, tile in enumerate(tiles):
             self.local[tile] = (index // share, index % share * BLK)
-        self.moment_rows = state_total // 64
 
     def tile(self, i, j):
         core, row = self.local[i, j]
         return core * self.half + row
+
+    def diagonal_row(self, k):
+        return self.local[k - 1, k - 1][0] * self.half + self.extra + self.blocks + k // 2
 
     def digit(self, index, stage):
         return lax.rem(index // self.stride[stage], self.radix[stage])
@@ -119,11 +122,9 @@
         return jnp.where(top, jnp.broadcast_to(row, (head, row.shape[1])), 0.0)
 
     prior_pad[...] = jnp.zeros_like(prior_pad)
-    used = max(row for _, row in plan.local.values()) + BLK
-    if used < plan.half:
-        packed[used:, :] = jnp.zeros((plan.half - used, BLK), F32)
-    for copy in copies:
-        copy.wait()
+    packed[plan.extra :, :] = jnp.zeros((plan.half - plan.extra, BLK), F32)
+    for index in (1, 2, 3):
+        copies[index].wait()
 
     readings = jnp.concatenate(
         [readings_ref[k : k + 1, :] for k in range(readings_ref.shape[0])], axis=1
@@ -135,12 +136,15 @@
         for k in range(states_ref.shape[0]):
             summed = summed + jnp.where(ids == states_ref[k : k + 1, :], coeffs_ref[k : k + 1, :], 0.0)
         put(sens_hi, sens_lo, head + at, 0, summed)
+    copies[0].wait()
     white = split2(white_ref[...])
     whitened = dot3((sens_hi[...], sens_lo[...]), white, 1, 1)
     for at in range(0, n + head, step):
         size = min(step, n + head - at)
         put(at_hi, at_lo, at, 0, whitened[at : at + size, :])
 
+    for copy in copies[4:]:
+        copy.wait()
     conductance = conductance_ref[...]
     put(at_hi, at_lo, 0, block_rows, head_rows(conductance * balance_rhs_ref[...]))
     for at in range(0, n, step):
@@ -158,26 +162,40 @@
 
     me, core = lax.axis_index("rows"), lax.axis_index("cols")
 
+    row_id = lax.broadcasted_iota(jnp.int32, (BLK, BLK), 0)
+    col_id = lax.broadcasted_iota(jnp.int32, (BLK, BLK), 1)
+
     def tiles_of(part):
-        moments = []
         for at in range(0, plan.blocks, 2):
             wanted = [(i, j) for (i, j), (c, _) in plan.local.items() if c == part and j // 2 == at // 2]
             if not wanted:
                 continue
-            low, high = min(i for i, _ in wanted), max(i for i, _ in wanted) + 1
+            low = min(i for i, _ in wanted)
+            high = max(i + (i == j) for i, j in wanted) + 1
             top = head + low * BLK if low else 0
             rows = slice(top, head + high * BLK)
             cols = slice(head + at * BLK, head + (at + 2) * BLK)
             out = dot3((at_hi[rows, :], at_lo[rows, :]), (at_hi[cols, :], at_lo[cols, :]), 1, 1)
-            if not low:
-                moments += [out[0:1, k * 64 : k * 64 + 64] for k in range(2 * BLK // 64)]
+
+            def piece_of(i, j):
+                where, col = head + i * BLK - top, (j - at) * BLK
+                return out[where : where + BLK, col : col + BLK]
+
+            if part == 0:
+                for j in (at, at + 1):
+                    col = (j - at) * BLK
+                    packed[plan.extra + j : plan.extra + j + 1, :] = out[0:1, col : col + BLK]
             for i, j in wanted:
-                row, col = plan.local[i, j][1], (j - at) * BLK
-                where = head + i * BLK - top
-                packed[row : row + BLK, :] = out[where : where + BLK, col : col + BLK]
-        for k, value in enumerate(moments):
-            row = plan.local[0, 0][1] + BLK - plan.moment_rows + k
-            packed[row : row + 1, 0:64] = value
+                row = plan.local[i, j][1]
+                value = piece_of(i, j)
+                if i == j:
+                    second = piece_of(i + 1, j + 1)
+                    spare = plan.extra + plan.blocks + i // 2
+                    packed[spare : spare + 1, :] = jnp.sum(
+                        jnp.where(row_id == col_id, second, 0.0), axis=0, keepdims=True
+                    )
+                    value = jnp.where(col_id >= row_id, value, second)
+                packed[row : row + BLK, :] = value
 
     for part in range(plan.cols):
         pl.when(core == part)(functools.partial(tiles_of, part))
@@ -340,6 +358,7 @@
         next_ref,
         full_ref,
         col_ref,
+        diag_ref,
         root_ref,
         *state,
     ) = scratch
@@ -373,26 +392,26 @@
     def turned(row):
         return jnp.broadcast_to(row, (BLK, BLK)).T
 
-    corner = plan.tile(0, 0)
-    tile = packed[corner : corner + BLK, :]
-    hidden = (row_id >= BLK - plan.moment_rows) & (col_id < 64)
-    moments = []
-    for k in range(nb):
-        at = BLK - plan.moment_rows + 2 * k
-        moments.append(jnp.concatenate([tile[at : at + 1, 0:64], tile[at + 1 : at + 2, 0:64]], axis=1))
-    packed[corner : corner + BLK, :] = jnp.where(hidden, tile.T, tile)
+    moments = [packed[plan.extra + k : plan.extra + k + 1, :] for k in range(nb)]
 
     scales = []
-    for k in range(nb):
-        row = plan.tile(k, k)
-        diagonal = jnp.sum(
-            jnp.where(row_id == col_id, packed[row : row + BLK, :], 0.0), axis=0, keepdims=True
-        )
-        scales.append(lax.rsqrt(diagonal))
-        root_ref[k : k + 1, :] = diagonal * scales[k]
-        col_ref[k] = turned(scales[k])
+    for k in range(0, nb, 2):
+        row, spare = plan.tile(k, k), plan.diagonal_row(k + 1)
+        both = packed[row : row + BLK, :]
+        mirror = both.T
+        second = packed[spare : spare + 1, :]
+        diag_ref[k] = jnp.where(col_id >= row_id, both, mirror)
+        lower = jnp.where(col_id < row_id, both, mirror)
+        diag_ref[k + 1] = jnp.where(col_id == row_id, jnp.broadcast_to(second, (BLK, BLK)), lower)
+        first = jnp.sum(jnp.where(row_id == col_id, both, 0.0), axis=0, keepdims=True)
+        for at, diagonal in ((k, first), (k + 1, second)):
+            scales.append(lax.rsqrt(diagonal))
+            root_ref[at : at + 1, :] = diagonal * scales[at]
+            col_ref[at] = turned(scales[at])
 
     def base(k, j):
+        if j == k:
+            return diag_ref[k] * col_ref[k] * scales[k]
         if j < nb:
             row = plan.tile(k, j)
             return packed[row : row + BLK, :] * col_ref[k] * scales[j]
@@ -619,6 +638,7 @@
             pltpu.VMEM((BLK, BLK), F32),
             pltpu.VMEM((n, n), F32),
             pltpu.VMEM((plan.blocks, BLK, BLK), F32),
+            pltpu.VMEM((plan.blocks, BLK, BLK), F32),
             pltpu.VMEM((plan.blocks, BLK), F32),
             pltpu.VMEM((n, n), BF16),
             pltpu.VMEM((n, n), BF16),

time: 89 us -> 89.3 us (level)
  waiting for transfers between devices: 33.9 us -> 32.2 us
  local copies, waits for them, and re-layouts: 0.97 us -> 2.55 us
    ppermute x12, waiting for transfers between devices: 32.4 us -> 30.7 us  [exchange(): return lax.ppermute(block, 'rows', [(i, i ^ flip) for i in range(rows)])]
    unnamed x4, local copies, waits for them, and re-layouts: 0.97 us -> 2.55 us
where the time goes in v7:
time: 89.3 us; the launch traced here: 89.1 us
  Pallas kernels  36.2 us (41%)
  waiting for transfers between devices  32.2 us (36%)
  starting transfers between devices  17.5 us (20%)
  local copies, waits for them, and re-layouts  2.55 us (3%)
    ppermute x12, waiting for transfers between devices, exchange(): return lax.ppermute(block, 'rows', [(i, i ^ flip) for i in range(rows)])  30.7 us
    pallas_call x1, Pallas kernels, per_device(): pl.pallas_call(functools.partial(factor_kernel, plan, out_rows, width), o...  29 us
    ppermute x12, starting transfers between devices, exchange(): return lax.ppermute(block, 'rows', [(i, i ^ flip) for i in range(rows)])  17 us
    pallas_call x1, Pallas kernels, per_device(): pl.pallas_call(functools.partial(assemble_kernel, plan), out_shape=[typed...  7.08 us
    unnamed x4, local copies, waits for them, and re-layouts  2.55 us
  transfers between devices with their start and end apart: 16, of which 11 were waited for; matrix products, arithmetic and copies ran while one was open for 0% of the time, Pallas kernels for 0%

profile of v7, /device:TPU:0, one launch (start us, length us, event | category | flops | bytes accessed | tf_op | source)
XLA Modules:
  0.0 89.1 jit_solution(5704718292930153818)
XLA Ops:
  0.6 7.1 %assemble.1 = (f32[544,128]{1,0:T(8,128)}, f32[544,128]{1,0:T(8,128)}, f32[544,128]{1,0:T(8,128)}, f32[544,128]{1,0:T(8,128)}) custom-call(f32[384,384]{1,0:T(8,128)} %refs_0_.1, s32[4,384]{1,0:T(4,128)} %bitcast.9, f32[4,384]{1,0:T(4,128)} %bitcast.10, f32[3,128]{1,0:T(4,128)} %bitcast.11, s32[2,128]{1,0:T(2,128)} %bitcast.12, f32[1,128]{1,0:T(1,128)} %bitcast.13, ...), custom_call_target="tpu_custom_call" | custom-call | tf_op jit(solution)/shard_map/assemble/pallas_call | solution.py:565
  7.7 3.0 %collective-permute-start = (f32[544,128]{1,0:T(8,128)}, f32[544,128]{1,0:T(8,128)S(1)}, u32[]{:S(2)}, u32[]{:S(2)}) collective-permute-start(f32[544,128]{1,0:T(8,128)} %get-tuple-element.15), channel_id=1, source_target_pairs={{0,2},{2,0},{4,6},{6,4},{8,10},{10,8},{12,14},{14,12},{16,18},{18,... | collective-permute-start | bytes 835592 | tf_op jit(solution)/shard_map/ppermute | solution.py:586
  10.7 1.5 %collective-permute-start.1 = (f32[544,128]{1,0:T(8,128)}, f32[544,128]{1,0:T(8,128)S(1)}, u32[]{:S(2)}, u32[]{:S(2)}) collective-permute-start(f32[544,128]{1,0:T(8,128)} %get-tuple-element.16), channel_id=1, source_target_pairs={{0,4},{2,6},{4,0},{6,2},{8,12},{10,14},{12,8},{14,10},{16,20},{18,... | collective-permute-start | bytes 835592 | tf_op jit(solution)/shard_map/ppermute | solution.py:586
  12.2 0.0 collective-permute-start.2
  12.3 6.2 %collective-permute-done.refs_1_ = f32[544,128]{1,0:T(8,128)S(1)} collective-permute-done((f32[544,128]{1,0:T(8,128)}, f32[544,128]{1,0:T(8,128)S(1)}, u32[]{:S(2)}, u32[]{:S(2)}) %collective-permute-start) | collective-permute-done | bytes 278560 | tf_op jit(solution)/shard_map/ppermute | solution.py:586
  18.4 6.5 %collective-permute-done.1.refs_2_ = f32[544,128]{1,0:T(8,128)S(1)} collective-permute-done((f32[544,128]{1,0:T(8,128)}, f32[544,128]{1,0:T(8,128)S(1)}, u32[]{:S(2)}, u32[]{:S(2)}) %collective-permute-start.1) | collective-permute-done | bytes 278560 | tf_op jit(solution)/shard_map/ppermute | solution.py:586
  25.0 0.0 collective-permute-done.2.refs_3_
  25.0 0.0 copy-start.1
  25.0 1.0 %copy-done.1 = f32[544,128]{1,0:T(8,128)S(1)} copy-done((f32[544,128]{1,0:T(8,128)S(1)}, f32[544,128]{1,0:T(8,128)}, u32[]{:S(2)}) %copy-start.1) | copy-done | bytes 278552
  25.9 0.1 partial_sums.2
  26.0 1.6 %collective-permute-start.3 = (f32[136,128]{1,0:T(8,128)S(1)}, f32[136,128]{1,0:T(8,128)S(1)}, u32[]{:S(2)}, u32[]{:S(2)}) collective-permute-start(f32[136,128]{1,0:T(8,128)S(1)} %get-tuple-element.19), channel_id=1, source_target_pairs={{0,8},{2,10},{4,12},{6,14},{8,0},{10,2},{12,4},{14,6},{16,24},{18,... | collective-permute-start | bytes 208904 | tf_op jit(solution)/shard_map/ppermute | solution.py:586
  27.6 2.6 %collective-permute-start.4 = (f32[136,128]{1,0:T(8,128)S(1)}, f32[136,128]{1,0:T(8,128)S(1)}, u32[]{:S(2)}, u32[]{:S(2)}) collective-permute-start(f32[136,128]{1,0:T(8,128)S(1)} %get-tuple-element.20), channel_id=1, source_target_pairs={{0,16},{2,18},{4,20},{6,22},{8,24},{10,26},{12,28},{14,30},{16,0},... | collective-permute-start | bytes 208904 | tf_op jit(solution)/shard_map/ppermute | solution.py:586
  30.2 0.2 collective-permute-start.5
  30.4 0.5 collective-permute-done.3.refs_1_
  30.9 3.4 %collective-permute-done.4.refs_2_ = f32[136,128]{1,0:T(8,128)S(1)} collective-permute-done((f32[136,128]{1,0:T(8,128)S(1)}, f32[136,128]{1,0:T(8,128)S(1)}, u32[]{:S(2)}, u32[]{:S(2)}) %collective-permute-start.4) | collective-permute-done | bytes 69664 | tf_op jit(solution)/shard_map/ppermute | solution.py:586
  34.3 2.1 %collective-permute-done.5.refs_3_ = f32[136,128]{1,0:T(8,128)S(1)} collective-permute-done((f32[136,128]{1,0:T(8,128)S(1)}, f32[136,128]{1,0:T(8,128)S(1)}, u32[]{:S(2)}, u32[]{:S(2)}) %collective-permute-start.5) | collective-permute-done | bytes 69664 | tf_op jit(solution)/shard_map/ppermute | solution.py:586
  36.5 1.4 %collective-permute-start.8 = (f32[136,128]{1,0:T(8,128)S(1)}, f32[136,128]{1,0:T(8,128)S(1)}, u32[]{:S(2)}, u32[]{:S(2)}) collective-permute-start(f32[136,128]{1,0:T(8,128)S(1)} %partial_sums.3), channel_id=1, source_target_pairs={{0,24},{2,26},{4,28},{6,30},{8,16},{10,18},{12,20},{14,22},{16,8},... | collective-permute-start | bytes 208904 | tf_op jit(solution)/shard_map/ppermute | solution.py:586
  37.9 0.3 collective-permute-start.7
  38.2 2.7 %collective-permute-start.6 = (f32[136,128]{1,0:T(8,128)S(1)}, f32[136,128]{1,0:T(8,128)S(1)}, u32[]{:S(2)}, u32[]{:S(2)}) collective-permute-start(f32[136,128]{1,0:T(8,128)S(1)} %partial_sums.3), channel_id=1, source_target_pairs={{0,8},{2,10},{4,12},{6,14},{8,0},{10,2},{12,4},{14,6},{16,24},{18,... | collective-permute-start | bytes 208904 | tf_op jit(solution)/shard_map/ppermute | solution.py:586
  40.9 1.8 %collective-permute-done.8 = f32[136,128]{1,0:T(8,128)S(1)} collective-permute-done((f32[136,128]{1,0:T(8,128)S(1)}, f32[136,128]{1,0:T(8,128)S(1)}, u32[]{:S(2)}, u32[]{:S(2)}) %collective-permute-start.8) | collective-permute-done | bytes 69664 | tf_op jit(solution)/shard_map/ppermute | solution.py:586
  42.7 1.4 %collective-permute-done.7 = f32[136,128]{1,0:T(8,128)S(1)} collective-permute-done((f32[136,128]{1,0:T(8,128)S(1)}, f32[136,128]{1,0:T(8,128)S(1)}, u32[]{:S(2)}, u32[]{:S(2)}) %collective-permute-start.7) | collective-permute-done | bytes 69664 | tf_op jit(solution)/shard_map/ppermute | solution.py:586
  44.1 0.0 collective-permute-done.6
  44.2 1.6 %collective-permute-start.11 = (f32[544,128]{1,0:T(8,128)S(1)}, f32[544,128]{1,0:T(8,128)S(1)}, u32[]{:S(2)}, u32[]{:S(2)}) collective-permute-start(f32[544,128]{1,0:T(8,128)S(1)} %pad_maximum_fusion.refs_0_), channel_id=1, source_target_pairs={{0,6},{2,4},{4,2},{6,0},{8,14},{10,12},{12,10},{14,8},{16,22},{18,... | collective-permute-start | bytes 835592 | tf_op jit(solution)/shard_map/ppermute | solution.py:586
  45.7 1.2 %collective-permute-start.10 = (f32[544,128]{1,0:T(8,128)S(1)}, f32[544,128]{1,0:T(8,128)S(1)}, u32[]{:S(2)}, u32[]{:S(2)}) collective-permute-start(f32[544,128]{1,0:T(8,128)S(1)} %pad_maximum_fusion.refs_0_), channel_id=1, source_target_pairs={{0,4},{2,6},{4,0},{6,2},{8,12},{10,14},{12,8},{14,10},{16,20},{18,... | collective-permute-start | bytes 835592 | tf_op jit(solution)/shard_map/ppermute | solution.py:586
  46.9 0.8 collective-permute-start.9
  47.7 0.0 collective-permute-start.12
  47.7 6.0 %collective-permute-done.11.refs_3_ = f32[544,128]{1,0:T(8,128)S(1)} collective-permute-done((f32[544,128]{1,0:T(8,128)S(1)}, f32[544,128]{1,0:T(8,128)S(1)}, u32[]{:S(2)}, u32[]{:S(2)}) %collective-permute-start.11) | collective-permute-done | bytes 278560 | tf_op jit(solution)/shard_map/ppermute | solution.py:586
  53.7 0.0 collective-permute-start.15
  53.7 2.8 %collective-permute-done.10.refs_2_ = f32[544,128]{1,0:T(8,128)S(1)} collective-permute-done((f32[544,128]{1,0:T(8,128)S(1)}, f32[544,128]{1,0:T(8,128)S(1)}, u32[]{:S(2)}, u32[]{:S(2)}) %collective-permute-start.10) | collective-permute-done | bytes 278560 | tf_op jit(solution)/shard_map/ppermute | solution.py:586
  56.5 0.0 collective-permute-start.14
  56.5 0.0 collective-permute-done.9.refs_1_
  56.5 0.5 collective-permute-start.13
  57.0 0.0 collective-permute-done.12.refs_4_
  57.0 0.0 collective-permute-done.15.refs_7_
  57.0 1.0 %collective-permute-done.14.refs_6_ = f32[544,128]{1,0:T(8,128)S(1)} collective-permute-done((f32[544,128]{1,0:T(8,128)S(1)}, f32[544,128]{1,0:T(8,128)S(1)}, u32[]{:S(2)}, u32[]{:S(2)}) %collective-permute-start.14) | collective-permute-done | bytes 278560 | tf_op jit(solution)/shard_map/ppermute | solution.py:618
  58.1 0.4 collective-permute-done.13.refs_5_
  58.5 0.0 copy-start
  58.5 1.6 %copy-done = f32[512,1024]{1,0:T(8,128)S(1)} copy-done((f32[512,1024]{1,0:T(8,128)S(1)}, f32[512,1024]{1,0:T(8,128)}, u32[]{:S(2)}) %copy-start) | copy-done | bytes 2097176
  60.1 29.0 %factor.1 = (f32[64,512]{1,0:T(8,128)}, f32[1,512]{1,0:T(1,128)}, f32[1,512]{1,0:T(1,128)}) custom-call(f32[544,128]{1,0:T(8,128)S(1)} %pad_maximum_fusion.refs_0_, f32[544,128]{1,0:T(8,128)S(1)} %collective-permute-done.9.refs_1_, f32[544,128]{1,0:T(8,128)S(1)} %collective-permute-done.10.refs_2_, f32[544,128]{1,0:T(8,128)S(1)} %collective-permute-done.11.refs_3_, ...), custom_call_target="tpu_custom_call" | custom-call | tf_op jit(solution)/shard_map/factor/pallas_call | solution.py:623
  (2 shorter events, 0.0 us)
Async XLA Ops:
  7.7 10.7 %collective-permute-start = (f32[544,128]{1,0:T(8,128)}, f32[544,128]{1,0:T(8,128)S(1)}, u32[]{:S(2)}, u32[]{:S(2)}) collective-permute-start(f32[544,128]{1,0:T(8,128)} %get-tuple-element.15), channel_id=1, source_target_pairs={{0,2},{2,0},{4,6},{6,4},{8,10},{10,8},{12,14},{14,12},{16,18},{18,... | collective-permute-start | bytes 835592 | tf_op jit(solution)/shard_map/ppermute | solution.py:586
  10.7 14.2 %collective-permute-start.1 = (f32[544,128]{1,0:T(8,128)}, f32[544,128]{1,0:T(8,128)S(1)}, u32[]{:S(2)}, u32[]{:S(2)}) collective-permute-start(f32[544,128]{1,0:T(8,128)} %get-tuple-element.16), channel_id=1, source_target_pairs={{0,4},{2,6},{4,0},{6,2},{8,12},{10,14},{12,8},{14,10},{16,20},{18,... | collective-permute-start | bytes 835592 | tf_op jit(solution)/shard_map/ppermute | solution.py:586
  12.2 12.7 %collective-permute-start.2 = (f32[544,128]{1,0:T(8,128)}, f32[544,128]{1,0:T(8,128)S(1)}, u32[]{:S(2)}, u32[]{:S(2)}) collective-permute-start(f32[544,128]{1,0:T(8,128)} %get-tuple-element.17), channel_id=1, source_target_pairs={{0,6},{2,4},{4,2},{6,0},{8,14},{10,12},{12,10},{14,8},{16,22},{18,... | collective-permute-start | bytes 835592 | tf_op jit(solution)/shard_map/ppermute | solution.py:586
  25.0 1.0 %copy-start.1 = (f32[544,128]{1,0:T(8,128)S(1)}, f32[544,128]{1,0:T(8,128)}, u32[]{:S(2)}) copy-start(f32[544,128]{1,0:T(8,128)} %get-tuple-element.14.refs_0_) | copy-start | bytes 835588
  26.0 5.0 %collective-permute-start.3 = (f32[136,128]{1,0:T(8,128)S(1)}, f32[136,128]{1,0:T(8,128)S(1)}, u32[]{:S(2)}, u32[]{:S(2)}) collective-permute-start(f32[136,128]{1,0:T(8,128)S(1)} %get-tuple-element.19), channel_id=1, source_target_pairs={{0,8},{2,10},{4,12},{6,14},{8,0},{10,2},{12,4},{14,6},{16,24},{18,... | collective-permute-start | bytes 208904 | tf_op jit(solution)/shard_map/ppermute | solution.py:586
  27.6 6.7 %collective-permute-start.4 = (f32[136,128]{1,0:T(8,128)S(1)}, f32[136,128]{1,0:T(8,128)S(1)}, u32[]{:S(2)}, u32[]{:S(2)}) collective-permute-start(f32[136,128]{1,0:T(8,128)S(1)} %get-tuple-element.20), channel_id=1, source_target_pairs={{0,16},{2,18},{4,20},{6,22},{8,24},{10,26},{12,28},{14,30},{16,0},... | collective-permute-start | bytes 208904 | tf_op jit(solution)/shard_map/ppermute | solution.py:586
  30.2 6.2 %collective-permute-start.5 = (f32[136,128]{1,0:T(8,128)S(1)}, f32[136,128]{1,0:T(8,128)S(1)}, u32[]{:S(2)}, u32[]{:S(2)}) collective-permute-start(f32[136,128]{1,0:T(8,128)S(1)} %get-tuple-element.21), channel_id=1, source_target_pairs={{0,24},{2,26},{4,28},{6,30},{8,16},{10,18},{12,20},{14,22},{16,8},... | collective-permute-start | bytes 208904 | tf_op jit(solution)/shard_map/ppermute | solution.py:586
  36.5 6.2 %collective-permute-start.8 = (f32[136,128]{1,0:T(8,128)S(1)}, f32[136,128]{1,0:T(8,128)S(1)}, u32[]{:S(2)}, u32[]{:S(2)}) collective-permute-start(f32[136,128]{1,0:T(8,128)S(1)} %partial_sums.3), channel_id=1, source_target_pairs={{0,24},{2,26},{4,28},{6,30},{8,16},{10,18},{12,20},{14,22},{16,8},... | collective-permute-start | bytes 208904 | tf_op jit(solution)/shard_map/ppermute | solution.py:586
  37.9 6.2 %collective-permute-start.7 = (f32[136,128]{1,0:T(8,128)S(1)}, f32[136,128]{1,0:T(8,128)S(1)}, u32[]{:S(2)}, u32[]{:S(2)}) collective-permute-start(f32[136,128]{1,0:T(8,128)S(1)} %partial_sums.3), channel_id=1, source_target_pairs={{0,16},{2,18},{4,20},{6,22},{8,24},{10,26},{12,28},{14,30},{16,0},... | collective-permute-start | bytes 208904 | tf_op jit(solution)/shard_map/ppermute | solution.py:586
  38.2 5.9 %collective-permute-start.6 = (f32[136,128]{1,0:T(8,128)S(1)}, f32[136,128]{1,0:T(8,128)S(1)}, u32[]{:S(2)}, u32[]{:S(2)}) collective-permute-start(f32[136,128]{1,0:T(8,128)S(1)} %partial_sums.3), channel_id=1, source_target_pairs={{0,8},{2,10},{4,12},{6,14},{8,0},{10,2},{12,4},{14,6},{16,24},{18,... | collective-permute-start | bytes 208904 | tf_op jit(solution)/shard_map/ppermute | solution.py:586
  44.2 9.5 %collective-permute-start.11 = (f32[544,128]{1,0:T(8,128)S(1)}, f32[544,128]{1,0:T(8,128)S(1)}, u32[]{:S(2)}, u32[]{:S(2)}) collective-permute-start(f32[544,128]{1,0:T(8,128)S(1)} %pad_maximum_fusion.refs_0_), channel_id=1, source_target_pairs={{0,6},{2,4},{4,2},{6,0},{8,14},{10,12},{12,10},{14,8},{16,22},{18,... | collective-permute-start | bytes 835592 | tf_op jit(solution)/shard_map/ppermute | solution.py:586
  45.7 10.8 %collective-permute-start.10 = (f32[544,128]{1,0:T(8,128)S(1)}, f32[544,128]{1,0:T(8,128)S(1)}, u32[]{:S(2)}, u32[]{:S(2)}) collective-permute-start(f32[544,128]{1,0:T(8,128)S(1)} %pad_maximum_fusion.refs_0_), channel_id=1, source_target_pairs={{0,4},{2,6},{4,0},{6,2},{8,12},{10,14},{12,8},{14,10},{16,20},{18,... | collective-permute-start | bytes 835592 | tf_op jit(solution)/shard_map/ppermute | solution.py:586
  46.9 9.6 %collective-permute-start.9 = (f32[544,128]{1,0:T(8,128)S(1)}, f32[544,128]{1,0:T(8,128)S(1)}, u32[]{:S(2)}, u32[]{:S(2)}) collective-permute-start(f32[544,128]{1,0:T(8,128)S(1)} %pad_maximum_fusion.refs_0_), channel_id=1, source_target_pairs={{0,2},{2,0},{4,6},{6,4},{8,10},{10,8},{12,14},{14,12},{16,18},{18,... | collective-permute-start | bytes 835592 | tf_op jit(solution)/shard_map/ppermute | solution.py:586
  47.7 9.3 %collective-permute-start.12 = (f32[544,128]{1,0:T(8,128)S(1)}, f32[544,128]{1,0:T(8,128)S(1)}, u32[]{:S(2)}, u32[]{:S(2)}) collective-permute-start(f32[544,128]{1,0:T(8,128)S(1)} %pad_maximum_fusion.refs_0_), channel_id=1, source_target_pairs={{0,1},{1,0},{2,3},{3,2},{4,5},{5,4},{6,7},{7,6},{8,9},{9,8},{10,11... | collective-permute-start | bytes 835592 | tf_op jit(solution)/shard_map/ppermute | solution.py:618
  53.7 3.4 %collective-permute-start.15 = (f32[544,128]{1,0:T(8,128)S(1)}, f32[544,128]{1,0:T(8,128)S(1)}, u32[]{:S(2)}, u32[]{:S(2)}) collective-permute-start(f32[544,128]{1,0:T(8,128)S(1)} %collective-permute-done.11.refs_3_), channel_id=1, source_target_pairs={{0,1},{1,0},{2,3},{3,2},{4,5},{5,4},{6,7},{7,6},{8,9},{9,8},{10,11... | collective-permute-start | bytes 835592 | tf_op jit(solution)/shard_map/ppermute | solution.py:618
  56.5 1.6 %collective-permute-start.14 = (f32[544,128]{1,0:T(8,128)S(1)}, f32[544,128]{1,0:T(8,128)S(1)}, u32[]{:S(2)}, u32[]{:S(2)}) collective-permute-start(f32[544,128]{1,0:T(8,128)S(1)} %collective-permute-done.10.refs_2_), channel_id=1, source_target_pairs={{0,1},{1,0},{2,3},{3,2},{4,5},{5,4},{6,7},{7,6},{8,9},{9,8},{10,11... | collective-permute-start | bytes 835592 | tf_op jit(solution)/shard_map/ppermute | solution.py:618
  56.5 2.0 %collective-permute-start.13 = (f32[544,128]{1,0:T(8,128)S(1)}, f32[544,128]{1,0:T(8,128)S(1)}, u32[]{:S(2)}, u32[]{:S(2)}) collective-permute-start(f32[544,128]{1,0:T(8,128)S(1)} %collective-permute-done.9.refs_1_), channel_id=1, source_target_pairs={{0,1},{1,0},{2,3},{3,2},{4,5},{5,4},{6,7},{7,6},{8,9},{9,8},{10,11... | collective-permute-start | bytes 835592 | tf_op jit(solution)/shard_map/ppermute | solution.py:618
  58.5 1.6 %copy-start = (f32[512,1024]{1,0:T(8,128)S(1)}, f32[512,1024]{1,0:T(8,128)}, u32[]{:S(2)}) copy-start(f32[512,1024]{1,0:T(8,128)} %refs_8_.1) | copy-start | bytes 6291460
